TPU v7x, 128 devices: a whole 4x4x4 slice. The times are simulated.
128 devices in a mesh: section: 4 (over z_lo, core), blk: 32 (over x, y, z_hi).
Axes of the slice: x: 4, y: 4, z: 4 (z_hi: 2, z_lo: 2; z = z_hi * 2 + z_lo), core: 2. Of those that a mesh axis runs over, the one named last changes fastest.
Arguments:
- queries: bfloat16 [4, 4096, 4096], P('section', 'blk'), may hold values from -200 to 200
- out_grad: bfloat16 [4, 4096, 4096], P('section', 'blk'), may hold values from -6 to 6
- kv_codes: int32 [2, 4096, 1024], P(None, 'blk', 'section'), may hold values from -127 to 127, as said below
- kv_scales: float32 [2, 128, 8], P(None, 'blk', 'section'), may hold values from 0.005 to 0.012
Outputs:
- query_grad: bfloat16 [4, 4096, 4096], P('section', 'blk')
- kv_grad: float32 [2, 4096, 1024], P(None, 'blk', 'section')
Inputs may be any that keep to these rules, and one draw needn't show every extreme that they name: `kv_codes`: whole numbers.
All inputs are finite; a program needn't handle non-finite values.
Results may differ from a plain program's by a relative error of at most 0.03.
Values may be sent and summed in bfloat16 or wider, within the bound.
No kernel may reach another device: no remote copies, remote signals or barrier semaphores. Data moves between devices by JAX's collectives and lax.ppermute only.
A program may use at most 128 MiB of HBM per device.

v0:
```python
import math

import jax
import jax.numpy as jnp
from jax import lax
from jax.sharding import PartitionSpec as P

HEADS = 32
KV_HEADS = 8
HEAD_DIM = 128
QUANT_BLOCK = 32
KEY_BLOCK = 512


def dequantize(kv_codes, kv_scales):
    per_entry = jnp.repeat(jnp.repeat(kv_scales, QUANT_BLOCK, axis=1), HEAD_DIM, axis=2)
    return (kv_codes.astype(jnp.float32) * per_entry).astype(jnp.bfloat16)


def shards(queries, out_grad, kv_codes, kv_scales):
    local_cache = dequantize(kv_codes, kv_scales)
    all_heads = lax.all_gather(local_cache, "section", axis=2, tiled=True)
    whole_cache = lax.all_gather(all_heads, "blk", axis=1, tiled=True)
    row_count = queries.shape[1]
    total_rows = whole_cache.shape[1]
    groups = HEADS // KV_HEADS
    inv_scale = 1.0 / math.sqrt(HEAD_DIM)
    query_heads = queries[0].reshape(row_count, KV_HEADS, groups, HEAD_DIM)
    cotangent = out_grad[0].reshape(row_count, KV_HEADS, groups, HEAD_DIM)
    key_cache = whole_cache[0]
    value_cache = whole_cache[1]
    first_row = lax.axis_index("blk") * row_count
    row_pos = first_row + jnp.arange(row_count, dtype=jnp.int32)
    block_count = (first_row + row_count + KEY_BLOCK - 1) // KEY_BLOCK

    def block_terms(index):
        offset = index * KEY_BLOCK
        key_block = lax.dynamic_slice_in_dim(key_cache, offset, KEY_BLOCK, 0).reshape(
            KEY_BLOCK, KV_HEADS, HEAD_DIM
        )
        value_block = lax.dynamic_slice_in_dim(value_cache, offset, KEY_BLOCK, 0).reshape(
            KEY_BLOCK, KV_HEADS, HEAD_DIM
        )
        scores = (
            jnp.einsum("ihgd,jhd->hgij", query_heads, key_block, preferred_element_type=jnp.float32)
            * inv_scale
        )
        visible = (offset + jnp.arange(KEY_BLOCK, dtype=jnp.int32))[None, :] <= row_pos[:, None]
        scores = jnp.where(visible, scores, -1e30)
        prob_grad = jnp.einsum(
            "ihgd,jhd->hgij", cotangent, value_block, preferred_element_type=jnp.float32
        )
        return (key_block, scores, prob_grad)

    def first_pass(index, carry):
        running_max, running_sum, running_dot = carry
        unused_block, scores, prob_grad = block_terms(index)
        new_max = jnp.maximum(running_max, jnp.max(scores, axis=-1))
        weights = jnp.exp(scores - new_max[..., None])
        factor = jnp.exp(running_max - new_max)
        new_sum = running_sum * factor + jnp.sum(weights, axis=-1)
        new_dot = running_dot * factor + jnp.sum(weights * prob_grad, axis=-1)
        return (new_max, new_sum, new_dot)

    stat_shape = (KV_HEADS, groups, row_count)
    start_stats = (
        jnp.full(stat_shape, -1e30, jnp.float32),
        jnp.zeros(stat_shape, jnp.float32),
        jnp.zeros(stat_shape, jnp.float32),
    )
    row_max, row_sum, row_dot = lax.fori_loop(0, block_count, first_pass, start_stats)
    row_delta = row_dot / row_sum

    def second_pass(index, carry):
        query_acc, kv_term = carry
        key_block, scores, prob_grad = block_terms(index)
        probs = jnp.exp(scores - row_max[..., None]) / row_sum[..., None]
        score_grad = (probs * (prob_grad - row_delta[..., None]) * inv_scale).astype(jnp.bfloat16)
        probs_low = probs.astype(jnp.bfloat16)
        query_acc = query_acc + jnp.einsum(
            "hgij,jhd->ihgd", score_grad, key_block, preferred_element_type=jnp.float32
        )
        key_grad = jnp.einsum(
            "hgij,ihgd->jhd", score_grad, query_heads, preferred_element_type=jnp.float32
        )
        value_grad = jnp.einsum(
            "hgij,ihgd->jhd", probs_low, cotangent, preferred_element_type=jnp.float32
        )
        block_grad = jnp.stack([key_grad, value_grad]).reshape(2, KEY_BLOCK, KV_HEADS * HEAD_DIM)
        kv_term = lax.dynamic_update_slice_in_dim(kv_term, block_grad, index * KEY_BLOCK, 1)
        return (query_acc, kv_term)

    start_acc = (
        jnp.zeros((row_count, KV_HEADS, groups, HEAD_DIM), jnp.float32),
        jnp.zeros((2, total_rows, KV_HEADS * HEAD_DIM), jnp.float32),
    )
    query_acc, kv_term = lax.fori_loop(0, block_count, second_pass, start_acc)
    query_grad = query_acc.reshape(row_count, HEADS * HEAD_DIM).astype(jnp.bfloat16)[None]
    position_part = lax.psum_scatter(
        kv_term.astype(jnp.bfloat16), "blk", scatter_dimension=1, tiled=True
    )
    kv_grad = lax.psum_scatter(position_part, "section", scatter_dimension=2, tiled=True).astype(
        jnp.float32
    )
    return (query_grad, kv_grad)


def solution(mesh):
    in_specs = (
        P("section", "blk", None),
        P("section", "blk", None),
        P(None, "blk", "section"),
        P(None, "blk", "section"),
    )
    out_specs = (P("section", "blk", None), P(None, "blk", "section"))
    return jax.shard_map(shards, mesh=mesh, in_specs=in_specs, out_specs=out_specs, check_vma=False)
```

profile of v0, /device:TPU:1, one launch (start us, length us, event | category | flops | bytes accessed | tf_op | source)
XLA Modules:
  0.0 890.7 jit_solution(15699132963001567280)
XLA Ops:
  7.2 0.8 broadcast_in_dim.40
  8.0 1.1 copy.28
  9.2 9.4 %all_gather.6 = bf16[2,128,1024]{1,2,0:T(8,128)(2,1)} all-gather(bf16[2,128,256]{1,2,0:T(8,128)(2,1)S(1)} %fusion.15), channel_id=1, replica_groups=mesh['section'=4,'blk'=32] {'section'}, dimensions={2}, use_global_device_ids=true | all-gather | bytes 655360 | tf_op jit(solution)/shard_map/all_gather | solution.py:22
  18.7 1.6 copy.29
  20.3 1.0 copy-done
  21.2 0.7 copy.31
  21.9 1.6 copy.30
  23.5 1.3 copy.32
  24.8 224.8 %all-gather.2.cloned.1.call-done = bf16[2,4096,1024]{1,2,0:T(8,128)(2,1)} async-done(((bf16[2,128,1024]{1,2,0:T(8,128)(2,1)}), bf16[2,4096,1024]{1,2,0:T(8,128)(2,1)}) %all-gather.2.cloned.1.call-update) | async-done | bytes 16777232 | tf_op jit(solution)/shard_map/all_gather | solution.py:23
  249.6 11.7 %slice_bitcast_fusion = (bf16[4096,1024]{0,1:T(8,128)(2,1)}, bf16[4096,1024]{0,1:T(8,128)(2,1)}) fusion(bf16[2,4096,1024]{1,2,0:T(8,128)(2,1)} %all-gather.2.cloned.1.call-done), kind=kLoop, calls=%fused_computation.34 | loop fusion | bytes 33554432 | tf_op jit(solution)/shard_map/squeeze | solution.py:31
  261.3 9.2 %while.28 = (s32[]{:T(128)}, f32[8,4,128]{2,1,0:T(4,128)S(1)}, f32[8,4,128]{2,1,0:T(4,128)S(1)}, f32[8,4,128]{2,1,0:T(4,128)S(1)}, s32[]{:T(128)}, /*index=5*/bf...) while((s32[]{:T(128)}, f32[8,4,128]{2,1,0:T(4,128)S(1)}, ...), condition=%wide.region_4.5_spmd.clone, body=%wide.region_0.4_spmd.clone.sunk | while | flops 1098986112 | bytes 34116800 | solution.py:71
  261.5 1.7 constant_dynamic-slice_fusion.6
  263.2 1.5 fusion.55
  264.7 4.0 fusion.56
  268.7 1.8 fusion.57
  270.6 0.2 broadcast_in_dim.38
  270.8 6.0 broadcast_in_dim.39.clone
  276.8 19.7 %while.29 = (s32[]{:T(128)}, f32[128,8,4,128]{0,3,2,1:T(8,128)S(1)}, bf16[2,4096,1024]{2,1,0:T(8,128)(2,1)}, s32[]{:T(128)}, bf16[4096,1024]{0,1:T(8,128)(2,1)},...) while((s32[]{:T(128)}, ...), condition=%wide.region_6.7_spmd.clone, body=%wide.region_5.6_spmd.clone.sunk | while | flops 2704867840 | bytes 72537320 | solution.py:97
  277.0 1.7 constant_dynamic-slice_fusion.7
  278.7 3.6 fusion.68
  282.3 1.5 fusion.70
  283.8 1.4 fusion.69
  285.2 1.5 fusion.71
  286.7 1.2 bitcast_add_fusion.2
  287.9 1.5 pad_maximum_fusion.2
  289.4 3.9 copy.59
  293.4 3.1 constant_dynamic-update-slice_fusion.2
  296.6 562.6 %reduce-scatter.3.cloned.1.call-done = bf16[2,128,1024]{2,1,0:T(8,128)(2,1)} async-done(((bf16[2,4096,1024]{2,1,0:T(8,128)(2,1)}), bf16[2,128,1024]{2,1,0:T(8,128)(2,1)}) %reduce-scatter.3.cloned.1.call-update) | async-done | bytes 524304 | tf_op jit(solution)/shard_map/reduce_scatter | solution.py:99
  859.3 0.2 convert_element_type.33
  859.4 1.3 copy.47
  860.7 21.8 %reduce-scatter.5.cloned.1.call-done = bf16[2,128,256]{2,1,0:T(8,128)(2,1)} async-done(((bf16[2,128,1024]{2,1,0:T(8,128)(2,1)}), bf16[2,128,256]{2,1,0:T(8,128)(2,1)}) %reduce-scatter.5.cloned.1.call-update) | async-done | bytes 131088 | tf_op jit(solution)/shard_map/reduce_scatter | solution.py:102
  882.5 1.6 convert_element_type.36
  (24 shorter events, 0.6 us)
Async XLA Ops:
  7.2 242.5 %all-gather.2.cloned.1.call-start = ((), (), s32[]{:S(2)}) async-start(), calls=%async_computation.2 | async-start | bytes 17301504 | tf_op jit(solution)/shard_map/all_gather | solution.py:23
  18.6 840.7 %reduce-scatter.3.cloned.1.call-start = ((), (), s32[]{:S(2)}) async-start(), calls=%async_computation.3 | async-start | bytes 17301504 | tf_op jit(solution)/shard_map/reduce_scatter | solution.py:99
  20.3 1.0 copy-start
  283.8 1.4 copy-start.1
  296.6 586.0 %reduce-scatter.5.cloned.1.call-start = ((), (), s32[]{:S(2)}) async-start(), calls=%async_computation.4 | async-start | bytes 655360 | tf_op jit(solution)/shard_map/reduce_scatter | solution.py:102
Sparse Core Ops, SparseCore 0:
  18.7 230.8 all-gather.1
  296.7 562.5 reduce-scatter.2
  861.6 20.8 reduce-scatter.4
where the time goes:
time: 893 us; the launch traced here: 891 us
  waiting for transfers between devices  809 us (91%)
  local copies, waits for them, and re-layouts  37.8 us (4%)
  matrix products  14.7 us (2%)
  between operations  13.8 us (2%)
  blocking collectives  9.4 us (1%)
    reduce_scatter x1, waiting for transfers between devices, shards(): lax.psum_scatter(kv_term.astype(jnp.bfloat16), 'blk', scatter_dimension=1...  563 us
    all_gather x1, waiting for transfers between devices, shards(): whole_cache = lax.all_gather(all_heads, 'blk', axis=1, tiled=True)  225 us
    reduce_scatter x1, waiting for transfers between devices, shards(): lax.psum_scatter(position_part, 'section', scatter_dimension=2, tiled=True)  21.8 us
  transfers between devices with their start and end apart: 3, of which 3 were waited for; matrix products, arithmetic and copies ran while one was open for 1% of the time, Pallas kernels for 0%

commit v1 on v0

v1 whole, which is shorter than its diff:
```python
import functools
import math

import jax
import jax.numpy as jnp
from jax import lax
from jax.experimental import pallas as pl
from jax.experimental.pallas import tpu as pltpu
from jax.sharding import PartitionSpec as P

HEAD_DIM = 128
GROUPS = 4
QUANT_BLOCK = 32
ROWS = 128
BLOCKS = 32
WIDTH = GROUPS * HEAD_DIM
AXES = ("section", "blk")
SCALE = 1.0 / math.sqrt(HEAD_DIM)
EXP2_SCALE = SCALE * math.log2(math.e)
F32 = jnp.float32
BF16 = jnp.bfloat16
NT = (((1,), (1,)), ((), ()))
NN = (((1,), (0,)), ((), ()))

STACK = 2
KEYS = 512
SPAN = KEYS // ROWS
STEP_ROWS = STACK * WIDTH
STEPS = 8 // STACK
CHUNKS = BLOCKS // SPAN
ORDER = (0, 2, 4, 6, 1, 3, 5, 7)


def flip(blk):
    return blk ^ 30


def attention_kernel(blocks_ref, *refs):
    units, kv_ref, outs, term_ref = refs[:8], refs[8], refs[9:17], refs[17]
    q_s, do_s, kt_s, w_s, g_s, m_s, dk_s, dv_s, dq_s = refs[18:]
    for n, k in enumerate(ORDER):
        for g in range(GROUPS):
            lo = (n % STACK) * WIDTH + g * HEAD_DIM
            q_s[n // STACK, lo : lo + ROWS, :] = units[k][0, :, g * HEAD_DIM : (g + 1) * HEAD_DIM]
            do_s[n // STACK, lo : lo + ROWS, :] = units[k][1, :, g * HEAD_DIM : (g + 1) * HEAD_DIM]
    for j in range(BLOCKS):
        kt_s[:, j * ROWS : (j + 1) * ROWS] = kv_ref[j, 0].T
    dk_s[...] = jnp.zeros_like(dk_s)
    dv_s[...] = jnp.zeros_like(dv_s)

    def one_group(group, _):
        block = blocks_ref[group // (STEPS // 2)]
        last = block // SPAN
        q, do = q_s.at[group], do_s.at[group]

        def keys(j, which):
            return kv_ref[pl.ds(j * SPAN, SPAN), which].reshape(KEYS, HEAD_DIM)

        def fold(x, op):
            return op(x.reshape(KEYS // 8, 8, STEP_ROWS), axis=0)

        def forward(j, carry, masked):
            top, total8, dot8 = carry
            scores = lax.dot_general(keys(j, 0), q[...], NT, preferred_element_type=F32)
            if masked:
                key_at = lax.broadcasted_iota(jnp.int32, (KEYS, STEP_ROWS), 0)
                row_at = lax.broadcasted_iota(jnp.int32, (KEYS, STEP_ROWS), 1) & (ROWS - 1)
                scores = jnp.where(key_at <= row_at + (block - j * SPAN) * ROWS, scores, -1e30)
            prob_grad = lax.dot_general(keys(j, 1), do[...], NT, preferred_element_type=F32)
            here = jnp.max(fold(scores, jnp.max), axis=0, keepdims=True) * EXP2_SCALE
            new_top = here if masked else jnp.maximum(top, here)
            weights = jnp.exp2(scores * EXP2_SCALE - new_top)
            w_s[j] = weights
            g_s[j] = prob_grad
            m_s[j] = jnp.broadcast_to(new_top, (8, STEP_ROWS))
            total, dot = fold(weights, jnp.sum), fold(weights * prob_grad, jnp.sum)
            if masked:
                return new_top, total, dot
            factor = jnp.exp2(top - new_top)
            return new_top, total8 * factor + total, dot8 * factor + dot

        start = forward(last, (None, None, None), True)
        top, total8, dot8 = lax.fori_loop(0, last, lambda j, c: forward(j, c, False), start)
        inverse = 1.0 / jnp.sum(total8, axis=0, keepdims=True)
        delta = jnp.sum(dot8, axis=0, keepdims=True) * inverse
        dq_s[...] = jnp.zeros_like(dq_s)

        def backward(j, _):
            factor = jnp.exp2(m_s[j][0:1] - top) * inverse
            probs = w_s[j] * factor
            score_grad = (probs * (g_s[j] - delta)).astype(BF16)
            dv_s[j] += lax.dot_general(probs.astype(BF16), do[...], NN, preferred_element_type=F32)
            dk_s[j] += lax.dot_general(score_grad, q[...], NN, preferred_element_type=F32)
            columns = kt_s[:, pl.ds(pl.multiple_of(j * KEYS, KEYS), KEYS)]
            dq_s[...] += lax.dot_general(columns, score_grad, NN, preferred_element_type=F32)
            return 0

        lax.fori_loop(0, last + 1, backward, 0)
        for h in range(STEP_ROWS // ROWS):
            part = dq_s[:, h * ROWS : (h + 1) * ROWS]
            q_s[group, h * ROWS : (h + 1) * ROWS, :] = (part.T * SCALE).astype(BF16)
        return 0

    lax.fori_loop(0, STEPS, one_group, 0)
    for n, k in enumerate(ORDER):
        for g in range(GROUPS):
            lo = (n % STACK) * WIDTH + g * HEAD_DIM
            outs[k][:, g * HEAD_DIM : (g + 1) * HEAD_DIM] = q_s[n // STACK, lo : lo + ROWS, :]
    for j in range(CHUNKS):
        term_ref[j * SPAN : (j + 1) * SPAN, 0] = (dk_s[j] * SCALE).astype(BF16).reshape(SPAN, ROWS, HEAD_DIM)
        term_ref[j * SPAN : (j + 1) * SPAN, 1] = dv_s[j].astype(BF16).reshape(SPAN, ROWS, HEAD_DIM)


def attention(blocks, units, kv):
    vmem = pl.BlockSpec(memory_space=pltpu.VMEM)
    return pl.pallas_call(
        attention_kernel,
        out_shape=[jax.ShapeDtypeStruct((ROWS, WIDTH), BF16)] * 8
        + [jax.ShapeDtypeStruct((BLOCKS, 2, ROWS, HEAD_DIM), BF16)],
        in_specs=[pl.BlockSpec(memory_space=pltpu.SMEM)] + [vmem] * 9,
        out_specs=[vmem] * 9,
        scratch_shapes=[
            pltpu.VMEM((STEPS, STEP_ROWS, HEAD_DIM), BF16),
            pltpu.VMEM((STEPS, STEP_ROWS, HEAD_DIM), BF16),
            pltpu.VMEM((HEAD_DIM, BLOCKS * ROWS), BF16),
            pltpu.VMEM((CHUNKS, KEYS, STEP_ROWS), F32),
            pltpu.VMEM((CHUNKS, KEYS, STEP_ROWS), F32),
            pltpu.VMEM((CHUNKS, 8, STEP_ROWS), F32),
            pltpu.VMEM((CHUNKS, KEYS, HEAD_DIM), F32),
            pltpu.VMEM((CHUNKS, KEYS, HEAD_DIM), F32),
            pltpu.VMEM((HEAD_DIM, STEP_ROWS), F32),
        ],
        compiler_params=pltpu.CompilerParams(vmem_limit_bytes=60 * 1024 * 1024),
        cost_estimate=pl.CostEstimate(flops=20_000_000_000, bytes_accessed=8_000_000, transcendentals=9_000_000),
        name="attention",
    )(blocks, *units, kv)


def partners(k):
    return [
        (s * BLOCKS + b, (s ^ (k >> 1)) * BLOCKS + (flip(b) if k & 1 else b)) for s in range(4) for b in range(BLOCKS)
    ]


def shards(queries, out_grad, kv_codes, kv_scales):
    section, blk = lax.axis_index("section"), lax.axis_index("blk")
    head = section * 2 + blk // 16

    codes = kv_codes.reshape(2, ROWS // QUANT_BLOCK, QUANT_BLOCK, 2, HEAD_DIM).astype(F32)
    cache = (codes * kv_scales[:, :, None, :, None]).astype(BF16)
    cache = cache.reshape(2, ROWS, 2, HEAD_DIM).transpose(2, 0, 1, 3)
    spread = jnp.broadcast_to(cache[:, None], (2, 16, 2, ROWS, HEAD_DIM)).reshape(BLOCKS, 2, ROWS, HEAD_DIM)

    units = []
    for k in range(8):
        at = (head ^ k) * WIDTH
        unit = jnp.stack(
            [lax.dynamic_slice_in_dim(queries[0], at, WIDTH, 1), lax.dynamic_slice_in_dim(out_grad[0], at, WIDTH, 1)]
        )
        units.append(lax.ppermute(unit, AXES, partners(k)) if k else unit)
    kv = lax.all_to_all(spread, "blk", 0, 0, tiled=True)

    blocks = jnp.stack([blk, flip(blk)]).astype(jnp.int32)
    *grads, term = attention(blocks, units, kv)

    received = lax.all_to_all(term, "blk", 0, 0, tiled=True)
    kv_grad = received.reshape(2, 16, 2, ROWS, HEAD_DIM).astype(F32).sum(1)
    kv_grad = kv_grad.transpose(1, 2, 0, 3).reshape(2, ROWS, 2 * HEAD_DIM)

    query_grad = jnp.zeros((ROWS, 8 * WIDTH), BF16)
    for k in range(8):
        grad = lax.ppermute(grads[k], AXES, partners(k)) if k else grads[k]
        query_grad = lax.dynamic_update_slice_in_dim(query_grad, grad, (head ^ k) * WIDTH, 1)
    return query_grad[None], kv_grad


def solution(mesh):
    in_specs = (
        P("section", "blk", None),
        P("section", "blk", None),
        P(None, "blk", "section"),
        P(None, "blk", "section"),
    )
    out_specs = (P("section", "blk", None), P(None, "blk", "section"))
    return jax.shard_map(shards, mesh=mesh, in_specs=in_specs, out_specs=out_specs, check_vma=False)
```

time: 893 us -> 161 us (0.18)
  waiting for transfers between devices: 809 us -> 60.7 us
  starting transfers between devices: 0.12 us -> 51.3 us
  Pallas kernels: 0 us -> 36.7 us
  local copies, waits for them, and re-layouts: 37.8 us -> 7.53 us
  matrix products: 14.7 us -> 0 us
  between operations: 13.8 us -> 0.94 us
  blocking collectives: 9.4 us -> 0 us
    reduce_scatter x2 -> x0, waiting for transfers between devices: 584 us -> none  [the longest x1 563 us: shards(): lax.psum_scatter(kv_term.astype(jnp.bfloat16), 'blk', scatter_dimension=1...]
    all_gather x1 -> x0, waiting for transfers between devices: 225 us -> none  [shards(): whole_cache = lax.all_gather(all_heads, 'blk', axis=1, tiled=True)]
    ppermute x0 -> x14, waiting for transfers between devices: none -> 60.7 us  [the longest x7 32.7 us: shards(): units.append(lax.ppermute(unit, AXES, partners(k)) if k else unit)]
    pallas_call x0 -> x1, Pallas kernels: none -> 36.7 us  [attention(): pl.pallas_call(attention_kernel, out_shape=[jax.ShapeDtypeStruct((ROWS, W...]
    ppermute x0 -> x14, starting transfers between devices: none -> 32.6 us  [the longest x7 17.6 us: shards(): units.append(lax.ppermute(unit, AXES, partners(k)) if k else unit)]
    all_to_all x0 -> x2, starting transfers between devices: none -> 18.7 us  [the longest x1 11.3 us: shards(): kv = lax.all_to_all(spread, 'blk', 0, 0, tiled=True)]
    dot_general x7 -> x0, matrix products: 14.7 us -> none  [the longest x2 5.37 us: block_terms(): jnp.einsum('ihgd,jhd->hgij', cotangent, value_block, preferred_element_ty...]
    squeeze x1 -> x0, local copies, waits for them, and re-layouts: 11.7 us -> none  [shards(): value_cache = whole_cache[1]]
  transfers between devices with their start and end apart: 3 -> 16, of which waited for: 3 -> 8; matrix products, arithmetic and copies ran while one was open for 1% -> 2% of each run, Pallas kernels for 0% -> 0%
where the time goes in v1:
time: 161 us
  waiting for transfers between devices  60.7 us (38%)
  starting transfers between devices  51.3 us (32%)
  Pallas kernels  36.7 us (23%)
  local copies, waits for them, and re-layouts  7.53 us (5%)
  other arithmetic  3.84 us (2%)
    pallas_call x1, Pallas kernels, attention(): pl.pallas_call(attention_kernel, out_shape=[jax.ShapeDtypeStruct((ROWS, W...  36.7 us
    ppermute x7, waiting for transfers between devices, shards(): units.append(lax.ppermute(unit, AXES, partners(k)) if k else unit)  32.7 us
    ppermute x7, waiting for transfers between devices, shards(): grad = lax.ppermute(grads[k], AXES, partners(k)) if k else grads[k]  28 us
    ppermute x7, starting transfers between devices, shards(): units.append(lax.ppermute(unit, AXES, partners(k)) if k else unit)  17.6 us
    ppermute x7, starting transfers between devices, shards(): grad = lax.ppermute(grads[k], AXES, partners(k)) if k else grads[k]  14.9 us
    all_to_all x1, starting transfers between devices, shards(): kv = lax.all_to_all(spread, 'blk', 0, 0, tiled=True)  11.3 us
    all_to_all x1, starting transfers between devices, shards(): received = lax.all_to_all(term, 'blk', 0, 0, tiled=True)  7.4 us
    unnamed x16, local copies, waits for them, and re-layouts  3.67 us
  transfers between devices with their start and end apart: 16, of which 8 were waited for; matrix products, arithmetic and copies ran while one was open for 2% of the time, Pallas kernels for 0%

profile of v1, /device:TPU:1, one launch (start us, length us, event | category | flops | bytes accessed | tf_op | source)
XLA Modules:
  0.0 161.0 jit_solution(14412066593432617501)
XLA Ops:
  0.6 1.0 convert_element_type.17
  1.6 0.1 convert_element_type.18
  1.7 0.8 copy.10
  2.5 0.3 fusion
  2.9 1.8 %broadcast_in_dim.28 = bf16[2,16,2,128,128]{4,3,2,1,0:T(8,128)(2,1)} broadcast(bf16[2,2,128,128]{3,2,1,0:T(8,128)(2,1)S(1)} %copy.11), dimensions={0,2,3,4} | broadcast | bytes 2228224 | tf_op jit(solution)/shard_map/broadcast_in_dim | solution.py:152
  4.8 11.3 %all-to-all-start = ((bf16[32,2,128,128]{3,2,1,0:T(8,128)(2,1)}), bf16[32,2,128,128]{3,2,1,0:T(8,128)(2,1)S(1)}, u32[]{:S(2)}, u32[]{:S(2)}) async-start(bf16[32,2,128,128]{3,2,1,0:T(8,128)(2,1)} %bitcast.4), calls=%async_computation | async-start | bytes 4194304 | tf_op jit(solution)/shard_map/all_to_all | solution.py:161
  16.1 1.5 constant_dynamic-slice_fusion
  17.7 6.3 %collective-permute-start.6 = (bf16[2,128,512]{2,1,0:T(8,128)(2,1)S(1)}, bf16[2,128,512]{2,1,0:T(8,128)(2,1)S(1)}, u32[]{:S(2)}, u32[]{:S(2)}) collective-permute-start(bf16[2,128,512]{2,1,0:T(8,128)(2,1)S(1)} %pad_maximum_fusion.7), channel_id=1, source_target_pairs={{0,126},{1,127},{2,124},{3,125},{4,122},{5,123},{6,120},{7,121},{8... | collective-permute-start | bytes 786440 | tf_op jit(solution)/shard_map/ppermute | solution.py:160
  24.1 0.8 collective-permute-start.4
  25.0 0.8 collective-permute-start.3
  25.8 6.1 %collective-permute-start.2 = (bf16[2,128,512]{2,1,0:T(8,128)(2,1)S(1)}, bf16[2,128,512]{2,1,0:T(8,128)(2,1)}, u32[]{:S(2)}, u32[]{:S(2)}) collective-permute-start(bf16[2,128,512]{2,1,0:T(8,128)(2,1)S(1)} %pad_maximum_fusion.3), channel_id=1, source_target_pairs={{0,62},{1,63},{2,60},{3,61},{4,58},{5,59},{6,56},{7,57},{8,54},{9,... | collective-permute-start | bytes 786440 | tf_op jit(solution)/shard_map/ppermute | solution.py:160
  32.0 0.7 pad_maximum_fusion.2
  32.7 19.3 %collective-permute-done.6.refs_7_ = bf16[2,128,512]{2,1,0:T(8,128)(2,1)S(1)} collective-permute-done((bf16[2,128,512]{2,1,0:T(8,128)(2,1)S(1)}, bf16[2,128,512]{2,1,0:T(8,128)(2,1)S(1)}, u32[]{:S(2)}, u32[]{:S(2)}) %collective-permute-start.6) | collective-permute-done | bytes 262176 | tf_op jit(solution)/shard_map/ppermute | solution.py:160
  52.0 7.0 %collective-permute-done.5.refs_6_ = bf16[2,128,512]{2,1,0:T(8,128)(2,1)S(1)} collective-permute-done((bf16[2,128,512]{2,1,0:T(8,128)(2,1)S(1)}, bf16[2,128,512]{2,1,0:T(8,128)(2,1)S(1)}, u32[]{:S(2)}, u32[]{:S(2)}) %collective-permute-start.5) | collective-permute-done | bytes 262176 | tf_op jit(solution)/shard_map/ppermute | solution.py:160
  59.0 0.7 copy-done.5
  59.7 3.5 %collective-permute-start = (bf16[2,128,512]{2,1,0:T(8,128)(2,1)S(1)}, bf16[2,128,512]{2,1,0:T(8,128)(2,1)}, u32[]{:S(2)}, u32[]{:S(2)}) collective-permute-start(bf16[2,128,512]{2,1,0:T(8,128)(2,1)S(1)} %pad_maximum_fusion.1), channel_id=1, source_target_pairs={{0,30},{1,31},{2,28},{3,29},{4,26},{5,27},{6,24},{7,25},{8,22},{9,... | collective-permute-start | bytes 786440 | tf_op jit(solution)/shard_map/ppermute | solution.py:160
  63.2 0.6 pad_add_fusion.blocks_ref
  63.8 0.7 pad_maximum_fusion.refs_0_
  64.5 6.4 %collective-permute-done.refs_1_ = bf16[2,128,512]{2,1,0:T(8,128)(2,1)} collective-permute-done((bf16[2,128,512]{2,1,0:T(8,128)(2,1)S(1)}, bf16[2,128,512]{2,1,0:T(8,128)(2,1)}, u32[]{:S(2)}, u32[]{:S(2)}) %collective-permute-start) | collective-permute-done | bytes 262176 | tf_op jit(solution)/shard_map/ppermute | solution.py:160
  71.0 1.3 copy-done
  72.3 36.7 %attention.1 = (bf16[128,512]{1,0:T(8,128)(2,1)}, bf16[128,512]{1,0:T(8,128)(2,1)}, bf16[128,512]{1,0:T(8,128)(2,1)}, bf16[128,512]{1,0:T(8,128)(2,1)}, bf16[128...) custom-call(s32[2]{0:T(128)} %pad_add_fusion.blocks_ref, ...), custom_call_target="tpu_custom_call" | custom-call | flops 20000000000 | bytes 8000000 | tf_op jit(solution)/shard_map/attention/pallas_call | solution.py:116
  109.0 7.4 %all-to-all-start.1 = ((bf16[32,2,128,128]{3,2,1,0:T(8,128)(2,1)}), bf16[32,2,128,128]{3,2,1,0:T(8,128)(2,1)S(1)}, u32[]{:S(2)}, u32[]{:S(2)}) async-start(bf16[32,2,128,128]{3,2,1,0:T(8,128)(2,1)} %get-tuple-element.19), calls=%async_computation.1 | async-start | bytes 4194304 | tf_op jit(solution)/shard_map/all_to_all | solution.py:166
  116.5 4.7 %collective-permute-start.7 = (bf16[128,512]{1,0:T(8,128)(2,1)}, bf16[128,512]{1,0:T(8,128)(2,1)S(1)}, u32[]{:S(2)}, u32[]{:S(2)}) collective-permute-start(bf16[128,512]{1,0:T(8,128)(2,1)} %get-tuple-element.12), channel_id=1, source_target_pairs={{0,30},{1,31},{2,28},{3,29},{4,26},{5,27},{6,24},{7,25},{8,22},{9,... | collective-permute-start | bytes 393224 | tf_op jit(solution)/shard_map/ppermute | solution.py:172
  121.2 2.1 %collective-permute-start.8 = (bf16[128,512]{1,0:T(8,128)(2,1)}, bf16[128,512]{1,0:T(8,128)(2,1)S(1)}, u32[]{:S(2)}, u32[]{:S(2)}) collective-permute-start(bf16[128,512]{1,0:T(8,128)(2,1)} %get-tuple-element.13), channel_id=1, source_target_pairs={{0,32},{1,33},{2,34},{3,35},{4,36},{5,37},{6,38},{7,39},{8,40},{9,... | collective-permute-start | bytes 393224 | tf_op jit(solution)/shard_map/ppermute | solution.py:172
  123.2 5.9 %collective-permute-start.11 = (bf16[128,512]{1,0:T(8,128)(2,1)}, bf16[128,512]{1,0:T(8,128)(2,1)S(1)}, u32[]{:S(2)}, u32[]{:S(2)}) collective-permute-start(bf16[128,512]{1,0:T(8,128)(2,1)} %get-tuple-element.16), channel_id=1, source_target_pairs={{0,94},{1,95},{2,92},{3,93},{4,90},{5,91},{6,88},{7,89},{8,86},{9,... | collective-permute-start | bytes 393224 | tf_op jit(solution)/shard_map/ppermute | solution.py:172
  129.2 18.2 %collective-permute-done.7 = bf16[128,512]{1,0:T(8,128)(2,1)S(1)} collective-permute-done((bf16[128,512]{1,0:T(8,128)(2,1)}, bf16[128,512]{1,0:T(8,128)(2,1)S(1)}, u32[]{:S(2)}, u32[]{:S(2)}) %collective-permute-start.7) | collective-permute-done | bytes 131104 | tf_op jit(solution)/shard_map/ppermute | solution.py:172
  147.4 2.2 %collective-permute-start.12 = (bf16[128,512]{1,0:T(8,128)(2,1)}, bf16[128,512]{1,0:T(8,128)(2,1)S(1)}, u32[]{:S(2)}, u32[]{:S(2)}) collective-permute-start(bf16[128,512]{1,0:T(8,128)(2,1)} %get-tuple-element.17), channel_id=1, source_target_pairs={{0,96},{1,97},{2,98},{3,99},{4,100},{5,101},{6,102},{7,103},{8,104... | collective-permute-start | bytes 393224 | tf_op jit(solution)/shard_map/ppermute | solution.py:172
  149.7 2.7 %collective-permute-done.9 = bf16[128,512]{1,0:T(8,128)(2,1)S(1)} collective-permute-done((bf16[128,512]{1,0:T(8,128)(2,1)}, bf16[128,512]{1,0:T(8,128)(2,1)S(1)}, u32[]{:S(2)}, u32[]{:S(2)}) %collective-permute-start.9) | collective-permute-done | bytes 131104 | tf_op jit(solution)/shard_map/ppermute | solution.py:172
  152.6 3.9 %collective-permute-done.12 = bf16[128,512]{1,0:T(8,128)(2,1)S(1)} collective-permute-done((bf16[128,512]{1,0:T(8,128)(2,1)}, bf16[128,512]{1,0:T(8,128)(2,1)S(1)}, u32[]{:S(2)}, u32[]{:S(2)}) %collective-permute-start.12) | collective-permute-done | bytes 131104 | tf_op jit(solution)/shard_map/ppermute | solution.py:172
  156.6 3.1 %collective-permute-done.13 = bf16[128,512]{1,0:T(8,128)(2,1)S(1)} collective-permute-done((bf16[128,512]{1,0:T(8,128)(2,1)S(1)}, bf16[128,512]{1,0:T(8,128)(2,1)S(1)}, u32[]{:S(2)}, u32[]{:S(2)}) %collective-permute-start.13) | collective-permute-done | bytes 131104 | tf_op jit(solution)/shard_map/ppermute | solution.py:172
  159.7 0.3 convert_reduce_fusion
  160.2 0.8 copy.13
  (44 shorter events, 0.9 us)
Async XLA Ops:
  4.7 11.4 %copy-start.1 = (bf16[1,128,4096]{2,1,0:T(8,128)(2,1)S(1)}, bf16[1,128,4096]{2,1,0:T(8,128)(2,1)}, u32[]{:S(2)}) copy-start(bf16[1,128,4096]{2,1,0:T(8,128)(2,1)} %param.5) | copy-start | bytes 3145732
  4.8 66.2 %all-to-all-start = ((bf16[32,2,128,128]{3,2,1,0:T(8,128)(2,1)}), bf16[32,2,128,128]{3,2,1,0:T(8,128)(2,1)S(1)}, u32[]{:S(2)}, u32[]{:S(2)}) async-start(bf16[32,2,128,128]{3,2,1,0:T(8,128)(2,1)} %bitcast.4), calls=%async_computation | async-start | bytes 4194304 | tf_op jit(solution)/shard_map/all_to_all | solution.py:161
  17.7 34.3 %collective-permute-start.6 = (bf16[2,128,512]{2,1,0:T(8,128)(2,1)S(1)}, bf16[2,128,512]{2,1,0:T(8,128)(2,1)S(1)}, u32[]{:S(2)}, u32[]{:S(2)}) collective-permute-start(bf16[2,128,512]{2,1,0:T(8,128)(2,1)S(1)} %pad_maximum_fusion.7), channel_id=1, source_target_pairs={{0,126},{1,127},{2,124},{3,125},{4,122},{5,123},{6,120},{7,121},{8... | collective-permute-start | bytes 786440 | tf_op jit(solution)/shard_map/ppermute | solution.py:160
  24.0 35.0 %collective-permute-start.5 = (bf16[2,128,512]{2,1,0:T(8,128)(2,1)S(1)}, bf16[2,128,512]{2,1,0:T(8,128)(2,1)S(1)}, u32[]{:S(2)}, u32[]{:S(2)}) collective-permute-start(bf16[2,128,512]{2,1,0:T(8,128)(2,1)S(1)} %pad_maximum_fusion.6), channel_id=1, source_target_pairs={{0,96},{1,97},{2,98},{3,99},{4,100},{5,101},{6,102},{7,103},{8,104... | collective-permute-start | bytes 786440 | tf_op jit(solution)/shard_map/ppermute | solution.py:160
  24.1 40.4 %collective-permute-start.4 = (bf16[2,128,512]{2,1,0:T(8,128)(2,1)S(1)}, bf16[2,128,512]{2,1,0:T(8,128)(2,1)}, u32[]{:S(2)}, u32[]{:S(2)}) collective-permute-start(bf16[2,128,512]{2,1,0:T(8,128)(2,1)S(1)} %pad_maximum_fusion.5), channel_id=1, source_target_pairs={{0,94},{1,95},{2,92},{3,93},{4,90},{5,91},{6,88},{7,89},{8,86},{9,... | collective-permute-start | bytes 786440 | tf_op jit(solution)/shard_map/ppermute | solution.py:160
  25.0 39.5 %collective-permute-start.3 = (bf16[2,128,512]{2,1,0:T(8,128)(2,1)S(1)}, bf16[2,128,512]{2,1,0:T(8,128)(2,1)}, u32[]{:S(2)}, u32[]{:S(2)}) collective-permute-start(bf16[2,128,512]{2,1,0:T(8,128)(2,1)S(1)} %pad_maximum_fusion.4), channel_id=1, source_target_pairs={{0,64},{1,65},{2,66},{3,67},{4,68},{5,69},{6,70},{7,71},{8,72},{9,... | collective-permute-start | bytes 786440 | tf_op jit(solution)/shard_map/ppermute | solution.py:160
  25.8 38.7 %collective-permute-start.2 = (bf16[2,128,512]{2,1,0:T(8,128)(2,1)S(1)}, bf16[2,128,512]{2,1,0:T(8,128)(2,1)}, u32[]{:S(2)}, u32[]{:S(2)}) collective-permute-start(bf16[2,128,512]{2,1,0:T(8,128)(2,1)S(1)} %pad_maximum_fusion.3), channel_id=1, source_target_pairs={{0,62},{1,63},{2,60},{3,61},{4,58},{5,59},{6,56},{7,57},{8,54},{9,... | collective-permute-start | bytes 786440 | tf_op jit(solution)/shard_map/ppermute | solution.py:160
  52.0 7.0 %copy-start.4 = (bf16[2,128,512]{2,1,0:T(8,128)(2,1)}, bf16[2,128,512]{2,1,0:T(8,128)(2,1)S(1)}, u32[]{:S(2)}) copy-start(bf16[2,128,512]{2,1,0:T(8,128)(2,1)S(1)} %collective-permute-done.6.refs_7_) | copy-start | bytes 786436
  52.0 12.5 %collective-permute-start.1 = (bf16[2,128,512]{2,1,0:T(8,128)(2,1)}, bf16[2,128,512]{2,1,0:T(8,128)(2,1)}, u32[]{:S(2)}, u32[]{:S(2)}) collective-permute-start(bf16[2,128,512]{2,1,0:T(8,128)(2,1)} %pad_maximum_fusion.2), channel_id=1, source_target_pairs={{0,32},{1,33},{2,34},{3,35},{4,36},{5,37},{6,38},{7,39},{8,40},{9,... | collective-permute-start | bytes 786440 | tf_op jit(solution)/shard_map/ppermute | solution.py:160
  59.0 0.7 copy-start.5
  59.7 11.3 %collective-permute-start = (bf16[2,128,512]{2,1,0:T(8,128)(2,1)S(1)}, bf16[2,128,512]{2,1,0:T(8,128)(2,1)}, u32[]{:S(2)}, u32[]{:S(2)}) collective-permute-start(bf16[2,128,512]{2,1,0:T(8,128)(2,1)S(1)} %pad_maximum_fusion.1), channel_id=1, source_target_pairs={{0,30},{1,31},{2,28},{3,29},{4,26},{5,27},{6,24},{7,25},{8,22},{9,... | collective-permute-start | bytes 786440 | tf_op jit(solution)/shard_map/ppermute | solution.py:160
  71.0 1.3 copy-start
  109.0 20.2 %copy-start.3 = (bf16[128,512]{1,0:T(8,128)(2,1)S(1)}, bf16[128,512]{1,0:T(8,128)(2,1)}, u32[]{:S(2)}) copy-start(bf16[128,512]{1,0:T(8,128)(2,1)} %get-tuple-element.11) | copy-start | bytes 393220
  109.0 40.6 %copy-start.6 = (bf16[128,512]{1,0:T(8,128)(2,1)S(1)}, bf16[128,512]{1,0:T(8,128)(2,1)}, u32[]{:S(2)}) copy-start(bf16[128,512]{1,0:T(8,128)(2,1)} %get-tuple-element.18) | copy-start | bytes 393220
  109.0 50.6 %all-to-all-start.1 = ((bf16[32,2,128,128]{3,2,1,0:T(8,128)(2,1)}), bf16[32,2,128,128]{3,2,1,0:T(8,128)(2,1)S(1)}, u32[]{:S(2)}, u32[]{:S(2)}) async-start(bf16[32,2,128,128]{3,2,1,0:T(8,128)(2,1)} %get-tuple-element.19), calls=%async_computation.1 | async-start | bytes 4194304 | tf_op jit(solution)/shard_map/all_to_all | solution.py:166
  116.5 30.9 %collective-permute-start.7 = (bf16[128,512]{1,0:T(8,128)(2,1)}, bf16[128,512]{1,0:T(8,128)(2,1)S(1)}, u32[]{:S(2)}, u32[]{:S(2)}) collective-permute-start(bf16[128,512]{1,0:T(8,128)(2,1)} %get-tuple-element.12), channel_id=1, source_target_pairs={{0,30},{1,31},{2,28},{3,29},{4,26},{5,27},{6,24},{7,25},{8,22},{9,... | collective-permute-start | bytes 393224 | tf_op jit(solution)/shard_map/ppermute | solution.py:172
  121.2 28.4 %collective-permute-start.8 = (bf16[128,512]{1,0:T(8,128)(2,1)}, bf16[128,512]{1,0:T(8,128)(2,1)S(1)}, u32[]{:S(2)}, u32[]{:S(2)}) collective-permute-start(bf16[128,512]{1,0:T(8,128)(2,1)} %get-tuple-element.13), channel_id=1, source_target_pairs={{0,32},{1,33},{2,34},{3,35},{4,36},{5,37},{6,38},{7,39},{8,40},{9,... | collective-permute-start | bytes 393224 | tf_op jit(solution)/shard_map/ppermute | solution.py:172
  123.2 29.2 %collective-permute-start.9 = (bf16[128,512]{1,0:T(8,128)(2,1)}, bf16[128,512]{1,0:T(8,128)(2,1)S(1)}, u32[]{:S(2)}, u32[]{:S(2)}) collective-permute-start(bf16[128,512]{1,0:T(8,128)(2,1)} %get-tuple-element.14), channel_id=1, source_target_pairs={{0,62},{1,63},{2,60},{3,61},{4,58},{5,59},{6,56},{7,57},{8,54},{9,... | collective-permute-start | bytes 393224 | tf_op jit(solution)/shard_map/ppermute | solution.py:172
  123.2 29.2 %collective-permute-start.10 = (bf16[128,512]{1,0:T(8,128)(2,1)}, bf16[128,512]{1,0:T(8,128)(2,1)S(1)}, u32[]{:S(2)}, u32[]{:S(2)}) collective-permute-start(bf16[128,512]{1,0:T(8,128)(2,1)} %get-tuple-element.15), channel_id=1, source_target_pairs={{0,64},{1,65},{2,66},{3,67},{4,68},{5,69},{6,70},{7,71},{8,72},{9,... | collective-permute-start | bytes 393224 | tf_op jit(solution)/shard_map/ppermute | solution.py:172
  123.2 29.4 %collective-permute-start.11 = (bf16[128,512]{1,0:T(8,128)(2,1)}, bf16[128,512]{1,0:T(8,128)(2,1)S(1)}, u32[]{:S(2)}, u32[]{:S(2)}) collective-permute-start(bf16[128,512]{1,0:T(8,128)(2,1)} %get-tuple-element.16), channel_id=1, source_target_pairs={{0,94},{1,95},{2,92},{3,93},{4,90},{5,91},{6,88},{7,89},{8,86},{9,... | collective-permute-start | bytes 393224 | tf_op jit(solution)/shard_map/ppermute | solution.py:172
  147.4 9.1 %collective-permute-start.12 = (bf16[128,512]{1,0:T(8,128)(2,1)}, bf16[128,512]{1,0:T(8,128)(2,1)S(1)}, u32[]{:S(2)}, u32[]{:S(2)}) collective-permute-start(bf16[128,512]{1,0:T(8,128)(2,1)} %get-tuple-element.17), channel_id=1, source_target_pairs={{0,96},{1,97},{2,98},{3,99},{4,100},{5,101},{6,102},{7,103},{8,104... | collective-permute-start | bytes 393224 | tf_op jit(solution)/shard_map/ppermute | solution.py:172
  149.6 10.0 %collective-permute-start.13 = (bf16[128,512]{1,0:T(8,128)(2,1)S(1)}, bf16[128,512]{1,0:T(8,128)(2,1)S(1)}, u32[]{:S(2)}, u32[]{:S(2)}) collective-permute-start(bf16[128,512]{1,0:T(8,128)(2,1)S(1)} %copy-done.6), channel_id=1, source_target_pairs={{0,126},{1,127},{2,124},{3,125},{4,122},{5,123},{6,120},{7,121},{8... | collective-permute-start | bytes 393224 | tf_op jit(solution)/shard_map/ppermute | solution.py:172
  159.7 1.3 copy-start.2

commit v2 on v1

v2 whole, which is shorter than its diff:
```python
import functools
import math

import jax
import jax.numpy as jnp
from jax import lax
from jax.experimental import pallas as pl
from jax.experimental.pallas import tpu as pltpu
from jax.sharding import PartitionSpec as P

HEAD_DIM = 128
GROUPS = 4
QUANT_BLOCK = 32
ROWS = 128
BLOCKS = 32
WIDTH = GROUPS * HEAD_DIM
AXES = ("section", "blk")
SCALE = 1.0 / math.sqrt(HEAD_DIM)
EXP2_SCALE = SCALE * math.log2(math.e)
F32 = jnp.float32
BF16 = jnp.bfloat16
NT = (((1,), (1,)), ((), ()))
NN = (((1,), (0,)), ((), ()))

LAYERS = 2
KEYS = 512
SPAN = KEYS // ROWS
GROUP_ROWS = LAYERS * WIDTH
CHUNKS = BLOCKS // SPAN


def flip(blk):
    return blk ^ 30


def attention_kernel(first, blocks_ref, *refs):
    units, kv_ref, refs = (refs[0:2], refs[2:4]), refs[4], refs[5:]
    if not first:
        dk_in, dv_in, refs = refs[0], refs[1], refs[2:]
    outs, refs = refs[:2], refs[2:]
    if first:
        dk_s, dv_s, refs = refs[0], refs[1], refs[2:]
    else:
        term_ref, refs = refs[0], refs[1:]
    q_s, do_s, kt_s, w_s, g_s, m_s, dq_s = refs[:7]
    if not first:
        dk_s, dv_s = refs[7:]
    for n in range(2):
        for layer in range(LAYERS):
            for g in range(GROUPS):
                lo = layer * WIDTH + g * HEAD_DIM
                columns = slice(g * HEAD_DIM, (g + 1) * HEAD_DIM)
                q_s[n, lo : lo + ROWS, :] = units[n][layer][0, 0, :, columns]
                do_s[n, lo : lo + ROWS, :] = units[n][layer][0, 1, :, columns]
    for j in range(BLOCKS):
        kt_s[:, j * ROWS : (j + 1) * ROWS] = kv_ref[j, 0].T
    if first:
        dk_s[...] = jnp.zeros_like(dk_s)
        dv_s[...] = jnp.zeros_like(dv_s)
    else:
        dk_s[...] = dk_in[...]
        dv_s[...] = dv_in[...]

    def one_group(group, _):
        block = blocks_ref[group]
        last = block // SPAN
        q, do = q_s.at[group], do_s.at[group]

        def keys(j, which):
            return kv_ref[pl.ds(j * SPAN, SPAN), which].reshape(KEYS, HEAD_DIM)

        def fold(x, op):
            return op(x.reshape(KEYS // 8, 8, GROUP_ROWS), axis=0)

        def forward(j, carry, masked):
            top, total8, dot8 = carry
            scores = lax.dot_general(keys(j, 0), q[...], NT, preferred_element_type=F32)
            if masked:
                key_at = lax.broadcasted_iota(jnp.int32, (KEYS, GROUP_ROWS), 0)
                row_at = lax.broadcasted_iota(jnp.int32, (KEYS, GROUP_ROWS), 1) & (ROWS - 1)
                scores = jnp.where(key_at <= row_at + (block - j * SPAN) * ROWS, scores, -1e30)
            prob_grad = lax.dot_general(keys(j, 1), do[...], NT, preferred_element_type=F32)
            here = jnp.max(fold(scores, jnp.max), axis=0, keepdims=True) * EXP2_SCALE
            new_top = here if masked else jnp.maximum(top, here)
            weights = jnp.exp2(scores * EXP2_SCALE - new_top)
            w_s[j] = weights
            g_s[j] = prob_grad
            m_s[j] = jnp.broadcast_to(new_top, (8, GROUP_ROWS))
            total, dot = fold(weights, jnp.sum), fold(weights * prob_grad, jnp.sum)
            if masked:
                return new_top, total, dot
            factor = jnp.exp2(top - new_top)
            return new_top, total8 * factor + total, dot8 * factor + dot

        start = forward(last, (None, None, None), True)
        top, total8, dot8 = lax.fori_loop(0, last, lambda j, c: forward(j, c, False), start)
        inverse = 1.0 / jnp.sum(total8, axis=0, keepdims=True)
        delta = jnp.sum(dot8, axis=0, keepdims=True) * inverse
        dq_s[...] = jnp.zeros_like(dq_s)

        def backward(j, _):
            factor = jnp.exp2(m_s[j][0:1] - top) * inverse
            probs = w_s[j] * factor
            score_grad = (probs * (g_s[j] - delta)).astype(BF16)
            dv_s[j] += lax.dot_general(probs.astype(BF16), do[...], NN, preferred_element_type=F32)
            dk_s[j] += lax.dot_general(score_grad, q[...], NN, preferred_element_type=F32)
            columns = kt_s[:, pl.ds(pl.multiple_of(j * KEYS, KEYS), KEYS)]
            dq_s[...] += lax.dot_general(columns, score_grad, NN, preferred_element_type=F32)
            return 0

        lax.fori_loop(0, last + 1, backward, 0)
        for h in range(GROUP_ROWS // ROWS):
            part = dq_s[:, h * ROWS : (h + 1) * ROWS]
            q_s[group, h * ROWS : (h + 1) * ROWS, :] = (part.T * SCALE).astype(BF16)
        return 0

    lax.fori_loop(0, 2, one_group, 0)
    for n in range(2):
        for layer in range(LAYERS):
            for g in range(GROUPS):
                lo = layer * WIDTH + g * HEAD_DIM
                outs[n][layer, :, g * HEAD_DIM : (g + 1) * HEAD_DIM] = q_s[n, lo : lo + ROWS, :]
    if not first:
        for j in range(CHUNKS):
            blocks = slice(j * SPAN, (j + 1) * SPAN)
            term_ref[blocks, 0] = (dk_s[j] * SCALE).astype(BF16).reshape(SPAN, ROWS, HEAD_DIM)
            term_ref[blocks, 1] = dv_s[j].astype(BF16).reshape(SPAN, ROWS, HEAD_DIM)


def attention(blocks, units, kv, sums=None):
    first = sums is None
    vmem = pl.BlockSpec(memory_space=pltpu.VMEM)
    total = (CHUNKS, KEYS, HEAD_DIM)
    grads = [jax.ShapeDtypeStruct((LAYERS, ROWS, WIDTH), BF16)] * 2
    scratch = [
        pltpu.VMEM((2, GROUP_ROWS, HEAD_DIM), BF16),
        pltpu.VMEM((2, GROUP_ROWS, HEAD_DIM), BF16),
        pltpu.VMEM((HEAD_DIM, BLOCKS * ROWS), BF16),
        pltpu.VMEM((CHUNKS, KEYS, GROUP_ROWS), F32),
        pltpu.VMEM((CHUNKS, KEYS, GROUP_ROWS), F32),
        pltpu.VMEM((CHUNKS, 8, GROUP_ROWS), F32),
        pltpu.VMEM((HEAD_DIM, GROUP_ROWS), F32),
    ]
    if first:
        outs = grads + [jax.ShapeDtypeStruct(total, F32)] * 2
    else:
        outs = grads + [jax.ShapeDtypeStruct((BLOCKS, 2, ROWS, HEAD_DIM), BF16)]
        scratch += [pltpu.VMEM(total, F32)] * 2
    args = [*units[0], *units[1], kv] + ([] if first else list(sums))
    return pl.pallas_call(
        functools.partial(attention_kernel, first),
        out_shape=outs,
        in_specs=[pl.BlockSpec(memory_space=pltpu.SMEM)] + [vmem] * len(args),
        out_specs=[vmem] * len(outs),
        scratch_shapes=scratch,
        compiler_params=pltpu.CompilerParams(vmem_limit_bytes=60 * 1024 * 1024),
        cost_estimate=pl.CostEstimate(flops=12_000_000_000, bytes_accessed=8_000_000, transcendentals=4_500_000),
        name="attention_first" if first else "attention_second",
    )(blocks, *args)


CORE, FLIP, NEAR = 1, 2, 4


def partners(k):
    return [
        (s * BLOCKS + b, (s ^ (k & CORE) ^ (2 if k & NEAR else 0)) * BLOCKS + (flip(b) if k & FLIP else b))
        for s in range(4)
        for b in range(BLOCKS)
    ]


def move(x, k):
    return lax.ppermute(x, AXES, partners(k)) if k else x


def shards(queries, out_grad, kv_codes, kv_scales):
    section, blk = lax.axis_index("section"), lax.axis_index("blk")
    head = section * 2 + blk // 16

    def of(k):
        return head ^ (4 if k & NEAR else 0) ^ (2 if k & CORE else 0) ^ (1 if k & FLIP else 0)

    codes = kv_codes.reshape(2, ROWS // QUANT_BLOCK, QUANT_BLOCK, 2, HEAD_DIM).astype(F32)
    cache = (codes * kv_scales[:, :, None, :, None]).astype(BF16)
    cache = cache.reshape(2, ROWS, 2, HEAD_DIM).transpose(2, 0, 1, 3)
    spread = jnp.broadcast_to(cache[:, None], (2, 16, 2, ROWS, HEAD_DIM)).reshape(BLOCKS, 2, ROWS, HEAD_DIM)
    kv = lax.all_to_all(spread, "blk", 0, 0, tiled=True)

    def pick(k):
        at = of(k) * WIDTH
        return [lax.dynamic_slice_in_dim(queries[0], at, WIDTH, 1), lax.dynamic_slice_in_dim(out_grad[0], at, WIDTH, 1)]

    def packed(k):
        return jnp.stack(pick(k) + pick(k | CORE)).reshape(2, 2, ROWS, WIDTH)

    def fetch(x):
        return (x, move(x[1:], CORE))

    def give(x):
        return (x[0], move(x[1], CORE))

    blocks = jnp.stack([blk, flip(blk)]).astype(jnp.int32)
    own = packed(0)
    turned = move(packed(FLIP), FLIP)
    near, near_turned, kv = lax.optimization_barrier((packed(NEAR), packed(NEAR | FLIP), kv))
    near = move(near, NEAR)
    near_turned = move(near_turned, NEAR | FLIP)
    d_own, d_turned, *sums = attention(blocks, (fetch(own), fetch(turned)), kv)
    d_near, d_near_turned, term = attention(blocks, (fetch(near), fetch(near_turned)), kv, sums)

    received = lax.all_to_all(term, "blk", 0, 0, tiled=True)
    kv_grad = received.reshape(2, 16, 2, ROWS, HEAD_DIM).astype(F32).sum(1)
    kv_grad = kv_grad.transpose(1, 2, 0, 3).reshape(2, ROWS, 2 * HEAD_DIM)

    query_grad = jnp.zeros((ROWS, 8 * WIDTH), BF16)
    for k, grad in ((0, d_own), (FLIP, d_turned), (NEAR, d_near), (NEAR | FLIP, d_near_turned)):
        for c, part in enumerate(give(move(grad, k))):
            query_grad = lax.dynamic_update_slice_in_dim(query_grad, part, of(k | c) * WIDTH, 1)
    return query_grad[None], kv_grad


def solution(mesh):
    in_specs = (
        P("section", "blk", None),
        P("section", "blk", None),
        P(None, "blk", "section"),
        P(None, "blk", "section"),
    )
    out_specs = (P("section", "blk", None), P(None, "blk", "section"))
    return jax.shard_map(shards, mesh=mesh, in_specs=in_specs, out_specs=out_specs, check_vma=False)
```

time: 161 us -> 184 us (1.14)
  starting transfers between devices: 51.3 us -> 57.9 us
  Pallas kernels: 36.7 us -> 42.7 us
  local copies, waits for them, and re-layouts: 7.53 us -> 12.4 us
  waiting for transfers between devices: 60.7 us -> 63.4 us
  other arithmetic: 3.84 us -> 5.72 us
    all_to_all x1, waiting for transfers between devices: 0.01 us -> 21.2 us  [shards(): kv = lax.all_to_all(spread, 'blk', 0, 0, tiled=True)]
    ppermute x14, waiting for transfers between devices: 60.7 us -> 42.1 us  [move(): return lax.ppermute(x, AXES, partners(k)) if k else x]
    all_to_all x1, starting transfers between devices: 7.4 us -> 15.6 us  [shards(): received = lax.all_to_all(term, 'blk', 0, 0, tiled=True)]
    pallas_call x1 -> x2, Pallas kernels: 36.7 us -> 42.7 us  [attention(): pl.pallas_call(functools.partial(attention_kernel, first), out_shape=outs...]
    slice x0 -> x3, local copies, waits for them, and re-layouts: none -> 3.61 us  [fetch(): return (x, move(x[1:], CORE))]
  transfers between devices with their start and end apart: 16 -> 16, of which waited for: 8 -> 6; matrix products, arithmetic and copies ran while one was open for 2% -> 7% of each run, Pallas kernels for 0% -> 23%
where the time goes in v2:
time: 184 us; the launch traced here: 183 us
  waiting for transfers between devices  63.4 us (34%)
  starting transfers between devices  57.9 us (31%)
  Pallas kernels  42.7 us (23%)
  local copies, waits for them, and re-layouts  12.4 us (7%)
  other arithmetic  5.72 us (3%)
    pallas_call x2, Pallas kernels, attention(): pl.pallas_call(functools.partial(attention_kernel, first), out_shape=outs...  42.7 us
    ppermute x14, waiting for transfers between devices, move(): return lax.ppermute(x, AXES, partners(k)) if k else x  42.1 us
    ppermute x14, starting transfers between devices, move(): return lax.ppermute(x, AXES, partners(k)) if k else x  31 us
    all_to_all x1, waiting for transfers between devices, shards(): kv = lax.all_to_all(spread, 'blk', 0, 0, tiled=True)  21.2 us
    all_to_all x1, starting transfers between devices, shards(): received = lax.all_to_all(term, 'blk', 0, 0, tiled=True)  15.6 us
    all_to_all x1, starting transfers between devices, shards(): kv = lax.all_to_all(spread, 'blk', 0, 0, tiled=True)  11.3 us
  transfers between devices with their start and end apart: 16, of which 6 were waited for; matrix products, arithmetic and copies ran while one was open for 7% of the time, Pallas kernels for 23%

profile of v2, /device:TPU:1, one launch (start us, length us, event | category | flops | bytes accessed | tf_op | source)
XLA Modules:
  0.0 183.0 jit_solution(6527307149916630988)
XLA Ops:
  0.6 1.0 convert_element_type.17
  1.7 0.8 copy.10
  2.9 1.8 %broadcast_in_dim.20 = bf16[2,16,2,128,128]{4,3,2,1,0:T(8,128)(2,1)} broadcast(bf16[2,2,128,128]{3,2,1,0:T(8,128)(2,1)S(1)} %copy.11), dimensions={0,2,3,4} | broadcast | bytes 2228224 | tf_op jit(solution)/shard_map/broadcast_in_dim | solution.py:187
  4.8 11.3 %all-to-all-start = ((bf16[32,2,128,128]{3,2,1,0:T(8,128)(2,1)}), bf16[32,2,128,128]{3,2,1,0:T(8,128)(2,1)S(1)}, u32[]{:S(2)}, u32[]{:S(2)}) async-start(bf16[32,2,128,128]{3,2,1,0:T(8,128)(2,1)} %bitcast.9), calls=%async_computation | async-start | bytes 4194304 | tf_op jit(solution)/shard_map/all_to_all | solution.py:188
  16.1 2.2 %constant_dynamic-slice_fusion.2 = (bf16[1,128,512]{2,1,0:T(8,128)(2,1)S(1)}, bf16[1,128,512]{2,1,0:T(8,128)(2,1)S(1)}, bf16[1,128,512]{2,1,0:T(8,128)(2,1)S(1)}...) fusion(bf16[1,128,4096]{2,1,0:T(8,128)(2,1)S(1)} %copy-done.1, ...), kind=kLoop, calls=%fused_computation.22 | loop fusion | bytes 4194336 | tf_op jit(solution)/shard_map/dynamic_slice | solution.py:192
  18.3 0.9 pad_maximum_fusion.1
  19.2 4.6 %collective-permute-start.1 = (bf16[2,2,128,512]{3,2,1,0:T(8,128)(2,1)}, bf16[2,2,128,512]{3,2,1,0:T(8,128)(2,1)}, u32[]{:S(2)}, u32[]{:S(2)}) collective-permute-start(bf16[2,2,128,512]{3,2,1,0:T(8,128)(2,1)} %bitcast.4), channel_id=1, source_target_pairs={{0,30},{1,31},{2,28},{3,29},{4,26},{5,27},{6,24},{7,25},{8,22},{9,... | collective-permute-start | bytes 1572872 | tf_op jit(solution)/shard_map/ppermute | solution.py:174
  24.0 21.2 %all-to-all-done.refs_4_ = bf16[32,2,128,128]{3,2,1,0:T(8,128)(2,1)S(1)} async-done(((bf16[32,2,128,128]{3,2,1,0:T(8,128)(2,1)}), bf16[32,2,128,128]{3,2,1,0:T(8,128)(2,1)S(1)}, u32[]{:S(2)}, u32[]{:S(2)}) %all-to-all-start) | async-done | bytes 2097184 | tf_op jit(solution)/shard_map/all_to_all | solution.py:188
  45.2 0.7 collective-permute-start.6
  45.9 2.4 %collective-permute-start.8 = (bf16[2,2,128,512]{3,2,1,0:T(8,128)(2,1)S(1)}, bf16[2,2,128,512]{3,2,1,0:T(8,128)(2,1)}, u32[]{:S(2)}, u32[]{:S(2)}) collective-permute-start(bf16[2,2,128,512]{3,2,1,0:T(8,128)(2,1)S(1)} %bitcast.35), channel_id=1, source_target_pairs={{0,94},{1,95},{2,92},{3,93},{4,90},{5,91},{6,88},{7,89},{8,86},{9,... | collective-permute-start | bytes 1572872 | tf_op jit(solution)/shard_map/ppermute | solution.py:174
  49.0 2.4 %collective-permute-start = (bf16[1,2,128,512]{3,2,1,0:T(8,128)(2,1)}, bf16[1,2,128,512]{3,2,1,0:T(8,128)(2,1)}, u32[]{:S(2)}, u32[]{:S(2)}) collective-permute-start(bf16[1,2,128,512]{3,2,1,0:T(8,128)(2,1)} %maximum_bitcast_fusion), channel_id=1, source_target_pairs={{0,32},{1,33},{2,34},{3,35},{4,36},{5,37},{6,38},{7,39},{8,40},{9,... | collective-permute-start | bytes 786440 | tf_op jit(solution)/shard_map/ppermute | solution.py:174
  51.5 4.5 %collective-permute-done.1.refs_2_ = bf16[2,2,128,512]{3,2,1,0:T(8,128)(2,1)} collective-permute-done((bf16[2,2,128,512]{3,2,1,0:T(8,128)(2,1)}, bf16[2,2,128,512]{3,2,1,0:T(8,128)(2,1)}, u32[]{:S(2)}, u32[]{:S(2)}) %collective-permute-start.1) | collective-permute-done | bytes 524320 | tf_op jit(solution)/shard_map/ppermute | solution.py:174
  55.9 1.7 slice.50
  57.6 2.0 %collective-permute-start.2 = (bf16[1,2,128,512]{3,2,1,0:T(8,128)(2,1)}, bf16[1,2,128,512]{3,2,1,0:T(8,128)(2,1)}, u32[]{:S(2)}, u32[]{:S(2)}) collective-permute-start(bf16[1,2,128,512]{3,2,1,0:T(8,128)(2,1)} %slice.50), channel_id=1, source_target_pairs={{0,32},{1,33},{2,34},{3,35},{4,36},{5,37},{6,38},{7,39},{8,40},{9,... | collective-permute-start | bytes 786440 | tf_op jit(solution)/shard_map/ppermute | solution.py:174
  60.2 1.8 pad_maximum_fusion
  61.9 1.0 slice.53
  62.9 9.0 %collective-permute-start.7 = (bf16[1,2,128,512]{3,2,1,0:T(8,128)(2,1)S(1)}, bf16[1,2,128,512]{3,2,1,0:T(8,128)(2,1)S(1)}, u32[]{:S(2)}, u32[]{:S(2)}) collective-permute-start(bf16[1,2,128,512]{3,2,1,0:T(8,128)(2,1)S(1)} %slice.53), channel_id=1, source_target_pairs={{0,32},{1,33},{2,34},{3,35},{4,36},{5,37},{6,38},{7,39},{8,40},{9,... | collective-permute-start | bytes 786440 | tf_op jit(solution)/shard_map/ppermute | solution.py:174
  71.9 1.0 slice.54
  73.0 21.0 %attention_first.1 = (bf16[2,128,512]{2,1,0:T(8,128)(2,1)}, bf16[2,128,512]{2,1,0:T(8,128)(2,1)}, f32[8,512,128]{2,1,0:T(8,128)}, f32[8,512,128]{2,1,0:T(8,128)}) custom-call(s32[2]{0:T(128)} %pad_add_fusion.blocks_ref, bf16[2,2,128,512]{3,2,1,0:T(8,128)(2,1)} %bitcast.37, bf16[1,2,128,512]{3,2,1,0:T(8,128)(2,1)} %collective-permute-done.refs_1_, ...), custom_call_target="tpu_custom_call" | custom-call | flops 12000000000 | bytes 8000000 | tf_op jit(solution)/shard_map/attention_first/pallas_call | solution.py:150
  94.0 1.9 %collective-permute-start.4 = (bf16[2,128,512]{2,1,0:T(8,128)(2,1)}, bf16[2,128,512]{2,1,0:T(8,128)(2,1)S(1)}, u32[]{:S(2)}, u32[]{:S(2)}) collective-permute-start(bf16[2,128,512]{2,1,0:T(8,128)(2,1)} %get-tuple-element.14), channel_id=1, source_target_pairs={{0,30},{1,31},{2,28},{3,29},{4,26},{5,27},{6,24},{7,25},{8,22},{9,... | collective-permute-start | bytes 786440 | tf_op jit(solution)/shard_map/ppermute | solution.py:174
  96.0 1.0 slice_bitcast_fusion.3
  97.0 0.8 collective-permute-start.3
  98.7 21.7 %attention_second.1 = (bf16[2,128,512]{2,1,0:T(8,128)(2,1)}, bf16[2,128,512]{2,1,0:T(8,128)(2,1)}, bf16[32,2,128,128]{3,2,1,0:T(8,128)(2,1)}) custom-call(s32[2]{0:T(128)} %pad_add_fusion.blocks_ref, bf16[2,2,128,512]{3,2,1,0:T(8,128)(2,1)} %collective-permute-done.6.refs_0_, bf16[1,2,128,512]{3,2,1,0:T(8,128)(2,1)} %copy-done.3, ...), custom_call_target="tpu_custom_call" | custom-call | flops 12000000000 | bytes 8000000 | tf_op jit(solution)/shard_map/attention_second/pallas_call | solution.py:150
  120.4 15.6 %all-to-all-start.1 = ((bf16[32,2,128,128]{3,2,1,0:T(8,128)(2,1)}), bf16[32,2,128,128]{3,2,1,0:T(8,128)(2,1)S(1)}, u32[]{:S(2)}, u32[]{:S(2)}) async-start(bf16[32,2,128,128]{3,2,1,0:T(8,128)(2,1)} %get-tuple-element.21), calls=%async_computation.1 | async-start | bytes 4194304 | tf_op jit(solution)/shard_map/all_to_all | solution.py:212
  136.0 0.9 bitcast_dynamic-update-slice_fusion.3
  137.3 0.7 collective-permute-start.10
  138.4 28.4 %collective-permute-done.10 = bf16[2,128,512]{2,1,0:T(8,128)(2,1)S(1)} collective-permute-done((bf16[2,128,512]{2,1,0:T(8,128)(2,1)}, bf16[2,128,512]{2,1,0:T(8,128)(2,1)S(1)}, u32[]{:S(2)}, u32[]{:S(2)}) %collective-permute-start.10) | collective-permute-done | bytes 262176 | tf_op jit(solution)/shard_map/ppermute | solution.py:174
  167.4 4.3 %collective-permute-start.12 = (bf16[2,128,512]{2,1,0:T(8,128)(2,1)}, bf16[2,128,512]{2,1,0:T(8,128)(2,1)S(1)}, u32[]{:S(2)}, u32[]{:S(2)}) collective-permute-start(bf16[2,128,512]{2,1,0:T(8,128)(2,1)} %get-tuple-element.20), channel_id=1, source_target_pairs={{0,94},{1,95},{2,92},{3,93},{4,90},{5,91},{6,88},{7,89},{8,86},{9,... | collective-permute-start | bytes 786440 | tf_op jit(solution)/shard_map/ppermute | solution.py:174
  171.7 7.9 %collective-permute-done.12 = bf16[2,128,512]{2,1,0:T(8,128)(2,1)S(1)} collective-permute-done((bf16[2,128,512]{2,1,0:T(8,128)(2,1)}, bf16[2,128,512]{2,1,0:T(8,128)(2,1)S(1)}, u32[]{:S(2)}, u32[]{:S(2)}) %collective-permute-start.12) | collective-permute-done | bytes 262176 | tf_op jit(solution)/shard_map/ppermute | solution.py:174
  179.7 1.0 collective-permute-start.13
  180.6 1.0 collective-permute-done.13
  182.1 0.8 copy.13
  (41 shorter events, 4.8 us)
Async XLA Ops:
  4.7 11.4 %copy-start.1 = (bf16[1,128,4096]{2,1,0:T(8,128)(2,1)S(1)}, bf16[1,128,4096]{2,1,0:T(8,128)(2,1)}, u32[]{:S(2)}) copy-start(bf16[1,128,4096]{2,1,0:T(8,128)(2,1)} %param.5) | copy-start | bytes 3145732
  4.8 40.4 %all-to-all-start = ((bf16[32,2,128,128]{3,2,1,0:T(8,128)(2,1)}), bf16[32,2,128,128]{3,2,1,0:T(8,128)(2,1)S(1)}, u32[]{:S(2)}, u32[]{:S(2)}) async-start(bf16[32,2,128,128]{3,2,1,0:T(8,128)(2,1)} %bitcast.9), calls=%async_computation | async-start | bytes 4194304 | tf_op jit(solution)/shard_map/all_to_all | solution.py:188
  19.2 36.7 %collective-permute-start.1 = (bf16[2,2,128,512]{3,2,1,0:T(8,128)(2,1)}, bf16[2,2,128,512]{3,2,1,0:T(8,128)(2,1)}, u32[]{:S(2)}, u32[]{:S(2)}) collective-permute-start(bf16[2,2,128,512]{3,2,1,0:T(8,128)(2,1)} %bitcast.4), channel_id=1, source_target_pairs={{0,30},{1,31},{2,28},{3,29},{4,26},{5,27},{6,24},{7,25},{8,22},{9,... | collective-permute-start | bytes 1572872 | tf_op jit(solution)/shard_map/ppermute | solution.py:174
  45.2 27.8 %copy-start = (bf16[32,2,128,128]{3,2,1,0:T(8,128)(2,1)}, bf16[32,2,128,128]{3,2,1,0:T(8,128)(2,1)S(1)}, u32[]{:S(2)}) copy-start(bf16[32,2,128,128]{3,2,1,0:T(8,128)(2,1)S(1)} %all-to-all-done.refs_4_) | copy-start | bytes 6291460
  45.2 16.7 %collective-permute-start.6 = (bf16[2,2,128,512]{3,2,1,0:T(8,128)(2,1)S(1)}, bf16[2,2,128,512]{3,2,1,0:T(8,128)(2,1)}, u32[]{:S(2)}, u32[]{:S(2)}) collective-permute-start(bf16[2,2,128,512]{3,2,1,0:T(8,128)(2,1)S(1)} %bitcast.36), channel_id=1, source_target_pairs={{0,64},{1,65},{2,66},{3,67},{4,68},{5,69},{6,70},{7,71},{8,72},{9,... | collective-permute-start | bytes 1572872 | tf_op jit(solution)/shard_map/ppermute | solution.py:174
  45.9 26.0 %collective-permute-start.8 = (bf16[2,2,128,512]{3,2,1,0:T(8,128)(2,1)S(1)}, bf16[2,2,128,512]{3,2,1,0:T(8,128)(2,1)}, u32[]{:S(2)}, u32[]{:S(2)}) collective-permute-start(bf16[2,2,128,512]{3,2,1,0:T(8,128)(2,1)S(1)} %bitcast.35), channel_id=1, source_target_pairs={{0,94},{1,95},{2,92},{3,93},{4,90},{5,91},{6,88},{7,89},{8,86},{9,... | collective-permute-start | bytes 1572872 | tf_op jit(solution)/shard_map/ppermute | solution.py:174
  49.0 24.0 %collective-permute-start = (bf16[1,2,128,512]{3,2,1,0:T(8,128)(2,1)}, bf16[1,2,128,512]{3,2,1,0:T(8,128)(2,1)}, u32[]{:S(2)}, u32[]{:S(2)}) collective-permute-start(bf16[1,2,128,512]{3,2,1,0:T(8,128)(2,1)} %maximum_bitcast_fusion), channel_id=1, source_target_pairs={{0,32},{1,33},{2,34},{3,35},{4,36},{5,37},{6,38},{7,39},{8,40},{9,... | collective-permute-start | bytes 786440 | tf_op jit(solution)/shard_map/ppermute | solution.py:174
  57.6 15.4 %collective-permute-start.2 = (bf16[1,2,128,512]{3,2,1,0:T(8,128)(2,1)}, bf16[1,2,128,512]{3,2,1,0:T(8,128)(2,1)}, u32[]{:S(2)}, u32[]{:S(2)}) collective-permute-start(bf16[1,2,128,512]{3,2,1,0:T(8,128)(2,1)} %slice.50), channel_id=1, source_target_pairs={{0,32},{1,33},{2,34},{3,35},{4,36},{5,37},{6,38},{7,39},{8,40},{9,... | collective-permute-start | bytes 786440 | tf_op jit(solution)/shard_map/ppermute | solution.py:174
  62.9 35.0 %collective-permute-start.7 = (bf16[1,2,128,512]{3,2,1,0:T(8,128)(2,1)S(1)}, bf16[1,2,128,512]{3,2,1,0:T(8,128)(2,1)S(1)}, u32[]{:S(2)}, u32[]{:S(2)}) collective-permute-start(bf16[1,2,128,512]{3,2,1,0:T(8,128)(2,1)S(1)} %slice.53), channel_id=1, source_target_pairs={{0,32},{1,33},{2,34},{3,35},{4,36},{5,37},{6,38},{7,39},{8,40},{9,... | collective-permute-start | bytes 786440 | tf_op jit(solution)/shard_map/ppermute | solution.py:174
  72.9 25.0 %collective-permute-start.9 = (bf16[1,2,128,512]{3,2,1,0:T(8,128)(2,1)S(1)}, bf16[1,2,128,512]{3,2,1,0:T(8,128)(2,1)S(1)}, u32[]{:S(2)}, u32[]{:S(2)}) collective-permute-start(bf16[1,2,128,512]{3,2,1,0:T(8,128)(2,1)S(1)} %slice.54), channel_id=1, source_target_pairs={{0,32},{1,33},{2,34},{3,35},{4,36},{5,37},{6,38},{7,39},{8,40},{9,... | collective-permute-start | bytes 786440 | tf_op jit(solution)/shard_map/ppermute | solution.py:174
  94.0 42.9 %collective-permute-start.4 = (bf16[2,128,512]{2,1,0:T(8,128)(2,1)}, bf16[2,128,512]{2,1,0:T(8,128)(2,1)S(1)}, u32[]{:S(2)}, u32[]{:S(2)}) collective-permute-start(bf16[2,128,512]{2,1,0:T(8,128)(2,1)} %get-tuple-element.14), channel_id=1, source_target_pairs={{0,30},{1,31},{2,28},{3,29},{4,26},{5,27},{6,24},{7,25},{8,22},{9,... | collective-permute-start | bytes 786440 | tf_op jit(solution)/shard_map/ppermute | solution.py:174
  97.0 38.9 %collective-permute-start.3 = (bf16[128,512]{1,0:T(8,128)(2,1)S(1)}, bf16[128,512]{1,0:T(8,128)(2,1)}, u32[]{:S(2)}, u32[]{:S(2)}) collective-permute-start(bf16[128,512]{1,0:T(8,128)(2,1)S(1)} %get-tuple-element.46), channel_id=1, source_target_pairs={{0,32},{1,33},{2,34},{3,35},{4,36},{5,37},{6,38},{7,39},{8,40},{9,... | collective-permute-start | bytes 393224 | tf_op jit(solution)/shard_map/ppermute | solution.py:174
  97.9 0.7 copy-start.3
  97.9 0.8 copy-start.4
  120.4 61.3 %all-to-all-start.1 = ((bf16[32,2,128,128]{3,2,1,0:T(8,128)(2,1)}), bf16[32,2,128,128]{3,2,1,0:T(8,128)(2,1)S(1)}, u32[]{:S(2)}, u32[]{:S(2)}) async-start(bf16[32,2,128,128]{3,2,1,0:T(8,128)(2,1)} %get-tuple-element.21), calls=%async_computation.1 | async-start | bytes 4194304 | tf_op jit(solution)/shard_map/all_to_all | solution.py:212
  136.9 1.4 collective-permute-start.5
  137.3 29.5 %collective-permute-start.10 = (bf16[2,128,512]{2,1,0:T(8,128)(2,1)}, bf16[2,128,512]{2,1,0:T(8,128)(2,1)S(1)}, u32[]{:S(2)}, u32[]{:S(2)}) collective-permute-start(bf16[2,128,512]{2,1,0:T(8,128)(2,1)} %get-tuple-element.19), channel_id=1, source_target_pairs={{0,64},{1,65},{2,66},{3,67},{4,68},{5,69},{6,70},{7,71},{8,72},{9,... | collective-permute-start | bytes 786440 | tf_op jit(solution)/shard_map/ppermute | solution.py:174
  166.8 4.9 %collective-permute-start.11 = (bf16[128,512]{1,0:T(8,128)(2,1)S(1)}, bf16[128,512]{1,0:T(8,128)(2,1)S(1)}, u32[]{:S(2)}, u32[]{:S(2)}) collective-permute-start(bf16[128,512]{1,0:T(8,128)(2,1)S(1)} %get-tuple-element.42), channel_id=1, source_target_pairs={{0,32},{1,33},{2,34},{3,35},{4,36},{5,37},{6,38},{7,39},{8,40},{9,... | collective-permute-start | bytes 393224 | tf_op jit(solution)/shard_map/ppermute | solution.py:174
  167.4 12.3 %collective-permute-start.12 = (bf16[2,128,512]{2,1,0:T(8,128)(2,1)}, bf16[2,128,512]{2,1,0:T(8,128)(2,1)S(1)}, u32[]{:S(2)}, u32[]{:S(2)}) collective-permute-start(bf16[2,128,512]{2,1,0:T(8,128)(2,1)} %get-tuple-element.20), channel_id=1, source_target_pairs={{0,94},{1,95},{2,92},{3,93},{4,90},{5,91},{6,88},{7,89},{8,86},{9,... | collective-permute-start | bytes 786440 | tf_op jit(solution)/shard_map/ppermute | solution.py:174
  179.7 1.9 %collective-permute-start.13 = (bf16[128,512]{1,0:T(8,128)(2,1)S(1)}, bf16[128,512]{1,0:T(8,128)(2,1)S(1)}, u32[]{:S(2)}, u32[]{:S(2)}) collective-permute-start(bf16[128,512]{1,0:T(8,128)(2,1)S(1)} %get-tuple-element.40), channel_id=1, source_target_pairs={{0,32},{1,33},{2,34},{3,35},{4,36},{5,37},{6,38},{7,39},{8,40},{9,... | collective-permute-start | bytes 393224 | tf_op jit(solution)/shard_map/ppermute | solution.py:174
  181.6 1.3 copy-start.2

commit v3 on v2

--- a/solution.py
+++ b/solution.py
@@ -202,19 +202,19 @@
 
     blocks = jnp.stack([blk, flip(blk)]).astype(jnp.int32)
     own = packed(0)
-    turned = move(packed(FLIP), FLIP)
-    near, near_turned, kv = lax.optimization_barrier((packed(NEAR), packed(NEAR | FLIP), kv))
-    near = move(near, NEAR)
-    near_turned = move(near_turned, NEAR | FLIP)
-    d_own, d_turned, *sums = attention(blocks, (fetch(own), fetch(turned)), kv)
-    d_near, d_near_turned, term = attention(blocks, (fetch(near), fetch(near_turned)), kv, sums)
+    across = move(packed(NEAR | FLIP), NEAR | FLIP)
+    near, turned, kv = lax.optimization_barrier((packed(NEAR), packed(FLIP), kv))
+    near, turned = move(near, NEAR), move(turned, FLIP)
+    d_own, d_across, *sums = attention(blocks, (fetch(own), fetch(across)), kv)
+    near, turned, sums = lax.optimization_barrier((near, turned, sums))
+    d_near, d_turned, term = attention(blocks, (fetch(near), fetch(turned)), kv, sums)
 
     received = lax.all_to_all(term, "blk", 0, 0, tiled=True)
     kv_grad = received.reshape(2, 16, 2, ROWS, HEAD_DIM).astype(F32).sum(1)
     kv_grad = kv_grad.transpose(1, 2, 0, 3).reshape(2, ROWS, 2 * HEAD_DIM)
 
     query_grad = jnp.zeros((ROWS, 8 * WIDTH), BF16)
-    for k, grad in ((0, d_own), (FLIP, d_turned), (NEAR, d_near), (NEAR | FLIP, d_near_turned)):
+    for k, grad in ((0, d_own), (NEAR | FLIP, d_across), (NEAR, d_near), (FLIP, d_turned)):
         for c, part in enumerate(give(move(grad, k))):
             query_grad = lax.dynamic_update_slice_in_dim(query_grad, part, of(k | c) * WIDTH, 1)
     return query_grad[None], kv_grad

time: 184 us -> 164 us (0.89)
  starting transfers between devices: 57.9 us -> 36.9 us
  waiting for transfers between devices: 63.4 us -> 65.8 us
    ppermute x14, waiting for transfers between devices: 42.1 us -> 65.8 us  [move(): return lax.ppermute(x, AXES, partners(k)) if k else x]
    all_to_all x1, waiting for transfers between devices: 21.2 us -> 0.01 us  [shards(): kv = lax.all_to_all(spread, 'blk', 0, 0, tiled=True)]
    all_to_all x1, starting transfers between devices: 15.6 us -> 4.58 us  [shards(): received = lax.all_to_all(term, 'blk', 0, 0, tiled=True)]
    ppermute x14, starting transfers between devices: 31 us -> 21.1 us  [move(): return lax.ppermute(x, AXES, partners(k)) if k else x]
  transfers between devices with their start and end apart: 16 -> 16, of which waited for: 6 -> 5; matrix products, arithmetic and copies ran while one was open for 7% -> 6% of each run, Pallas kernels for 23% -> 26%
where the time goes in v3:
time: 164 us
  waiting for transfers between devices  65.8 us (40%)
  Pallas kernels  42.7 us (26%)
  starting transfers between devices  36.9 us (22%)
  local copies, waits for them, and re-layouts  11.2 us (7%)
  other arithmetic  6 us (4%)
    ppermute x14, waiting for transfers between devices, move(): return lax.ppermute(x, AXES, partners(k)) if k else x  65.8 us
    pallas_call x2, Pallas kernels, attention(): pl.pallas_call(functools.partial(attention_kernel, first), out_shape=outs...  42.7 us
    ppermute x14, starting transfers between devices, move(): return lax.ppermute(x, AXES, partners(k)) if k else x  21.1 us
    all_to_all x1, starting transfers between devices, shards(): kv = lax.all_to_all(spread, 'blk', 0, 0, tiled=True)  11.3 us
    all_to_all x1, starting transfers between devices, shards(): received = lax.all_to_all(term, 'blk', 0, 0, tiled=True)  4.58 us
    unnamed x24, local copies, waits for them, and re-layouts  3.55 us
  transfers between devices with their start and end apart: 16, of which 5 were waited for; matrix products, arithmetic and copies ran while one was open for 6% of the time, Pallas kernels for 26%

profile of v3, /device:TPU:1, one launch (start us, length us, event | category | flops | bytes accessed | tf_op | source)
XLA Modules:
  0.0 163.6 jit_solution(16156826979242411987)
XLA Ops:
  0.6 1.0 convert_element_type.17
  1.7 0.8 copy.10
  2.9 1.9 %broadcast_in_dim.20 = bf16[2,16,2,128,128]{4,3,2,1,0:T(8,128)(2,1)} broadcast(bf16[2,2,128,128]{3,2,1,0:T(8,128)(2,1)S(1)} %copy.11), dimensions={0,2,3,4} | broadcast | bytes 2228224 | tf_op jit(solution)/shard_map/broadcast_in_dim | solution.py:187
  4.8 11.3 %all-to-all-start = ((bf16[32,2,128,128]{3,2,1,0:T(8,128)(2,1)}), bf16[32,2,128,128]{3,2,1,0:T(8,128)(2,1)S(1)}, u32[]{:S(2)}, u32[]{:S(2)}) async-start(bf16[32,2,128,128]{3,2,1,0:T(8,128)(2,1)} %bitcast.9), calls=%async_computation | async-start | bytes 4194304 | tf_op jit(solution)/shard_map/all_to_all | solution.py:188
  16.2 2.4 %constant_dynamic-slice_fusion.2 = (bf16[1,128,512]{2,1,0:T(8,128)(2,1)S(1)}, bf16[1,128,512]{2,1,0:T(8,128)(2,1)}, bf16[1,128,512]{2,1,0:T(8,128)(2,1)}, bf16[1...) fusion(bf16[1,128,4096]{2,1,0:T(8,128)(2,1)S(1)} %copy-done.1, ...), kind=kLoop, calls=%fused_computation.22 | loop fusion | bytes 4194336 | tf_op jit(solution)/shard_map/dynamic_slice | solution.py:192
  18.6 5.2 %collective-permute-start.1 = (bf16[2,2,128,512]{3,2,1,0:T(8,128)(2,1)S(1)}, bf16[2,2,128,512]{3,2,1,0:T(8,128)(2,1)}, u32[]{:S(2)}, u32[]{:S(2)}) collective-permute-start(bf16[2,2,128,512]{3,2,1,0:T(8,128)(2,1)S(1)} %bitcast.38), channel_id=1, source_target_pairs={{0,94},{1,95},{2,92},{3,93},{4,90},{5,91},{6,88},{7,89},{8,86},{9,... | collective-permute-start | bytes 1572872 | tf_op jit(solution)/shard_map/ppermute | solution.py:174
  23.8 0.7 maximum_bitcast_fusion
  24.5 1.5 collective-permute-start
  26.1 1.8 %pad_maximum_fusion = bf16[4,128,512]{2,1,0:T(8,128)(2,1)} fusion(bf16[1,128,512]{2,1,0:T(8,128)(2,1)S(1)} %get-tuple-element.45, bf16[1,128,512]{2,1,0:T(8,128)(2,1)S(1)} %get-tuple-element.58, bf16[1,128,512]{2,1,0:T(8,128)(2,1)} %get-tuple-element.46, bf16[1,128,512]{2,1,0:T(8,128)(2,1)} %get-tuple-element.57), kind=kLoop, calls=%fused_computation.1 | loop fusion | flops 786432 | bytes 1048576 | tf_op jit(solution)/shard_map/stack | solution.py:195
  27.9 28.5 %collective-permute-done.1.refs_2_ = bf16[2,2,128,512]{3,2,1,0:T(8,128)(2,1)} collective-permute-done((bf16[2,2,128,512]{3,2,1,0:T(8,128)(2,1)S(1)}, bf16[2,2,128,512]{3,2,1,0:T(8,128)(2,1)}, u32[]{:S(2)}, u32[]{:S(2)}) %collective-permute-start.1) | collective-permute-done | bytes 524320 | tf_op jit(solution)/shard_map/ppermute | solution.py:174
  56.4 1.0 slice.50
  57.4 1.3 collective-permute-start.2
  58.7 0.6 pad_add_fusion.blocks_ref
  59.3 1.1 pad_maximum_fusion.3
  60.4 0.8 collective-permute-start.6
  61.8 21.0 %attention_first.1 = (bf16[2,128,512]{2,1,0:T(8,128)(2,1)}, bf16[2,128,512]{2,1,0:T(8,128)(2,1)}, f32[8,512,128]{2,1,0:T(8,128)}, f32[8,512,128]{2,1,0:T(8,128)}) custom-call(s32[2]{0:T(128)} %pad_add_fusion.blocks_ref, bf16[2,2,128,512]{3,2,1,0:T(8,128)(2,1)} %bitcast.35, bf16[1,2,128,512]{3,2,1,0:T(8,128)(2,1)} %collective-permute-done.refs_1_, ...), custom_call_target="tpu_custom_call" | custom-call | flops 12000000000 | bytes 8000000 | tf_op jit(solution)/shard_map/attention_first/pallas_call | solution.py:150
  83.0 1.0 slice.45
  84.5 4.9 %collective-permute-start.4 = (bf16[2,128,512]{2,1,0:T(8,128)(2,1)}, bf16[2,128,512]{2,1,0:T(8,128)(2,1)S(1)}, u32[]{:S(2)}, u32[]{:S(2)}) collective-permute-start(bf16[2,128,512]{2,1,0:T(8,128)(2,1)} %get-tuple-element.18), channel_id=1, source_target_pairs={{0,94},{1,95},{2,92},{3,93},{4,90},{5,91},{6,88},{7,89},{8,86},{9,... | collective-permute-start | bytes 786440 | tf_op jit(solution)/shard_map/ppermute | solution.py:174
  89.6 0.7 collective-permute-start.3
  90.3 0.7 copy-done.9
  91.0 0.7 copy-done.10
  91.7 21.7 %attention_second.1 = (bf16[2,128,512]{2,1,0:T(8,128)(2,1)}, bf16[2,128,512]{2,1,0:T(8,128)(2,1)}, bf16[32,2,128,128]{3,2,1,0:T(8,128)(2,1)}) custom-call(s32[2]{0:T(128)} %pad_add_fusion.blocks_ref, bf16[2,2,128,512]{3,2,1,0:T(8,128)(2,1)} %copy-done.8, bf16[1,2,128,512]{3,2,1,0:T(8,128)(2,1)} %copy-done.9, ...), custom_call_target="tpu_custom_call" | custom-call | flops 12000000000 | bytes 8000000 | tf_op jit(solution)/shard_map/attention_second/pallas_call | solution.py:150
  113.4 4.6 %all-to-all-start.1 = ((bf16[32,2,128,128]{3,2,1,0:T(8,128)(2,1)}), bf16[32,2,128,128]{3,2,1,0:T(8,128)(2,1)S(1)}, u32[]{:S(2)}, u32[]{:S(2)}) async-start(bf16[32,2,128,128]{3,2,1,0:T(8,128)(2,1)} %get-tuple-element.29), calls=%async_computation.1 | async-start | bytes 4194304 | tf_op jit(solution)/shard_map/all_to_all | solution.py:212
  118.0 0.9 bitcast_dynamic-update-slice_fusion.3
  119.5 0.9 collective-permute-done.5
  120.4 28.0 %collective-permute-done.10 = bf16[2,128,512]{2,1,0:T(8,128)(2,1)S(1)} collective-permute-done((bf16[2,128,512]{2,1,0:T(8,128)(2,1)}, bf16[2,128,512]{2,1,0:T(8,128)(2,1)S(1)}, u32[]{:S(2)}, u32[]{:S(2)}) %collective-permute-start.10) | collective-permute-done | bytes 262176 | tf_op jit(solution)/shard_map/ppermute | solution.py:174
  148.4 0.5 collective-permute-start.11
  148.9 4.0 %collective-permute-start.12 = (bf16[2,128,512]{2,1,0:T(8,128)(2,1)}, bf16[2,128,512]{2,1,0:T(8,128)(2,1)S(1)}, u32[]{:S(2)}, u32[]{:S(2)}) collective-permute-start(bf16[2,128,512]{2,1,0:T(8,128)(2,1)} %get-tuple-element.28), channel_id=1, source_target_pairs={{0,30},{1,31},{2,28},{3,29},{4,26},{5,27},{6,24},{7,25},{8,22},{9,... | collective-permute-start | bytes 786440 | tf_op jit(solution)/shard_map/ppermute | solution.py:174
  152.9 7.4 %collective-permute-done.12 = bf16[2,128,512]{2,1,0:T(8,128)(2,1)S(1)} collective-permute-done((bf16[2,128,512]{2,1,0:T(8,128)(2,1)}, bf16[2,128,512]{2,1,0:T(8,128)(2,1)S(1)}, u32[]{:S(2)}, u32[]{:S(2)}) %collective-permute-start.12) | collective-permute-done | bytes 262176 | tf_op jit(solution)/shard_map/ppermute | solution.py:174
  160.3 1.0 collective-permute-start.13
  161.3 1.0 collective-permute-done.13
  162.8 0.8 copy.13
  (53 shorter events, 3.1 us)
Async XLA Ops:
  4.8 11.4 %copy-start.1 = (bf16[1,128,4096]{2,1,0:T(8,128)(2,1)S(1)}, bf16[1,128,4096]{2,1,0:T(8,128)(2,1)}, u32[]{:S(2)}) copy-start(bf16[1,128,4096]{2,1,0:T(8,128)(2,1)} %param.5) | copy-start | bytes 3145732
  4.8 55.6 %all-to-all-start = ((bf16[32,2,128,128]{3,2,1,0:T(8,128)(2,1)}), bf16[32,2,128,128]{3,2,1,0:T(8,128)(2,1)S(1)}, u32[]{:S(2)}, u32[]{:S(2)}) async-start(bf16[32,2,128,128]{3,2,1,0:T(8,128)(2,1)} %bitcast.9), calls=%async_computation | async-start | bytes 4194304 | tf_op jit(solution)/shard_map/all_to_all | solution.py:188
  18.5 40.7 %copy-start.3 = (bf16[1,128,512]{2,1,0:T(8,128)(2,1)S(1)}, bf16[1,128,512]{2,1,0:T(8,128)(2,1)}, u32[]{:S(2)}) copy-start(bf16[1,128,512]{2,1,0:T(8,128)(2,1)} %get-tuple-element.41) | copy-start | bytes 393220
  18.5 40.7 %copy-start.4 = (bf16[1,128,512]{2,1,0:T(8,128)(2,1)S(1)}, bf16[1,128,512]{2,1,0:T(8,128)(2,1)}, u32[]{:S(2)}) copy-start(bf16[1,128,512]{2,1,0:T(8,128)(2,1)} %get-tuple-element.42) | copy-start | bytes 393220
  18.6 40.7 %copy-start.5 = (bf16[1,128,512]{2,1,0:T(8,128)(2,1)S(1)}, bf16[1,128,512]{2,1,0:T(8,128)(2,1)}, u32[]{:S(2)}) copy-start(bf16[1,128,512]{2,1,0:T(8,128)(2,1)} %get-tuple-element.61) | copy-start | bytes 393220
  18.6 40.7 %copy-start.6 = (bf16[1,128,512]{2,1,0:T(8,128)(2,1)S(1)}, bf16[1,128,512]{2,1,0:T(8,128)(2,1)}, u32[]{:S(2)}) copy-start(bf16[1,128,512]{2,1,0:T(8,128)(2,1)} %get-tuple-element.62) | copy-start | bytes 393220
  18.6 37.8 %collective-permute-start.1 = (bf16[2,2,128,512]{3,2,1,0:T(8,128)(2,1)S(1)}, bf16[2,2,128,512]{3,2,1,0:T(8,128)(2,1)}, u32[]{:S(2)}, u32[]{:S(2)}) collective-permute-start(bf16[2,2,128,512]{3,2,1,0:T(8,128)(2,1)S(1)} %bitcast.38), channel_id=1, source_target_pairs={{0,94},{1,95},{2,92},{3,93},{4,90},{5,91},{6,88},{7,89},{8,86},{9,... | collective-permute-start | bytes 1572872 | tf_op jit(solution)/shard_map/ppermute | solution.py:174
  24.5 36.7 %collective-permute-start = (bf16[1,2,128,512]{3,2,1,0:T(8,128)(2,1)}, bf16[1,2,128,512]{3,2,1,0:T(8,128)(2,1)}, u32[]{:S(2)}, u32[]{:S(2)}) collective-permute-start(bf16[1,2,128,512]{3,2,1,0:T(8,128)(2,1)} %maximum_bitcast_fusion), channel_id=1, source_target_pairs={{0,32},{1,33},{2,34},{3,35},{4,36},{5,37},{6,38},{7,39},{8,40},{9,... | collective-permute-start | bytes 786440 | tf_op jit(solution)/shard_map/ppermute | solution.py:174
  57.4 3.9 %collective-permute-start.2 = (bf16[1,2,128,512]{3,2,1,0:T(8,128)(2,1)S(1)}, bf16[1,2,128,512]{3,2,1,0:T(8,128)(2,1)}, u32[]{:S(2)}, u32[]{:S(2)}) collective-permute-start(bf16[1,2,128,512]{3,2,1,0:T(8,128)(2,1)S(1)} %slice.50), channel_id=1, source_target_pairs={{0,32},{1,33},{2,34},{3,35},{4,36},{5,37},{6,38},{7,39},{8,40},{9,... | collective-permute-start | bytes 786440 | tf_op jit(solution)/shard_map/ppermute | solution.py:174
  60.4 1.4 copy-start
  60.4 22.4 %collective-permute-start.6 = (bf16[2,2,128,512]{3,2,1,0:T(8,128)(2,1)S(1)}, bf16[2,2,128,512]{3,2,1,0:T(8,128)(2,1)S(1)}, u32[]{:S(2)}, u32[]{:S(2)}) collective-permute-start(bf16[2,2,128,512]{3,2,1,0:T(8,128)(2,1)S(1)} %bitcast.36), channel_id=1, source_target_pairs={{0,64},{1,65},{2,66},{3,67},{4,68},{5,69},{6,70},{7,71},{8,72},{9,... | collective-permute-start | bytes 1572872 | tf_op jit(solution)/shard_map/ppermute | solution.py:174
  61.2 21.6 %collective-permute-start.7 = (bf16[2,2,128,512]{3,2,1,0:T(8,128)(2,1)S(1)}, bf16[2,2,128,512]{3,2,1,0:T(8,128)(2,1)}, u32[]{:S(2)}, u32[]{:S(2)}) collective-permute-start(bf16[2,2,128,512]{3,2,1,0:T(8,128)(2,1)S(1)} %bitcast.37), channel_id=1, source_target_pairs={{0,30},{1,31},{2,28},{3,29},{4,26},{5,27},{6,24},{7,25},{8,22},{9,... | collective-permute-start | bytes 1572872 | tf_op jit(solution)/shard_map/ppermute | solution.py:174
  82.8 6.7 %copy-start.7 = (bf16[2,128,512]{2,1,0:T(8,128)(2,1)S(1)}, bf16[2,128,512]{2,1,0:T(8,128)(2,1)}, u32[]{:S(2)}) copy-start(bf16[2,128,512]{2,1,0:T(8,128)(2,1)} %get-tuple-element.17) | copy-start | bytes 786436
  82.8 7.5 %copy-start.8 = (bf16[2,2,128,512]{3,2,1,0:T(8,128)(2,1)}, bf16[2,2,128,512]{3,2,1,0:T(8,128)(2,1)S(1)}, u32[]{:S(2)}) copy-start(bf16[2,2,128,512]{3,2,1,0:T(8,128)(2,1)S(1)} %collective-permute-done.6.refs_0_) | copy-start | bytes 1572868
  82.9 7.4 %collective-permute-start.8 = (bf16[1,2,128,512]{3,2,1,0:T(8,128)(2,1)S(1)}, bf16[1,2,128,512]{3,2,1,0:T(8,128)(2,1)S(1)}, u32[]{:S(2)}, u32[]{:S(2)}) collective-permute-start(bf16[1,2,128,512]{3,2,1,0:T(8,128)(2,1)S(1)} %slice.44), channel_id=1, source_target_pairs={{0,32},{1,33},{2,34},{3,35},{4,36},{5,37},{6,38},{7,39},{8,40},{9,... | collective-permute-start | bytes 786440 | tf_op jit(solution)/shard_map/ppermute | solution.py:174
  84.0 6.3 %collective-permute-start.9 = (bf16[1,2,128,512]{3,2,1,0:T(8,128)(2,1)S(1)}, bf16[1,2,128,512]{3,2,1,0:T(8,128)(2,1)S(1)}, u32[]{:S(2)}, u32[]{:S(2)}) collective-permute-start(bf16[1,2,128,512]{3,2,1,0:T(8,128)(2,1)S(1)} %slice.45), channel_id=1, source_target_pairs={{0,32},{1,33},{2,34},{3,35},{4,36},{5,37},{6,38},{7,39},{8,40},{9,... | collective-permute-start | bytes 786440 | tf_op jit(solution)/shard_map/ppermute | solution.py:174
  84.5 34.4 %collective-permute-start.4 = (bf16[2,128,512]{2,1,0:T(8,128)(2,1)}, bf16[2,128,512]{2,1,0:T(8,128)(2,1)S(1)}, u32[]{:S(2)}, u32[]{:S(2)}) collective-permute-start(bf16[2,128,512]{2,1,0:T(8,128)(2,1)} %get-tuple-element.18), channel_id=1, source_target_pairs={{0,94},{1,95},{2,92},{3,93},{4,90},{5,91},{6,88},{7,89},{8,86},{9,... | collective-permute-start | bytes 786440 | tf_op jit(solution)/shard_map/ppermute | solution.py:174
  89.6 28.4 %collective-permute-start.3 = (bf16[128,512]{1,0:T(8,128)(2,1)S(1)}, bf16[128,512]{1,0:T(8,128)(2,1)}, u32[]{:S(2)}, u32[]{:S(2)}) collective-permute-start(bf16[128,512]{1,0:T(8,128)(2,1)S(1)} %get-tuple-element.54), channel_id=1, source_target_pairs={{0,32},{1,33},{2,34},{3,35},{4,36},{5,37},{6,38},{7,39},{8,40},{9,... | collective-permute-start | bytes 393224 | tf_op jit(solution)/shard_map/ppermute | solution.py:174
  90.3 0.7 copy-start.9
  91.0 0.7 copy-start.10
  113.4 48.9 %all-to-all-start.1 = ((bf16[32,2,128,128]{3,2,1,0:T(8,128)(2,1)}), bf16[32,2,128,128]{3,2,1,0:T(8,128)(2,1)S(1)}, u32[]{:S(2)}, u32[]{:S(2)}) async-start(bf16[32,2,128,128]{3,2,1,0:T(8,128)(2,1)} %get-tuple-element.29), calls=%async_computation.1 | async-start | bytes 4194304 | tf_op jit(solution)/shard_map/all_to_all | solution.py:212
  119.0 1.4 collective-permute-start.5
  119.3 29.0 %collective-permute-start.10 = (bf16[2,128,512]{2,1,0:T(8,128)(2,1)}, bf16[2,128,512]{2,1,0:T(8,128)(2,1)S(1)}, u32[]{:S(2)}, u32[]{:S(2)}) collective-permute-start(bf16[2,128,512]{2,1,0:T(8,128)(2,1)} %get-tuple-element.27), channel_id=1, source_target_pairs={{0,64},{1,65},{2,66},{3,67},{4,68},{5,69},{6,70},{7,71},{8,72},{9,... | collective-permute-start | bytes 786440 | tf_op jit(solution)/shard_map/ppermute | solution.py:174
  148.4 4.5 %collective-permute-start.11 = (bf16[128,512]{1,0:T(8,128)(2,1)S(1)}, bf16[128,512]{1,0:T(8,128)(2,1)S(1)}, u32[]{:S(2)}, u32[]{:S(2)}) collective-permute-start(bf16[128,512]{1,0:T(8,128)(2,1)S(1)} %get-tuple-element.50), channel_id=1, source_target_pairs={{0,32},{1,33},{2,34},{3,35},{4,36},{5,37},{6,38},{7,39},{8,40},{9,... | collective-permute-start | bytes 393224 | tf_op jit(solution)/shard_map/ppermute | solution.py:174
  148.9 11.4 %collective-permute-start.12 = (bf16[2,128,512]{2,1,0:T(8,128)(2,1)}, bf16[2,128,512]{2,1,0:T(8,128)(2,1)S(1)}, u32[]{:S(2)}, u32[]{:S(2)}) collective-permute-start(bf16[2,128,512]{2,1,0:T(8,128)(2,1)} %get-tuple-element.28), channel_id=1, source_target_pairs={{0,30},{1,31},{2,28},{3,29},{4,26},{5,27},{6,24},{7,25},{8,22},{9,... | collective-permute-start | bytes 786440 | tf_op jit(solution)/shard_map/ppermute | solution.py:174
  160.3 1.9 %collective-permute-start.13 = (bf16[128,512]{1,0:T(8,128)(2,1)S(1)}, bf16[128,512]{1,0:T(8,128)(2,1)S(1)}, u32[]{:S(2)}, u32[]{:S(2)}) collective-permute-start(bf16[128,512]{1,0:T(8,128)(2,1)S(1)} %get-tuple-element.48), channel_id=1, source_target_pairs={{0,32},{1,33},{2,34},{3,35},{4,36},{5,37},{6,38},{7,39},{8,40},{9,... | collective-permute-start | bytes 393224 | tf_op jit(solution)/shard_map/ppermute | solution.py:174
  162.3 1.3 copy-start.2

commit v4 on v3

v4 whole, which is shorter than its diff:
```python
import functools
import math

import jax
import jax.numpy as jnp
from jax import lax
from jax.experimental import pallas as pl
from jax.experimental.pallas import tpu as pltpu
from jax.sharding import PartitionSpec as P

HEAD_DIM = 128
GROUPS = 4
QUANT_BLOCK = 32
ROWS = 128
BLOCKS = 32
WIDTH = GROUPS * HEAD_DIM
AXES = ("section", "blk")
SCALE = 1.0 / math.sqrt(HEAD_DIM)
EXP2_SCALE = SCALE * math.log2(math.e)
F32 = jnp.float32
BF16 = jnp.bfloat16
NT = (((1,), (1,)), ((), ()))
NN = (((1,), (0,)), ((), ()))

LAYERS = 2
KEYS = 256
UNROLL = 4
SPAN = KEYS // ROWS
GROUP_ROWS = LAYERS * WIDTH
CHUNKS = BLOCKS // SPAN
HEADROOM = 64.0


def flip(blk):
    return blk ^ 30


def attention_kernel(first, blocks_ref, *refs):
    units, refs = refs[:4], refs[4:]
    kv_ref, refs = refs[0], refs[1:]
    if not first:
        sums_ref, refs = refs[0], refs[1:]
    mine_ref, other_ref, term_ref = refs[:3]
    q_s, do_s, kt_s, w_s, g_s, m_s, dk_s, dv_s, dq_s, stat_s = refs[3:]
    for n in range(2):
        for layer in range(LAYERS):
            unit = units[n * LAYERS + layer]
            for g in range(GROUPS):
                lo = layer * WIDTH + g * HEAD_DIM
                columns = slice(g * HEAD_DIM, (g + 1) * HEAD_DIM)
                q_s[n, lo : lo + ROWS, :] = unit[0, :, columns]
                do_s[n, lo : lo + ROWS, :] = unit[1, :, columns]
    for j in range(BLOCKS):
        kt_s[:, j * ROWS : (j + 1) * ROWS] = kv_ref[j, 0].T
    if first:
        dk_s[...] = jnp.zeros_like(dk_s)
        dv_s[...] = jnp.zeros_like(dv_s)
    else:
        for j in range(CHUNKS):
            blocks = slice(j * SPAN, (j + 1) * SPAN)
            dk_s[j] = sums_ref[blocks, 0].reshape(KEYS, HEAD_DIM).astype(F32)
            dv_s[j] = sums_ref[blocks, 1].reshape(KEYS, HEAD_DIM).astype(F32)

    def one_group(group, _):
        block = blocks_ref[group]
        last = block // SPAN
        q, do = q_s.at[group], do_s.at[group]

        def keys(j, which):
            return kv_ref[pl.ds(j * SPAN, SPAN), which].reshape(KEYS, HEAD_DIM)

        def fold(x, op):
            return op(x.reshape(KEYS // 8, 8, GROUP_ROWS), axis=0)

        def products(j):
            scores = lax.dot_general(keys(j, 0), q[...], NT, preferred_element_type=F32)
            return scores, lax.dot_general(keys(j, 1), do[...], NT, preferred_element_type=F32)

        def keep(j, weights, prob_grad, top):
            w_s[j] = weights
            g_s[j] = prob_grad
            m_s[j] = jnp.broadcast_to(top, (8, GROUP_ROWS))
            return fold(weights, jnp.sum), fold(weights * prob_grad, jnp.sum)

        def highest(scores):
            return jnp.max(fold(scores, jnp.max), axis=0, keepdims=True) * EXP2_SCALE

        def unrolled(count, step, carry):
            def several(t, carry):
                for n in range(UNROLL):
                    carry = step(t * UNROLL + n, carry)
                return carry

            carry = lax.fori_loop(0, count // UNROLL, several, carry)
            return lax.fori_loop(count // UNROLL * UNROLL, count, step, carry)

        scores, prob_grad = products(last)
        key_at = lax.broadcasted_iota(jnp.int32, (KEYS, GROUP_ROWS), 0)
        row_at = lax.broadcasted_iota(jnp.int32, (KEYS, GROUP_ROWS), 1) & (ROWS - 1)
        scores = jnp.where(key_at <= row_at + (block - last * SPAN) * ROWS, scores, -1e30)
        base = highest(scores)
        total0, dot0 = keep(last, jnp.exp2(scores * EXP2_SCALE - base), prob_grad, base)

        def quick(j, carry):
            peak8, total8, dot8 = carry
            scores, prob_grad = products(j)
            total, dot = keep(j, jnp.exp2(scores * EXP2_SCALE - base), prob_grad, base)
            return jnp.maximum(peak8, fold(scores, jnp.max)), total8 + total, dot8 + dot

        peak8, total8, dot8 = unrolled(last, quick, (jnp.full((8, GROUP_ROWS), -1e30, F32), total0, dot0))
        stat_s[0:1] = base
        stat_s[8:16] = total8
        stat_s[16:24] = dot8

        @pl.when(jnp.max(peak8 * EXP2_SCALE - base) > HEADROOM)
        def _():
            def careful(j, carry):
                top, total8, dot8 = carry
                scores, prob_grad = products(j)
                new_top = jnp.maximum(top, highest(scores))
                total, dot = keep(j, jnp.exp2(scores * EXP2_SCALE - new_top), prob_grad, new_top)
                factor = jnp.exp2(top - new_top)
                return new_top, total8 * factor + total, dot8 * factor + dot

            top, total8, dot8 = lax.fori_loop(0, last, careful, (base, total0, dot0))
            stat_s[0:1] = top
            stat_s[8:16] = total8
            stat_s[16:24] = dot8

        top = stat_s[0:1]
        inverse = 1.0 / jnp.sum(stat_s[8:16], axis=0, keepdims=True)
        delta = jnp.sum(stat_s[16:24], axis=0, keepdims=True) * inverse
        dq_s[...] = jnp.zeros_like(dq_s)

        def backward(j, carry):
            probs = w_s[j] * (jnp.exp2(m_s[j][0:1] - top) * inverse)
            score_grad = (probs * (g_s[j] - delta)).astype(BF16)
            dv_s[j] += lax.dot_general(probs.astype(BF16), do[...], NN, preferred_element_type=F32)
            dk_s[j] += lax.dot_general(score_grad, q[...], NN, preferred_element_type=F32)
            columns = kt_s[:, pl.ds(pl.multiple_of(j * KEYS, KEYS), KEYS)]
            dq_s[...] += lax.dot_general(columns, score_grad, NN, preferred_element_type=F32)
            return carry

        unrolled(last + 1, backward, 0)
        for h in range(GROUP_ROWS // ROWS):
            part = dq_s[:, h * ROWS : (h + 1) * ROWS]
            q_s[group, h * ROWS : (h + 1) * ROWS, :] = (part.T * SCALE).astype(BF16)
        return 0

    lax.fori_loop(0, 2, one_group, 0)
    for n in range(2):
        for layer, out_ref in enumerate((mine_ref, other_ref)):
            for g in range(GROUPS):
                lo = layer * WIDTH + g * HEAD_DIM
                out_ref[n, :, g * HEAD_DIM : (g + 1) * HEAD_DIM] = q_s[n, lo : lo + ROWS, :]
    for j in range(CHUNKS):
        blocks = slice(j * SPAN, (j + 1) * SPAN)
        key_grad = dk_s[j] if first else dk_s[j] * SCALE
        term_ref[blocks, 0] = key_grad.astype(BF16).reshape(SPAN, ROWS, HEAD_DIM)
        term_ref[blocks, 1] = dv_s[j].astype(BF16).reshape(SPAN, ROWS, HEAD_DIM)


def attention(blocks, units, kv, sums=None):
    first = sums is None
    vmem = pl.BlockSpec(memory_space=pltpu.VMEM)
    args = [*units, kv] + ([] if first else [sums])
    return pl.pallas_call(
        functools.partial(attention_kernel, first),
        out_shape=[jax.ShapeDtypeStruct((2, ROWS, WIDTH), BF16)] * 2
        + [jax.ShapeDtypeStruct((BLOCKS, 2, ROWS, HEAD_DIM), BF16)],
        in_specs=[pl.BlockSpec(memory_space=pltpu.SMEM)] + [vmem] * len(args),
        out_specs=[vmem] * 3,
        scratch_shapes=[
            pltpu.VMEM((2, GROUP_ROWS, HEAD_DIM), BF16),
            pltpu.VMEM((2, GROUP_ROWS, HEAD_DIM), BF16),
            pltpu.VMEM((HEAD_DIM, BLOCKS * ROWS), BF16),
            pltpu.VMEM((CHUNKS, KEYS, GROUP_ROWS), F32),
            pltpu.VMEM((CHUNKS, KEYS, GROUP_ROWS), F32),
            pltpu.VMEM((CHUNKS, 8, GROUP_ROWS), F32),
            pltpu.VMEM((CHUNKS, KEYS, HEAD_DIM), F32),
            pltpu.VMEM((CHUNKS, KEYS, HEAD_DIM), F32),
            pltpu.VMEM((HEAD_DIM, GROUP_ROWS), F32),
            pltpu.VMEM((24, GROUP_ROWS), F32),
        ],
        compiler_params=pltpu.CompilerParams(vmem_limit_bytes=60 * 1024 * 1024),
        cost_estimate=pl.CostEstimate(flops=12_000_000_000, bytes_accessed=8_000_000, transcendentals=4_500_000),
        name="attention_first" if first else "attention_second",
    )(blocks, *args)


CORE, FLIP, NEAR = 1, 2, 4
ACROSS = NEAR | FLIP


def partners(k):
    return [
        (s * BLOCKS + b, (s ^ (k & CORE) ^ (2 if k & NEAR else 0)) * BLOCKS + (flip(b) if k & FLIP else b))
        for s in range(4)
        for b in range(BLOCKS)
    ]


def move(x, k):
    return lax.ppermute(x, AXES, partners(k))


def shards(queries, out_grad, kv_codes, kv_scales):
    section, blk = lax.axis_index("section"), lax.axis_index("blk")
    head = section * 2 + blk // 16

    def of(k):
        return head ^ (4 if k & NEAR else 0) ^ (2 if k & CORE else 0) ^ (1 if k & FLIP else 0)

    codes = kv_codes.reshape(2, ROWS // QUANT_BLOCK, QUANT_BLOCK, 2, HEAD_DIM).astype(F32)
    cache = (codes * kv_scales[:, :, None, :, None]).astype(BF16)
    cache = cache.reshape(2, ROWS, 2, HEAD_DIM).transpose(2, 0, 1, 3)
    spread = jnp.broadcast_to(cache[:, None], (2, 16, 2, ROWS, HEAD_DIM)).reshape(BLOCKS, 2, ROWS, HEAD_DIM)
    kv = lax.all_to_all(spread, "blk", 0, 0, tiled=True)

    def pick(k):
        at = of(k) * WIDTH
        return jnp.stack(
            [lax.dynamic_slice_in_dim(queries[0], at, WIDTH, 1), lax.dynamic_slice_in_dim(out_grad[0], at, WIDTH, 1)]
        )

    blocks = jnp.stack([blk, flip(blk)]).astype(jnp.int32)
    across = move(pick(ACROSS), ACROSS)
    across_core = move(pick(ACROSS | CORE), ACROSS | CORE)
    own, own_core = pick(0), move(pick(CORE), CORE)
    swapped = move(jnp.stack([pick(NEAR | CORE), pick(FLIP | CORE)]), CORE)
    near, turned, kv = lax.optimization_barrier(
        (jnp.stack([pick(NEAR), swapped[0]]), jnp.stack([pick(FLIP), swapped[1]]), kv)
    )
    near, turned = move(near, NEAR), move(turned, FLIP)

    mine, other, sums = attention(blocks, (own, own_core, across, across_core), kv)
    near, turned, mine = lax.optimization_barrier((near, turned, mine))
    other = move(other, CORE)
    grads = {0: mine[0], CORE: other[0]}
    sent = move(jnp.stack([mine[1], other[1]]), ACROSS)
    grads |= {ACROSS: sent[0], ACROSS | CORE: sent[1]}

    mine, other, term = attention(blocks, (near[0], near[1], turned[0], turned[1]), kv, sums)
    other, term = lax.optimization_barrier((move(other, CORE), term))
    received = lax.all_to_all(term, "blk", 0, 0, tiled=True)
    for n, k in enumerate((NEAR, FLIP)):
        sent = move(jnp.stack([mine[n], other[n]]), k)
        grads |= {k: sent[0], k | CORE: sent[1]}

    kv_grad = received.reshape(2, 16, 2, ROWS, HEAD_DIM).astype(F32).sum(1)
    kv_grad = kv_grad.transpose(1, 2, 0, 3).reshape(2, ROWS, 2 * HEAD_DIM)
    query_grad = jnp.zeros((ROWS, 8 * WIDTH), BF16)
    for k, part in grads.items():
        query_grad = lax.dynamic_update_slice_in_dim(query_grad, part, of(k) * WIDTH, 1)
    return query_grad[None], kv_grad


def solution(mesh):
    in_specs = (
        P("section", "blk", None),
        P("section", "blk", None),
        P(None, "blk", "section"),
        P(None, "blk", "section"),
    )
    out_specs = (P("section", "blk", None), P(None, "blk", "section"))
    return jax.shard_map(shards, mesh=mesh, in_specs=in_specs, out_specs=out_specs, check_vma=False)
```

time: 164 us -> 160 us (0.976); the launches traced: 164 us -> 158 us
  waiting for transfers between devices: 65.8 us -> 45.9 us
  starting transfers between devices: 36.9 us -> 53.4 us
  Pallas kernels: 42.7 us -> 36.8 us
  other arithmetic: 6 us -> 8.08 us
    ppermute x14 -> x11, waiting for transfers between devices: 65.8 us -> 32.2 us  [move(): return lax.ppermute(x, AXES, partners(k))]
    all_to_all x1, starting transfers between devices: 4.58 us -> 21.3 us  [shards(): received = lax.all_to_all(term, 'blk', 0, 0, tiled=True)]
    all_to_all x1, waiting for transfers between devices: 0.01 us -> 13.7 us  [shards(): kv = lax.all_to_all(spread, 'blk', 0, 0, tiled=True)]
    pallas_call x2, Pallas kernels: 42.7 us -> 36.8 us  [attention(): pl.pallas_call(functools.partial(attention_kernel, first), out_shape=[jax...]
    another operation x4 -> x14, other arithmetic: 3.07 us -> 5.83 us  [the longest x4 2.91 us: pick(): jnp.stack([lax.dynamic_slice_in_dim(queries[0], at, WIDTH, 1), lax.dynami...]
    squeeze x4 -> x2, local copies, waits for them, and re-layouts: 0.08 us -> 2.7 us  [the longest x1 1.86 us: shards(): turned[1]]
    unnamed x24 -> x14, local copies, waits for them, and re-layouts: 3.55 us -> 2.34 us
    ppermute x14 -> x11, starting transfers between devices: 21.1 us -> 20.8 us  [move(): return lax.ppermute(x, AXES, partners(k))]
  transfers between devices with their start and end apart: 16 -> 13, of which waited for: 5 -> 6; matrix products, arithmetic and copies ran while one was open for 6% -> 9% of each run, Pallas kernels for 26% -> 23%
where the time goes in v4:
time: 160 us; the launch traced here: 158 us
  starting transfers between devices  53.4 us (33%)
  waiting for transfers between devices  45.9 us (29%)
  Pallas kernels  36.8 us (23%)
  local copies, waits for them, and re-layouts  12.5 us (8%)
  other arithmetic  8.08 us (5%)
    pallas_call x2, Pallas kernels, attention(): pl.pallas_call(functools.partial(attention_kernel, first), out_shape=[jax...  36.8 us
    ppermute x11, waiting for transfers between devices, move(): return lax.ppermute(x, AXES, partners(k))  32.2 us
    all_to_all x1, starting transfers between devices, shards(): received = lax.all_to_all(term, 'blk', 0, 0, tiled=True)  21.3 us
    ppermute x11, starting transfers between devices, move(): return lax.ppermute(x, AXES, partners(k))  20.8 us
    all_to_all x1, waiting for transfers between devices, shards(): kv = lax.all_to_all(spread, 'blk', 0, 0, tiled=True)  13.7 us
    all_to_all x1, starting transfers between devices, shards(): kv = lax.all_to_all(spread, 'blk', 0, 0, tiled=True)  11.3 us
  transfers between devices with their start and end apart: 13, of which 6 were waited for; matrix products, arithmetic and copies ran while one was open for 9% of the time, Pallas kernels for 23%

profile of v4, /device:TPU:1, one launch (start us, length us, event | category | flops | bytes accessed | tf_op | source)
XLA Modules:
  0.0 157.6 jit_solution(1016049639324893016)
XLA Ops:
  0.6 1.0 convert_element_type.17
  1.7 0.8 copy.10
  2.9 1.9 %broadcast_in_dim.5 = bf16[2,16,2,128,128]{4,3,2,1,0:T(8,128)(2,1)} broadcast(bf16[2,2,128,128]{3,2,1,0:T(8,128)(2,1)S(1)} %copy.11), dimensions={0,2,3,4} | broadcast | bytes 2228224 | tf_op jit(solution)/shard_map/broadcast_in_dim | solution.py:217
  4.8 11.3 %all-to-all-start = ((bf16[32,2,128,128]{3,2,1,0:T(8,128)(2,1)}), bf16[32,2,128,128]{3,2,1,0:T(8,128)(2,1)S(1)}, u32[]{:S(2)}, u32[]{:S(2)}) async-start(bf16[32,2,128,128]{3,2,1,0:T(8,128)(2,1)} %bitcast.6), calls=%async_computation | async-start | bytes 4194304 | tf_op jit(solution)/shard_map/all_to_all | solution.py:218
  16.2 2.2 %constant_dynamic-slice_fusion = (bf16[1,128,512]{2,1,0:T(8,128)(2,1)S(1)}, bf16[1,128,512]{2,1,0:T(8,128)(2,1)S(1)}, bf16[1,128,512]{2,1,0:T(8,128)(2,1)S(1)}, ...) fusion(bf16[1,128,4096]{2,1,0:T(8,128)(2,1)S(1)} %copy-done.1, ...), kind=kLoop, calls=%fused_computation.29 | loop fusion | bytes 4194336 | tf_op jit(solution)/shard_map/dynamic_slice | solution.py:223
  18.5 1.0 collective-permute-start
  20.2 5.3 %collective-permute-start.5 = (bf16[2,128,512]{2,1,0:T(8,128)(2,1)}, bf16[2,128,512]{2,1,0:T(8,128)(2,1)}, u32[]{:S(2)}, u32[]{:S(2)}) collective-permute-start(bf16[2,128,512]{2,1,0:T(8,128)(2,1)} %pad_maximum_fusion.6), channel_id=1, source_target_pairs={{0,126},{1,127},{2,124},{3,125},{4,122},{5,123},{6,120},{7,121},{8... | collective-permute-start | bytes 786440 | tf_op jit(solution)/shard_map/ppermute | solution.py:204
  25.5 0.7 pad_maximum_fusion.5
  26.6 0.7 pad_maximum_fusion.4
  27.3 0.8 collective-permute-start.3
  28.7 1.0 maximum_bitcast_fusion.3
  29.7 0.9 maximum_bitcast_fusion
  30.6 0.7 pad_maximum_fusion.3.refs_0_
  31.5 13.7 %all-to-all-done.refs_4_ = bf16[32,2,128,128]{3,2,1,0:T(8,128)(2,1)S(1)} async-done(((bf16[32,2,128,128]{3,2,1,0:T(8,128)(2,1)}), bf16[32,2,128,128]{3,2,1,0:T(8,128)(2,1)S(1)}, u32[]{:S(2)}, u32[]{:S(2)}) %all-to-all-start) | async-done | bytes 2097184 | tf_op jit(solution)/shard_map/all_to_all | solution.py:218
  45.2 0.7 collective-permute-start.1
  46.0 2.0 %collective-permute-start.2 = (bf16[2,2,128,512]{3,2,1,0:T(8,128)(2,1)S(1)}, bf16[2,2,128,512]{3,2,1,0:T(8,128)(2,1)}, u32[]{:S(2)}, u32[]{:S(2)}) collective-permute-start(bf16[2,2,128,512]{3,2,1,0:T(8,128)(2,1)S(1)} %pad_maximum_fusion.2), channel_id=1, source_target_pairs={{0,30},{1,31},{2,28},{3,29},{4,26},{5,27},{6,24},{7,25},{8,22},{9,... | collective-permute-start | bytes 1572872 | tf_op jit(solution)/shard_map/ppermute | solution.py:204
  47.9 4.2 %collective-permute-done.5.refs_3_ = bf16[2,128,512]{2,1,0:T(8,128)(2,1)} collective-permute-done((bf16[2,128,512]{2,1,0:T(8,128)(2,1)}, bf16[2,128,512]{2,1,0:T(8,128)(2,1)}, u32[]{:S(2)}, u32[]{:S(2)}) %collective-permute-start.5) | collective-permute-done | bytes 262176 | tf_op jit(solution)/shard_map/ppermute | solution.py:204
  52.2 4.3 %collective-permute-done.4.refs_2_ = bf16[2,128,512]{2,1,0:T(8,128)(2,1)} collective-permute-done((bf16[2,128,512]{2,1,0:T(8,128)(2,1)}, bf16[2,128,512]{2,1,0:T(8,128)(2,1)}, u32[]{:S(2)}, u32[]{:S(2)}) %collective-permute-start.4) | collective-permute-done | bytes 262176 | tf_op jit(solution)/shard_map/ppermute | solution.py:204
  56.4 18.0 %attention_first.1 = (bf16[2,128,512]{2,1,0:T(8,128)(2,1)}, bf16[2,128,512]{2,1,0:T(8,128)(2,1)}, bf16[32,2,128,128]{3,2,1,0:T(8,128)(2,1)}) custom-call(s32[2]{0:T(128)} %pad_add_fusion.blocks_ref, bf16[2,128,512]{2,1,0:T(8,128)(2,1)} %pad_maximum_fusion.3.refs_0_, bf16[2,128,512]{2,1,0:T(8,128)(2,1)} %collective-permute-done.3.refs_1_, ...), custom_call_target="tpu_custom_call" | custom-call | flops 12000000000 | bytes 8000000 | tf_op jit(solution)/shard_map/attention_first/pallas_call | solution.py:167
  74.4 2.2 %collective-permute-start.6 = (bf16[2,128,512]{2,1,0:T(8,128)(2,1)}, bf16[2,128,512]{2,1,0:T(8,128)(2,1)S(1)}, u32[]{:S(2)}, u32[]{:S(2)}) collective-permute-start(bf16[2,128,512]{2,1,0:T(8,128)(2,1)} %get-tuple-element.21), channel_id=1, source_target_pairs={{0,32},{1,33},{2,34},{3,35},{4,36},{5,37},{6,38},{7,39},{8,40},{9,... | collective-permute-start | bytes 786440 | tf_op jit(solution)/shard_map/ppermute | solution.py:204
  76.6 1.9 %slice_bitcast_fusion = (bf16[2,128,512]{2,1,0:T(8,128)(2,1)}, bf16[2,128,512]{2,1,0:T(8,128)(2,1)}) fusion(bf16[2,2,128,512]{3,2,1,0:T(8,128)(2,1)} %collective-permute-done.2), kind=kLoop, calls=%fused_computation.15 | loop fusion | bytes 1048576 | tf_op jit(solution)/shard_map/squeeze | solution.py:243
  78.5 0.8 slice_bitcast_fusion.2
  79.3 18.8 %attention_second.1 = (bf16[2,128,512]{2,1,0:T(8,128)(2,1)}, bf16[2,128,512]{2,1,0:T(8,128)(2,1)}, bf16[32,2,128,128]{3,2,1,0:T(8,128)(2,1)}) custom-call(s32[2]{0:T(128)} %pad_add_fusion.blocks_ref, bf16[2,128,512]{2,1,0:T(8,128)(2,1)} %get-tuple-element.51.refs_0_, bf16[2,128,512]{2,1,0:T(8,128)(2,1)} %get-tuple-element.50.refs_1_, ...), custom_call_target="tpu_custom_call" | custom-call | flops 12000000000 | bytes 8000000 | tf_op jit(solution)/shard_map/attention_second/pallas_call | solution.py:167
  98.3 0.7 pad_maximum_fusion.7
  100.5 21.3 %all-to-all-start.1 = ((bf16[32,2,128,128]{3,2,1,0:T(8,128)(2,1)}), bf16[32,2,128,128]{3,2,1,0:T(8,128)(2,1)S(1)}, u32[]{:S(2)}, u32[]{:S(2)}) async-start(bf16[32,2,128,128]{3,2,1,0:T(8,128)(2,1)} %get-tuple-element.29), calls=%async_computation.1 | async-start | bytes 4194304 | tf_op jit(solution)/shard_map/all_to_all | solution.py:245
  121.8 1.0 fusion.3
  122.9 4.7 %collective-permute-start.10 = (bf16[2,128,512]{2,1,0:T(8,128)(2,1)S(1)}, bf16[2,128,512]{2,1,0:T(8,128)(2,1)S(1)}, u32[]{:S(2)}, u32[]{:S(2)}) collective-permute-start(bf16[2,128,512]{2,1,0:T(8,128)(2,1)S(1)} %pad_maximum_fusion.9), channel_id=1, source_target_pairs={{0,30},{1,31},{2,28},{3,29},{4,26},{5,27},{6,24},{7,25},{8,22},{9,... | collective-permute-start | bytes 786440 | tf_op jit(solution)/shard_map/ppermute | solution.py:204
  127.6 3.1 %collective-permute-start.9 = (bf16[2,128,512]{2,1,0:T(8,128)(2,1)S(1)}, bf16[2,128,512]{2,1,0:T(8,128)(2,1)S(1)}, u32[]{:S(2)}, u32[]{:S(2)}) collective-permute-start(bf16[2,128,512]{2,1,0:T(8,128)(2,1)S(1)} %pad_maximum_fusion.8), channel_id=1, source_target_pairs={{0,64},{1,65},{2,66},{3,67},{4,68},{5,69},{6,70},{7,71},{8,72},{9,... | collective-permute-start | bytes 786440 | tf_op jit(solution)/shard_map/ppermute | solution.py:204
  130.7 0.9 slice_dynamic-update-slice_fusion.5
  131.7 0.9 slice_dynamic-update-slice_fusion.4
  132.6 23.0 %collective-permute-done.9 = bf16[2,128,512]{2,1,0:T(8,128)(2,1)S(1)} collective-permute-done((bf16[2,128,512]{2,1,0:T(8,128)(2,1)S(1)}, bf16[2,128,512]{2,1,0:T(8,128)(2,1)S(1)}, u32[]{:S(2)}, u32[]{:S(2)}) %collective-permute-start.9) | collective-permute-done | bytes 262176 | tf_op jit(solution)/shard_map/ppermute | solution.py:204
  156.7 0.8 copy.13
  (48 shorter events, 5.2 us)
Async XLA Ops:
  4.8 11.4 %copy-start.1 = (bf16[1,128,4096]{2,1,0:T(8,128)(2,1)S(1)}, bf16[1,128,4096]{2,1,0:T(8,128)(2,1)}, u32[]{:S(2)}) copy-start(bf16[1,128,4096]{2,1,0:T(8,128)(2,1)} %param.5) | copy-start | bytes 3145732
  4.8 40.5 %all-to-all-start = ((bf16[32,2,128,128]{3,2,1,0:T(8,128)(2,1)}), bf16[32,2,128,128]{3,2,1,0:T(8,128)(2,1)S(1)}, u32[]{:S(2)}, u32[]{:S(2)}) async-start(bf16[32,2,128,128]{3,2,1,0:T(8,128)(2,1)} %bitcast.6), calls=%async_computation | async-start | bytes 4194304 | tf_op jit(solution)/shard_map/all_to_all | solution.py:218
  18.5 12.9 %collective-permute-start = (bf16[2,2,128,512]{3,2,1,0:T(8,128)(2,1)S(1)}, bf16[2,2,128,512]{3,2,1,0:T(8,128)(2,1)S(1)}, u32[]{:S(2)}, u32[]{:S(2)}) collective-permute-start(bf16[2,2,128,512]{3,2,1,0:T(8,128)(2,1)S(1)} %pad_maximum_fusion), channel_id=1, source_target_pairs={{0,32},{1,33},{2,34},{3,35},{4,36},{5,37},{6,38},{7,39},{8,40},{9,... | collective-permute-start | bytes 1572872 | tf_op jit(solution)/shard_map/ppermute | solution.py:204
  20.2 31.9 %collective-permute-start.5 = (bf16[2,128,512]{2,1,0:T(8,128)(2,1)}, bf16[2,128,512]{2,1,0:T(8,128)(2,1)}, u32[]{:S(2)}, u32[]{:S(2)}) collective-permute-start(bf16[2,128,512]{2,1,0:T(8,128)(2,1)} %pad_maximum_fusion.6), channel_id=1, source_target_pairs={{0,126},{1,127},{2,124},{3,125},{4,122},{5,123},{6,120},{7,121},{8... | collective-permute-start | bytes 786440 | tf_op jit(solution)/shard_map/ppermute | solution.py:204
  26.2 30.2 %collective-permute-start.4 = (bf16[2,128,512]{2,1,0:T(8,128)(2,1)}, bf16[2,128,512]{2,1,0:T(8,128)(2,1)}, u32[]{:S(2)}, u32[]{:S(2)}) collective-permute-start(bf16[2,128,512]{2,1,0:T(8,128)(2,1)} %pad_maximum_fusion.5), channel_id=1, source_target_pairs={{0,94},{1,95},{2,92},{3,93},{4,90},{5,91},{6,88},{7,89},{8,86},{9,... | collective-permute-start | bytes 786440 | tf_op jit(solution)/shard_map/ppermute | solution.py:204
  27.3 29.1 %collective-permute-start.3 = (bf16[2,128,512]{2,1,0:T(8,128)(2,1)}, bf16[2,128,512]{2,1,0:T(8,128)(2,1)}, u32[]{:S(2)}, u32[]{:S(2)}) collective-permute-start(bf16[2,128,512]{2,1,0:T(8,128)(2,1)} %pad_maximum_fusion.4), channel_id=1, source_target_pairs={{0,32},{1,33},{2,34},{3,35},{4,36},{5,37},{6,38},{7,39},{8,40},{9,... | collective-permute-start | bytes 786440 | tf_op jit(solution)/shard_map/ppermute | solution.py:204
  45.2 11.2 %copy-start = (bf16[32,2,128,128]{3,2,1,0:T(8,128)(2,1)}, bf16[32,2,128,128]{3,2,1,0:T(8,128)(2,1)S(1)}, u32[]{:S(2)}) copy-start(bf16[32,2,128,128]{3,2,1,0:T(8,128)(2,1)S(1)} %all-to-all-done.refs_4_) | copy-start | bytes 6291460
  45.2 31.4 %collective-permute-start.1 = (bf16[2,2,128,512]{3,2,1,0:T(8,128)(2,1)S(1)}, bf16[2,2,128,512]{3,2,1,0:T(8,128)(2,1)S(1)}, u32[]{:S(2)}, u32[]{:S(2)}) collective-permute-start(bf16[2,2,128,512]{3,2,1,0:T(8,128)(2,1)S(1)} %pad_maximum_fusion.1), channel_id=1, source_target_pairs={{0,64},{1,65},{2,66},{3,67},{4,68},{5,69},{6,70},{7,71},{8,72},{9,... | collective-permute-start | bytes 1572872 | tf_op jit(solution)/shard_map/ppermute | solution.py:204
  46.0 30.7 %collective-permute-start.2 = (bf16[2,2,128,512]{3,2,1,0:T(8,128)(2,1)S(1)}, bf16[2,2,128,512]{3,2,1,0:T(8,128)(2,1)}, u32[]{:S(2)}, u32[]{:S(2)}) collective-permute-start(bf16[2,2,128,512]{3,2,1,0:T(8,128)(2,1)S(1)} %pad_maximum_fusion.2), channel_id=1, source_target_pairs={{0,30},{1,31},{2,28},{3,29},{4,26},{5,27},{6,24},{7,25},{8,22},{9,... | collective-permute-start | bytes 1572872 | tf_op jit(solution)/shard_map/ppermute | solution.py:204
  74.4 23.8 %collective-permute-start.6 = (bf16[2,128,512]{2,1,0:T(8,128)(2,1)}, bf16[2,128,512]{2,1,0:T(8,128)(2,1)S(1)}, u32[]{:S(2)}, u32[]{:S(2)}) collective-permute-start(bf16[2,128,512]{2,1,0:T(8,128)(2,1)} %get-tuple-element.21), channel_id=1, source_target_pairs={{0,32},{1,33},{2,34},{3,35},{4,36},{5,37},{6,38},{7,39},{8,40},{9,... | collective-permute-start | bytes 786440 | tf_op jit(solution)/shard_map/ppermute | solution.py:204
  79.3 18.9 %copy-start.3 = (bf16[2,128,512]{2,1,0:T(8,128)(2,1)S(1)}, bf16[2,128,512]{2,1,0:T(8,128)(2,1)}, u32[]{:S(2)}) copy-start(bf16[2,128,512]{2,1,0:T(8,128)(2,1)} %get-tuple-element.20) | copy-start | bytes 786436
  98.1 1.7 %collective-permute-start.8 = (bf16[2,128,512]{2,1,0:T(8,128)(2,1)}, bf16[2,128,512]{2,1,0:T(8,128)(2,1)S(1)}, u32[]{:S(2)}, u32[]{:S(2)}) collective-permute-start(bf16[2,128,512]{2,1,0:T(8,128)(2,1)} %get-tuple-element.26), channel_id=1, source_target_pairs={{0,32},{1,33},{2,34},{3,35},{4,36},{5,37},{6,38},{7,39},{8,40},{9,... | collective-permute-start | bytes 786440 | tf_op jit(solution)/shard_map/ppermute | solution.py:204
  99.0 31.7 %collective-permute-start.7 = (bf16[2,128,512]{2,1,0:T(8,128)(2,1)}, bf16[2,128,512]{2,1,0:T(8,128)(2,1)}, u32[]{:S(2)}, u32[]{:S(2)}) collective-permute-start(bf16[2,128,512]{2,1,0:T(8,128)(2,1)} %pad_maximum_fusion.7), channel_id=1, source_target_pairs={{0,94},{1,95},{2,92},{3,93},{4,90},{5,91},{6,88},{7,89},{8,86},{9,... | collective-permute-start | bytes 786440 | tf_op jit(solution)/shard_map/ppermute | solution.py:204
  99.8 0.7 copy-start.5
  100.5 21.3 %copy-start.4 = (bf16[2,128,512]{2,1,0:T(8,128)(2,1)S(1)}, bf16[2,128,512]{2,1,0:T(8,128)(2,1)}, u32[]{:S(2)}) copy-start(bf16[2,128,512]{2,1,0:T(8,128)(2,1)} %get-tuple-element.25) | copy-start | bytes 786436
  100.5 55.7 %all-to-all-start.1 = ((bf16[32,2,128,128]{3,2,1,0:T(8,128)(2,1)}), bf16[32,2,128,128]{3,2,1,0:T(8,128)(2,1)S(1)}, u32[]{:S(2)}, u32[]{:S(2)}) async-start(bf16[32,2,128,128]{3,2,1,0:T(8,128)(2,1)} %get-tuple-element.29), calls=%async_computation.1 | async-start | bytes 4194304 | tf_op jit(solution)/shard_map/all_to_all | solution.py:245
  122.9 33.3 %collective-permute-start.10 = (bf16[2,128,512]{2,1,0:T(8,128)(2,1)S(1)}, bf16[2,128,512]{2,1,0:T(8,128)(2,1)S(1)}, u32[]{:S(2)}, u32[]{:S(2)}) collective-permute-start(bf16[2,128,512]{2,1,0:T(8,128)(2,1)S(1)} %pad_maximum_fusion.9), channel_id=1, source_target_pairs={{0,30},{1,31},{2,28},{3,29},{4,26},{5,27},{6,24},{7,25},{8,22},{9,... | collective-permute-start | bytes 786440 | tf_op jit(solution)/shard_map/ppermute | solution.py:204
  127.6 28.0 %collective-permute-start.9 = (bf16[2,128,512]{2,1,0:T(8,128)(2,1)S(1)}, bf16[2,128,512]{2,1,0:T(8,128)(2,1)S(1)}, u32[]{:S(2)}, u32[]{:S(2)}) collective-permute-start(bf16[2,128,512]{2,1,0:T(8,128)(2,1)S(1)} %pad_maximum_fusion.8), channel_id=1, source_target_pairs={{0,64},{1,65},{2,66},{3,67},{4,68},{5,69},{6,70},{7,71},{8,72},{9,... | collective-permute-start | bytes 786440 | tf_op jit(solution)/shard_map/ppermute | solution.py:204
  156.2 1.3 copy-start.2

commit v5 on v4

--- a/solution.py
+++ b/solution.py
@@ -36,12 +36,15 @@
 
 
 def attention_kernel(first, blocks_ref, *refs):
-    units, refs = refs[:4], refs[4:]
+    if first:
+        units, refs = refs[:4], refs[4:]
+    else:
+        units, refs = [ref.at[layer] for ref in refs[:2] for layer in range(LAYERS)], refs[2:]
     kv_ref, refs = refs[0], refs[1:]
     if not first:
         sums_ref, refs = refs[0], refs[1:]
-    mine_ref, other_ref, term_ref = refs[:3]
-    q_s, do_s, kt_s, w_s, g_s, m_s, dk_s, dv_s, dq_s, stat_s = refs[3:]
+    grad_refs, term_ref = refs[:4], refs[4]
+    q_s, do_s, kt_s, w_s, g_s, m_s, dk_s, dv_s, dq_s, stat_s = refs[5:]
     for n in range(2):
         for layer in range(LAYERS):
             unit = units[n * LAYERS + layer]
@@ -149,10 +152,10 @@
 
     lax.fori_loop(0, 2, one_group, 0)
     for n in range(2):
-        for layer, out_ref in enumerate((mine_ref, other_ref)):
+        for layer in range(LAYERS):
             for g in range(GROUPS):
                 lo = layer * WIDTH + g * HEAD_DIM
-                out_ref[n, :, g * HEAD_DIM : (g + 1) * HEAD_DIM] = q_s[n, lo : lo + ROWS, :]
+                grad_refs[n * LAYERS + layer][:, g * HEAD_DIM : (g + 1) * HEAD_DIM] = q_s[n, lo : lo + ROWS, :]
     for j in range(CHUNKS):
         blocks = slice(j * SPAN, (j + 1) * SPAN)
         key_grad = dk_s[j] if first else dk_s[j] * SCALE
@@ -166,10 +169,10 @@
     args = [*units, kv] + ([] if first else [sums])
     return pl.pallas_call(
         functools.partial(attention_kernel, first),
-        out_shape=[jax.ShapeDtypeStruct((2, ROWS, WIDTH), BF16)] * 2
+        out_shape=[jax.ShapeDtypeStruct((ROWS, WIDTH), BF16)] * 4
         + [jax.ShapeDtypeStruct((BLOCKS, 2, ROWS, HEAD_DIM), BF16)],
         in_specs=[pl.BlockSpec(memory_space=pltpu.SMEM)] + [vmem] * len(args),
-        out_specs=[vmem] * 3,
+        out_specs=[vmem] * 5,
         scratch_shapes=[
             pltpu.VMEM((2, GROUP_ROWS, HEAD_DIM), BF16),
             pltpu.VMEM((2, GROUP_ROWS, HEAD_DIM), BF16),
@@ -188,6 +191,27 @@
     )(blocks, *args)
 
 
+def spread_kernel(scales_ref, codes_ref, out_ref):
+    for which in range(2):
+        for part in range(ROWS // QUANT_BLOCK):
+            rows = slice(part * QUANT_BLOCK, (part + 1) * QUANT_BLOCK)
+            for head in range(2):
+                codes = codes_ref[which, rows, head * HEAD_DIM : (head + 1) * HEAD_DIM].astype(F32)
+                values = (codes * scales_ref[which, part, head]).astype(BF16)
+                for to in range(16):
+                    out_ref[head * 16 + to, which, rows, :] = values
+
+
+def spread_cache(kv_codes, kv_scales):
+    return pl.pallas_call(
+        spread_kernel,
+        out_shape=jax.ShapeDtypeStruct((BLOCKS, 2, ROWS, HEAD_DIM), BF16),
+        in_specs=[pl.BlockSpec(memory_space=pltpu.SMEM), pl.BlockSpec(memory_space=pltpu.VMEM)],
+        out_specs=pl.BlockSpec(memory_space=pltpu.VMEM),
+        name="spread_cache",
+    )(kv_scales, kv_codes)
+
+
 CORE, FLIP, NEAR = 1, 2, 4
 ACROSS = NEAR | FLIP
 
@@ -211,11 +235,7 @@
     def of(k):
         return head ^ (4 if k & NEAR else 0) ^ (2 if k & CORE else 0) ^ (1 if k & FLIP else 0)
 
-    codes = kv_codes.reshape(2, ROWS // QUANT_BLOCK, QUANT_BLOCK, 2, HEAD_DIM).astype(F32)
-    cache = (codes * kv_scales[:, :, None, :, None]).astype(BF16)
-    cache = cache.reshape(2, ROWS, 2, HEAD_DIM).transpose(2, 0, 1, 3)
-    spread = jnp.broadcast_to(cache[:, None], (2, 16, 2, ROWS, HEAD_DIM)).reshape(BLOCKS, 2, ROWS, HEAD_DIM)
-    kv = lax.all_to_all(spread, "blk", 0, 0, tiled=True)
+    kv = lax.all_to_all(spread_cache(kv_codes, kv_scales), "blk", 0, 0, tiled=True)
 
     def pick(k):
         at = of(k) * WIDTH
@@ -228,24 +248,17 @@
     across_core = move(pick(ACROSS | CORE), ACROSS | CORE)
     own, own_core = pick(0), move(pick(CORE), CORE)
     swapped = move(jnp.stack([pick(NEAR | CORE), pick(FLIP | CORE)]), CORE)
-    near, turned, kv = lax.optimization_barrier(
-        (jnp.stack([pick(NEAR), swapped[0]]), jnp.stack([pick(FLIP), swapped[1]]), kv)
-    )
+    near, turned = jnp.stack([pick(NEAR), swapped[0]]), jnp.stack([pick(FLIP), swapped[1]])
+    near, turned, kv, across, across_core = lax.optimization_barrier((near, turned, kv, across, across_core))
     near, turned = move(near, NEAR), move(turned, FLIP)
 
-    mine, other, sums = attention(blocks, (own, own_core, across, across_core), kv)
-    near, turned, mine = lax.optimization_barrier((near, turned, mine))
-    other = move(other, CORE)
-    grads = {0: mine[0], CORE: other[0]}
-    sent = move(jnp.stack([mine[1], other[1]]), ACROSS)
-    grads |= {ACROSS: sent[0], ACROSS | CORE: sent[1]}
-
-    mine, other, term = attention(blocks, (near[0], near[1], turned[0], turned[1]), kv, sums)
-    other, term = lax.optimization_barrier((move(other, CORE), term))
+    *first, sums = attention(blocks, (own, own_core, across, across_core), kv)
+    near, turned, first[0] = lax.optimization_barrier((near, turned, first[0]))
+    *second, term = attention(blocks, (near, turned), kv, sums)
     received = lax.all_to_all(term, "blk", 0, 0, tiled=True)
-    for n, k in enumerate((NEAR, FLIP)):
-        sent = move(jnp.stack([mine[n], other[n]]), k)
-        grads |= {k: sent[0], k | CORE: sent[1]}
+    grads = {}
+    for k, grad in zip((0, CORE, ACROSS, ACROSS | CORE, NEAR, NEAR | CORE, FLIP, FLIP | CORE), first + second):
+        grads[k] = move(grad, k) if k else grad
 
     kv_grad = received.reshape(2, 16, 2, ROWS, HEAD_DIM).astype(F32).sum(1)
     kv_grad = kv_grad.transpose(1, 2, 0, 3).reshape(2, ROWS, 2 * HEAD_DIM)

time: 160 us -> 151 us (0.944); the launches traced: 158 us -> 151 us
  local copies, waits for them, and re-layouts: 12.5 us -> 6.14 us
  starting transfers between devices: 53.4 us -> 50.1 us
  waiting for transfers between devices: 45.9 us -> 48.7 us
  Pallas kernels: 36.8 us -> 39.2 us
  other arithmetic: 8.08 us -> 6.02 us
    ppermute x11 -> x13, waiting for transfers between devices: 32.2 us -> 48.7 us  [move(): return lax.ppermute(x, AXES, partners(k))]
    all_to_all x1, waiting for transfers between devices: 13.7 us -> 0.01 us  [shards(): lax.all_to_all(spread_cache(kv_codes, kv_scales), 'blk', 0, 0, tiled=True)]
    all_to_all x1, starting transfers between devices: 21.3 us -> 13.5 us  [shards(): received = lax.all_to_all(term, 'blk', 0, 0, tiled=True)]
    ppermute x11 -> x13, starting transfers between devices: 20.8 us -> 25.2 us  [move(): return lax.ppermute(x, AXES, partners(k))]
    squeeze x2 -> x0, local copies, waits for them, and re-layouts: 2.7 us -> none  [the longest x1 1.86 us: shards(): turned[1]]
    pallas_call x0 -> x1, Pallas kernels: none -> 2.5 us  [spread_cache(): pl.pallas_call(spread_kernel, out_shape=jax.ShapeDtypeStruct((BLOCKS, 2,...]
    broadcast_in_dim x1 -> x0, local copies, waits for them, and re-layouts: 1.85 us -> none  [shards(): jnp.broadcast_to(cache[:, None], (2, 16, 2, ROWS, HEAD_DIM))]
    dynamic_update_slice x6 -> x8, local copies, waits for them, and re-layouts: 1.89 us -> 0.11 us  [shards(): lax.dynamic_update_slice_in_dim(query_grad, part, of(k) * WIDTH, 1)]
  transfers between devices with their start and end apart: 13 -> 15, of which waited for: 6 -> 6; matrix products, arithmetic and copies ran while one was open for 9% -> 5% of each run, Pallas kernels for 23% -> 12%
where the time goes in v5:
time: 151 us
  starting transfers between devices  50.1 us (33%)
  waiting for transfers between devices  48.7 us (32%)
  Pallas kernels  39.2 us (26%)
  local copies, waits for them, and re-layouts  6.14 us (4%)
  other arithmetic  6.02 us (4%)
    ppermute x13, waiting for transfers between devices, move(): return lax.ppermute(x, AXES, partners(k))  48.7 us
    pallas_call x2, Pallas kernels, attention(): pl.pallas_call(functools.partial(attention_kernel, first), out_shape=[jax...  36.7 us
    ppermute x13, starting transfers between devices, move(): return lax.ppermute(x, AXES, partners(k))  25.2 us
    all_to_all x1, starting transfers between devices, shards(): received = lax.all_to_all(term, 'blk', 0, 0, tiled=True)  13.5 us
    all_to_all x1, starting transfers between devices, shards(): lax.all_to_all(spread_cache(kv_codes, kv_scales), 'blk', 0, 0, tiled=True)  11.3 us
    unnamed x16, local copies, waits for them, and re-layouts  3.58 us
  transfers between devices with their start and end apart: 15, of which 6 were waited for; matrix products, arithmetic and copies ran while one was open for 5% of the time, Pallas kernels for 12%

profile of v5, /device:TPU:1, one launch (start us, length us, event | category | flops | bytes accessed | tf_op | source)
XLA Modules:
  0.0 151.1 jit_solution(5476330984884743731)
XLA Ops:
  0.6 1.4 copy.8.scales_ref
  2.0 2.5 %spread_cache.1 = bf16[32,2,128,128]{3,2,1,0:T(8,128)(2,1)} custom-call(f32[2,4,2]{2,1,0:T(4,128)} %copy.8.scales_ref, s32[2,128,256]{2,1,0:T(8,128)} %codes_ref.1), custom_call_target="tpu_custom_call" | custom-call | tf_op jit(solution)/shard_map/spread_cache/pallas_call | solution.py:206
  4.5 11.3 %all-to-all-start = ((bf16[32,2,128,128]{3,2,1,0:T(8,128)(2,1)}), bf16[32,2,128,128]{3,2,1,0:T(8,128)(2,1)S(1)}, u32[]{:S(2)}, u32[]{:S(2)}) async-start(bf16[32,2,128,128]{3,2,1,0:T(8,128)(2,1)} %spread_cache.1), calls=%async_computation | async-start | bytes 4194304 | tf_op jit(solution)/shard_map/all_to_all | solution.py:238
  15.9 2.2 %constant_dynamic-slice_fusion = (bf16[1,128,512]{2,1,0:T(8,128)(2,1)S(1)}, bf16[1,128,512]{2,1,0:T(8,128)(2,1)S(1)}, bf16[1,128,512]{2,1,0:T(8,128)(2,1)S(1)}, ...) fusion(bf16[1,128,4096]{2,1,0:T(8,128)(2,1)S(1)} %copy-done.1, ...), kind=kLoop, calls=%fused_computation.20 | loop fusion | bytes 4194336 | tf_op jit(solution)/shard_map/dynamic_slice | solution.py:243
  18.1 0.7 pad_maximum_fusion.3
  18.8 5.1 %collective-permute-start.1 = (bf16[2,128,512]{2,1,0:T(8,128)(2,1)}, bf16[2,128,512]{2,1,0:T(8,128)(2,1)}, u32[]{:S(2)}, u32[]{:S(2)}) collective-permute-start(bf16[2,128,512]{2,1,0:T(8,128)(2,1)} %pad_maximum_fusion.3), channel_id=1, source_target_pairs={{0,94},{1,95},{2,92},{3,93},{4,90},{5,91},{6,88},{7,89},{8,86},{9,... | collective-permute-start | bytes 786440 | tf_op jit(solution)/shard_map/ppermute | solution.py:228
  23.9 0.7 pad_maximum_fusion.4
  24.6 1.7 %collective-permute-start.2 = (bf16[2,128,512]{2,1,0:T(8,128)(2,1)}, bf16[2,128,512]{2,1,0:T(8,128)(2,1)}, u32[]{:S(2)}, u32[]{:S(2)}) collective-permute-start(bf16[2,128,512]{2,1,0:T(8,128)(2,1)} %pad_maximum_fusion.4), channel_id=1, source_target_pairs={{0,126},{1,127},{2,124},{3,125},{4,122},{5,123},{6,120},{7,121},{8... | collective-permute-start | bytes 786440 | tf_op jit(solution)/shard_map/ppermute | solution.py:228
  26.5 0.7 pad_maximum_fusion.6
  27.8 0.7 pad_add_fusion.blocks_ref
  28.4 1.0 maximum_bitcast_fusion.3
  29.4 0.9 maximum_bitcast_fusion
  30.4 0.7 pad_maximum_fusion.5.refs_0_
  31.2 19.3 %collective-permute-done.1.refs_2_ = bf16[2,128,512]{2,1,0:T(8,128)(2,1)} collective-permute-done((bf16[2,128,512]{2,1,0:T(8,128)(2,1)}, bf16[2,128,512]{2,1,0:T(8,128)(2,1)}, u32[]{:S(2)}, u32[]{:S(2)}) %collective-permute-start.1) | collective-permute-done | bytes 262176 | tf_op jit(solution)/shard_map/ppermute | solution.py:228
  50.5 6.1 %collective-permute-done.2.refs_3_ = bf16[2,128,512]{2,1,0:T(8,128)(2,1)} collective-permute-done((bf16[2,128,512]{2,1,0:T(8,128)(2,1)}, bf16[2,128,512]{2,1,0:T(8,128)(2,1)}, u32[]{:S(2)}, u32[]{:S(2)}) %collective-permute-start.2) | collective-permute-done | bytes 262176 | tf_op jit(solution)/shard_map/ppermute | solution.py:228
  56.7 0.7 collective-permute-start.3
  57.4 0.6 copy-done
  58.0 18.0 %attention_first.1 = (bf16[128,512]{1,0:T(8,128)(2,1)}, bf16[128,512]{1,0:T(8,128)(2,1)}, bf16[128,512]{1,0:T(8,128)(2,1)}, bf16[128,512]{1,0:T(8,128)(2,1)}, bf16[32,2,128,128]{3,2,1,0:T(8,128)(2,1)}) custom-call(s32[2]{0:T(128)} %pad_add_fusion.blocks_ref, bf16[2,128,512]{2,1,0:T(8,128)(2,1)} %pad_maximum_fusion.5.refs_0_, ...), custom_call_target="tpu_custom_call" | custom-call | flops 12000000000 | bytes 8000000 | tf_op jit(solution)/shard_map/attention_first/pallas_call | solution.py:170
  76.0 0.8 copy-done.4
  76.8 18.7 %attention_second.1 = (bf16[128,512]{1,0:T(8,128)(2,1)}, bf16[128,512]{1,0:T(8,128)(2,1)}, bf16[128,512]{1,0:T(8,128)(2,1)}, bf16[128,512]{1,0:T(8,128)(2,1)}, bf16[32,2,128,128]{3,2,1,0:T(8,128)(2,1)}) custom-call(s32[2]{0:T(128)} %pad_add_fusion.blocks_ref, bf16[2,2,128,512]{3,2,1,0:T(8,128)(2,1)} %copy-done.4, ...), custom_call_target="tpu_custom_call" | custom-call | flops 12000000000 | bytes 8000000 | tf_op jit(solution)/shard_map/attention_second/pallas_call | solution.py:170
  95.5 13.5 %all-to-all-start.1 = ((bf16[32,2,128,128]{3,2,1,0:T(8,128)(2,1)}), bf16[32,2,128,128]{3,2,1,0:T(8,128)(2,1)S(1)}, u32[]{:S(2)}, u32[]{:S(2)}) async-start(bf16[32,2,128,128]{3,2,1,0:T(8,128)(2,1)} %get-tuple-element.37), calls=%async_computation.1 | async-start | bytes 4194304 | tf_op jit(solution)/shard_map/all_to_all | solution.py:258
  109.0 2.3 %collective-permute-start.6 = (bf16[128,512]{1,0:T(8,128)(2,1)}, bf16[128,512]{1,0:T(8,128)(2,1)S(1)}, u32[]{:S(2)}, u32[]{:S(2)}) collective-permute-start(bf16[128,512]{1,0:T(8,128)(2,1)} %get-tuple-element.27), channel_id=1, source_target_pairs={{0,32},{1,33},{2,34},{3,35},{4,36},{5,37},{6,38},{7,39},{8,40},{9,... | collective-permute-start | bytes 393224 | tf_op jit(solution)/shard_map/ppermute | solution.py:228
  111.4 2.5 %collective-permute-start.7 = (bf16[128,512]{1,0:T(8,128)(2,1)}, bf16[128,512]{1,0:T(8,128)(2,1)S(1)}, u32[]{:S(2)}, u32[]{:S(2)}) collective-permute-start(bf16[128,512]{1,0:T(8,128)(2,1)} %get-tuple-element.28), channel_id=1, source_target_pairs={{0,94},{1,95},{2,92},{3,93},{4,90},{5,91},{6,88},{7,89},{8,86},{9,... | collective-permute-start | bytes 393224 | tf_op jit(solution)/shard_map/ppermute | solution.py:228
  113.9 3.5 %collective-permute-start.8 = (bf16[128,512]{1,0:T(8,128)(2,1)}, bf16[128,512]{1,0:T(8,128)(2,1)S(1)}, u32[]{:S(2)}, u32[]{:S(2)}) collective-permute-start(bf16[128,512]{1,0:T(8,128)(2,1)} %get-tuple-element.29), channel_id=1, source_target_pairs={{0,126},{1,127},{2,124},{3,125},{4,122},{5,123},{6,120},{7,121},{8... | collective-permute-start | bytes 393224 | tf_op jit(solution)/shard_map/ppermute | solution.py:228
  117.5 1.6 %collective-permute-start.10 = (bf16[128,512]{1,0:T(8,128)(2,1)}, bf16[128,512]{1,0:T(8,128)(2,1)S(1)}, u32[]{:S(2)}, u32[]{:S(2)}) collective-permute-start(bf16[128,512]{1,0:T(8,128)(2,1)} %get-tuple-element.34), channel_id=1, source_target_pairs={{0,96},{1,97},{2,98},{3,99},{4,100},{5,101},{6,102},{7,103},{8,104... | collective-permute-start | bytes 393224 | tf_op jit(solution)/shard_map/ppermute | solution.py:228
  119.3 5.0 %collective-permute-start.11 = (bf16[128,512]{1,0:T(8,128)(2,1)S(1)}, bf16[128,512]{1,0:T(8,128)(2,1)S(1)}, u32[]{:S(2)}, u32[]{:S(2)}) collective-permute-start(bf16[128,512]{1,0:T(8,128)(2,1)S(1)} %copy-done.6), channel_id=1, source_target_pairs={{0,30},{1,31},{2,28},{3,29},{4,26},{5,27},{6,24},{7,25},{8,22},{9,... | collective-permute-start | bytes 393224 | tf_op jit(solution)/shard_map/ppermute | solution.py:228
  124.3 16.2 %collective-permute-done.7 = bf16[128,512]{1,0:T(8,128)(2,1)S(1)} collective-permute-done((bf16[128,512]{1,0:T(8,128)(2,1)}, bf16[128,512]{1,0:T(8,128)(2,1)S(1)}, u32[]{:S(2)}, u32[]{:S(2)}) %collective-permute-start.7) | collective-permute-done | bytes 131104 | tf_op jit(solution)/shard_map/ppermute | solution.py:228
  140.5 2.0 %collective-permute-start.12 = (bf16[128,512]{1,0:T(8,128)(2,1)S(1)}, bf16[128,512]{1,0:T(8,128)(2,1)S(1)}, u32[]{:S(2)}, u32[]{:S(2)}) collective-permute-start(bf16[128,512]{1,0:T(8,128)(2,1)S(1)} %copy-done.5), channel_id=1, source_target_pairs={{0,62},{1,63},{2,60},{3,61},{4,58},{5,59},{6,56},{7,57},{8,54},{9,... | collective-permute-start | bytes 393224 | tf_op jit(solution)/shard_map/ppermute | solution.py:228
  142.6 1.9 %collective-permute-done.10 = bf16[128,512]{1,0:T(8,128)(2,1)S(1)} collective-permute-done((bf16[128,512]{1,0:T(8,128)(2,1)}, bf16[128,512]{1,0:T(8,128)(2,1)S(1)}, u32[]{:S(2)}, u32[]{:S(2)}) %collective-permute-start.10) | collective-permute-done | bytes 131104 | tf_op jit(solution)/shard_map/ppermute | solution.py:228
  144.6 1.2 collective-permute-done.11
  145.8 3.9 %collective-permute-done.12 = bf16[128,512]{1,0:T(8,128)(2,1)S(1)} collective-permute-done((bf16[128,512]{1,0:T(8,128)(2,1)S(1)}, bf16[128,512]{1,0:T(8,128)(2,1)S(1)}, u32[]{:S(2)}, u32[]{:S(2)}) %collective-permute-start.12) | collective-permute-done | bytes 131104 | tf_op jit(solution)/shard_map/ppermute | solution.py:228
  150.2 0.8 copy.10
  (42 shorter events, 1.8 us)
Async XLA Ops:
  4.5 11.4 %copy-start.1 = (bf16[1,128,4096]{2,1,0:T(8,128)(2,1)S(1)}, bf16[1,128,4096]{2,1,0:T(8,128)(2,1)}, u32[]{:S(2)}) copy-start(bf16[1,128,4096]{2,1,0:T(8,128)(2,1)} %param.5) | copy-start | bytes 3145732
  4.5 52.2 %all-to-all-start = ((bf16[32,2,128,128]{3,2,1,0:T(8,128)(2,1)}), bf16[32,2,128,128]{3,2,1,0:T(8,128)(2,1)S(1)}, u32[]{:S(2)}, u32[]{:S(2)}) async-start(bf16[32,2,128,128]{3,2,1,0:T(8,128)(2,1)} %spread_cache.1), calls=%async_computation | async-start | bytes 4194304 | tf_op jit(solution)/shard_map/all_to_all | solution.py:238
  18.8 31.7 %collective-permute-start.1 = (bf16[2,128,512]{2,1,0:T(8,128)(2,1)}, bf16[2,128,512]{2,1,0:T(8,128)(2,1)}, u32[]{:S(2)}, u32[]{:S(2)}) collective-permute-start(bf16[2,128,512]{2,1,0:T(8,128)(2,1)} %pad_maximum_fusion.3), channel_id=1, source_target_pairs={{0,94},{1,95},{2,92},{3,93},{4,90},{5,91},{6,88},{7,89},{8,86},{9,... | collective-permute-start | bytes 786440 | tf_op jit(solution)/shard_map/ppermute | solution.py:228
  24.6 32.0 %collective-permute-start.2 = (bf16[2,128,512]{2,1,0:T(8,128)(2,1)}, bf16[2,128,512]{2,1,0:T(8,128)(2,1)}, u32[]{:S(2)}, u32[]{:S(2)}) collective-permute-start(bf16[2,128,512]{2,1,0:T(8,128)(2,1)} %pad_maximum_fusion.4), channel_id=1, source_target_pairs={{0,126},{1,127},{2,124},{3,125},{4,122},{5,123},{6,120},{7,121},{8... | collective-permute-start | bytes 786440 | tf_op jit(solution)/shard_map/ppermute | solution.py:228
  26.5 4.6 %collective-permute-start = (bf16[2,2,128,512]{3,2,1,0:T(8,128)(2,1)S(1)}, bf16[2,2,128,512]{3,2,1,0:T(8,128)(2,1)S(1)}, u32[]{:S(2)}, u32[]{:S(2)}) collective-permute-start(bf16[2,2,128,512]{3,2,1,0:T(8,128)(2,1)S(1)} %pad_maximum_fusion), channel_id=1, source_target_pairs={{0,32},{1,33},{2,34},{3,35},{4,36},{5,37},{6,38},{7,39},{8,40},{9,... | collective-permute-start | bytes 1572872 | tf_op jit(solution)/shard_map/ppermute | solution.py:228
  27.3 30.1 %collective-permute-start.5 = (bf16[2,128,512]{2,1,0:T(8,128)(2,1)}, bf16[2,128,512]{2,1,0:T(8,128)(2,1)}, u32[]{:S(2)}, u32[]{:S(2)}) collective-permute-start(bf16[2,128,512]{2,1,0:T(8,128)(2,1)} %pad_maximum_fusion.6), channel_id=1, source_target_pairs={{0,32},{1,33},{2,34},{3,35},{4,36},{5,37},{6,38},{7,39},{8,40},{9,... | collective-permute-start | bytes 786440 | tf_op jit(solution)/shard_map/ppermute | solution.py:228
  56.6 1.3 copy-start
  56.7 19.3 %collective-permute-start.3 = (bf16[2,2,128,512]{3,2,1,0:T(8,128)(2,1)S(1)}, bf16[2,2,128,512]{3,2,1,0:T(8,128)(2,1)S(1)}, u32[]{:S(2)}, u32[]{:S(2)}) collective-permute-start(bf16[2,2,128,512]{3,2,1,0:T(8,128)(2,1)S(1)} %pad_maximum_fusion.1), channel_id=1, source_target_pairs={{0,64},{1,65},{2,66},{3,67},{4,68},{5,69},{6,70},{7,71},{8,72},{9,... | collective-permute-start | bytes 1572872 | tf_op jit(solution)/shard_map/ppermute | solution.py:228
  57.4 18.6 %collective-permute-start.4 = (bf16[2,2,128,512]{3,2,1,0:T(8,128)(2,1)S(1)}, bf16[2,2,128,512]{3,2,1,0:T(8,128)(2,1)}, u32[]{:S(2)}, u32[]{:S(2)}) collective-permute-start(bf16[2,2,128,512]{3,2,1,0:T(8,128)(2,1)S(1)} %pad_maximum_fusion.2), channel_id=1, source_target_pairs={{0,30},{1,31},{2,28},{3,29},{4,26},{5,27},{6,24},{7,25},{8,22},{9,... | collective-permute-start | bytes 1572872 | tf_op jit(solution)/shard_map/ppermute | solution.py:228
  76.0 0.8 copy-start.4
  95.5 23.7 %copy-start.3 = (bf16[128,512]{1,0:T(8,128)(2,1)S(1)}, bf16[128,512]{1,0:T(8,128)(2,1)}, u32[]{:S(2)}) copy-start(bf16[128,512]{1,0:T(8,128)(2,1)} %get-tuple-element.26) | copy-start | bytes 393220
  95.5 23.8 %copy-start.6 = (bf16[128,512]{1,0:T(8,128)(2,1)S(1)}, bf16[128,512]{1,0:T(8,128)(2,1)}, u32[]{:S(2)}) copy-start(bf16[128,512]{1,0:T(8,128)(2,1)} %get-tuple-element.35) | copy-start | bytes 393220
  95.5 45.0 %copy-start.5 = (bf16[128,512]{1,0:T(8,128)(2,1)S(1)}, bf16[128,512]{1,0:T(8,128)(2,1)}, u32[]{:S(2)}) copy-start(bf16[128,512]{1,0:T(8,128)(2,1)} %get-tuple-element.36) | copy-start | bytes 393220
  95.5 54.2 %all-to-all-start.1 = ((bf16[32,2,128,128]{3,2,1,0:T(8,128)(2,1)}), bf16[32,2,128,128]{3,2,1,0:T(8,128)(2,1)S(1)}, u32[]{:S(2)}, u32[]{:S(2)}) async-start(bf16[32,2,128,128]{3,2,1,0:T(8,128)(2,1)} %get-tuple-element.37), calls=%async_computation.1 | async-start | bytes 4194304 | tf_op jit(solution)/shard_map/all_to_all | solution.py:258
  109.0 10.2 %collective-permute-start.6 = (bf16[128,512]{1,0:T(8,128)(2,1)}, bf16[128,512]{1,0:T(8,128)(2,1)S(1)}, u32[]{:S(2)}, u32[]{:S(2)}) collective-permute-start(bf16[128,512]{1,0:T(8,128)(2,1)} %get-tuple-element.27), channel_id=1, source_target_pairs={{0,32},{1,33},{2,34},{3,35},{4,36},{5,37},{6,38},{7,39},{8,40},{9,... | collective-permute-start | bytes 393224 | tf_op jit(solution)/shard_map/ppermute | solution.py:228
  111.4 29.1 %collective-permute-start.7 = (bf16[128,512]{1,0:T(8,128)(2,1)}, bf16[128,512]{1,0:T(8,128)(2,1)S(1)}, u32[]{:S(2)}, u32[]{:S(2)}) collective-permute-start(bf16[128,512]{1,0:T(8,128)(2,1)} %get-tuple-element.28), channel_id=1, source_target_pairs={{0,94},{1,95},{2,92},{3,93},{4,90},{5,91},{6,88},{7,89},{8,86},{9,... | collective-permute-start | bytes 393224 | tf_op jit(solution)/shard_map/ppermute | solution.py:228
  113.9 28.7 %collective-permute-start.8 = (bf16[128,512]{1,0:T(8,128)(2,1)}, bf16[128,512]{1,0:T(8,128)(2,1)S(1)}, u32[]{:S(2)}, u32[]{:S(2)}) collective-permute-start(bf16[128,512]{1,0:T(8,128)(2,1)} %get-tuple-element.29), channel_id=1, source_target_pairs={{0,126},{1,127},{2,124},{3,125},{4,122},{5,123},{6,120},{7,121},{8... | collective-permute-start | bytes 393224 | tf_op jit(solution)/shard_map/ppermute | solution.py:228
  117.3 25.3 %collective-permute-start.9 = (bf16[128,512]{1,0:T(8,128)(2,1)}, bf16[128,512]{1,0:T(8,128)(2,1)S(1)}, u32[]{:S(2)}, u32[]{:S(2)}) collective-permute-start(bf16[128,512]{1,0:T(8,128)(2,1)} %get-tuple-element.33), channel_id=1, source_target_pairs={{0,64},{1,65},{2,66},{3,67},{4,68},{5,69},{6,70},{7,71},{8,72},{9,... | collective-permute-start | bytes 393224 | tf_op jit(solution)/shard_map/ppermute | solution.py:228
  117.5 27.0 %collective-permute-start.10 = (bf16[128,512]{1,0:T(8,128)(2,1)}, bf16[128,512]{1,0:T(8,128)(2,1)S(1)}, u32[]{:S(2)}, u32[]{:S(2)}) collective-permute-start(bf16[128,512]{1,0:T(8,128)(2,1)} %get-tuple-element.34), channel_id=1, source_target_pairs={{0,96},{1,97},{2,98},{3,99},{4,100},{5,101},{6,102},{7,103},{8,104... | collective-permute-start | bytes 393224 | tf_op jit(solution)/shard_map/ppermute | solution.py:228
  119.3 26.5 %collective-permute-start.11 = (bf16[128,512]{1,0:T(8,128)(2,1)S(1)}, bf16[128,512]{1,0:T(8,128)(2,1)S(1)}, u32[]{:S(2)}, u32[]{:S(2)}) collective-permute-start(bf16[128,512]{1,0:T(8,128)(2,1)S(1)} %copy-done.6), channel_id=1, source_target_pairs={{0,30},{1,31},{2,28},{3,29},{4,26},{5,27},{6,24},{7,25},{8,22},{9,... | collective-permute-start | bytes 393224 | tf_op jit(solution)/shard_map/ppermute | solution.py:228
  140.5 9.2 %collective-permute-start.12 = (bf16[128,512]{1,0:T(8,128)(2,1)S(1)}, bf16[128,512]{1,0:T(8,128)(2,1)S(1)}, u32[]{:S(2)}, u32[]{:S(2)}) collective-permute-start(bf16[128,512]{1,0:T(8,128)(2,1)S(1)} %copy-done.5), channel_id=1, source_target_pairs={{0,62},{1,63},{2,60},{3,61},{4,58},{5,59},{6,56},{7,57},{8,54},{9,... | collective-permute-start | bytes 393224 | tf_op jit(solution)/shard_map/ppermute | solution.py:228
  149.7 1.3 copy-start.2

commit v6 on v5

--- a/solution.py
+++ b/solution.py
@@ -43,8 +43,8 @@
     kv_ref, refs = refs[0], refs[1:]
     if not first:
         sums_ref, refs = refs[0], refs[1:]
-    grad_refs, term_ref = refs[:4], refs[4]
-    q_s, do_s, kt_s, w_s, g_s, m_s, dk_s, dv_s, dq_s, stat_s = refs[5:]
+    *grad_refs, term_ref = refs[:-10]
+    q_s, do_s, kt_s, w_s, g_s, m_s, dk_s, dv_s, dq_s, stat_s = refs[-10:]
     for n in range(2):
         for layer in range(LAYERS):
             unit = units[n * LAYERS + layer]
@@ -80,7 +80,7 @@
             return scores, lax.dot_general(keys(j, 1), do[...], NT, preferred_element_type=F32)
 
         def keep(j, weights, prob_grad, top):
-            w_s[j] = weights
+            w_s[j] = weights.astype(BF16)
             g_s[j] = prob_grad
             m_s[j] = jnp.broadcast_to(top, (8, GROUP_ROWS))
             return fold(weights, jnp.sum), fold(weights * prob_grad, jnp.sum)
@@ -136,7 +136,7 @@
         dq_s[...] = jnp.zeros_like(dq_s)
 
         def backward(j, carry):
-            probs = w_s[j] * (jnp.exp2(m_s[j][0:1] - top) * inverse)
+            probs = w_s[j].astype(F32) * (jnp.exp2(m_s[j][0:1] - top) * inverse)
             score_grad = (probs * (g_s[j] - delta)).astype(BF16)
             dv_s[j] += lax.dot_general(probs.astype(BF16), do[...], NN, preferred_element_type=F32)
             dk_s[j] += lax.dot_general(score_grad, q[...], NN, preferred_element_type=F32)
@@ -153,9 +153,10 @@
     lax.fori_loop(0, 2, one_group, 0)
     for n in range(2):
         for layer in range(LAYERS):
+            grad_ref = grad_refs[2].at[layer] if first and n else grad_refs[n * LAYERS + layer]
             for g in range(GROUPS):
                 lo = layer * WIDTH + g * HEAD_DIM
-                grad_refs[n * LAYERS + layer][:, g * HEAD_DIM : (g + 1) * HEAD_DIM] = q_s[n, lo : lo + ROWS, :]
+                grad_ref[:, g * HEAD_DIM : (g + 1) * HEAD_DIM] = q_s[n, lo : lo + ROWS, :]
     for j in range(CHUNKS):
         blocks = slice(j * SPAN, (j + 1) * SPAN)
         key_grad = dk_s[j] if first else dk_s[j] * SCALE
@@ -167,17 +168,20 @@
     first = sums is None
     vmem = pl.BlockSpec(memory_space=pltpu.VMEM)
     args = [*units, kv] + ([] if first else [sums])
+    grad = jax.ShapeDtypeStruct((ROWS, WIDTH), BF16)
+    pair = jax.ShapeDtypeStruct((LAYERS, ROWS, WIDTH), BF16)
+    outs = [grad, grad, pair] if first else [grad] * 4
+    outs.append(jax.ShapeDtypeStruct((BLOCKS, 2, ROWS, HEAD_DIM), BF16))
     return pl.pallas_call(
         functools.partial(attention_kernel, first),
-        out_shape=[jax.ShapeDtypeStruct((ROWS, WIDTH), BF16)] * 4
-        + [jax.ShapeDtypeStruct((BLOCKS, 2, ROWS, HEAD_DIM), BF16)],
+        out_shape=outs,
         in_specs=[pl.BlockSpec(memory_space=pltpu.SMEM)] + [vmem] * len(args),
-        out_specs=[vmem] * 5,
+        out_specs=[vmem] * len(outs),
         scratch_shapes=[
             pltpu.VMEM((2, GROUP_ROWS, HEAD_DIM), BF16),
             pltpu.VMEM((2, GROUP_ROWS, HEAD_DIM), BF16),
             pltpu.VMEM((HEAD_DIM, BLOCKS * ROWS), BF16),
-            pltpu.VMEM((CHUNKS, KEYS, GROUP_ROWS), F32),
+            pltpu.VMEM((CHUNKS, KEYS, GROUP_ROWS), BF16),
             pltpu.VMEM((CHUNKS, KEYS, GROUP_ROWS), F32),
             pltpu.VMEM((CHUNKS, 8, GROUP_ROWS), F32),
             pltpu.VMEM((CHUNKS, KEYS, HEAD_DIM), F32),
@@ -185,7 +189,7 @@
             pltpu.VMEM((HEAD_DIM, GROUP_ROWS), F32),
             pltpu.VMEM((24, GROUP_ROWS), F32),
         ],
-        compiler_params=pltpu.CompilerParams(vmem_limit_bytes=60 * 1024 * 1024),
+        compiler_params=pltpu.CompilerParams(vmem_limit_bytes=42 * 1024 * 1024),
         cost_estimate=pl.CostEstimate(flops=12_000_000_000, bytes_accessed=8_000_000, transcendentals=4_500_000),
         name="attention_first" if first else "attention_second",
     )(blocks, *args)
@@ -197,7 +201,8 @@
             rows = slice(part * QUANT_BLOCK, (part + 1) * QUANT_BLOCK)
             for head in range(2):
                 codes = codes_ref[which, rows, head * HEAD_DIM : (head + 1) * HEAD_DIM].astype(F32)
-                values = (codes * scales_ref[which, part, head]).astype(BF16)
+                scale = scales_ref[which, head : head + 1, part : part + 1]
+                values = (codes * jnp.broadcast_to(scale, codes.shape)).astype(BF16)
                 for to in range(16):
                     out_ref[head * 16 + to, which, rows, :] = values
 
@@ -206,10 +211,10 @@
     return pl.pallas_call(
         spread_kernel,
         out_shape=jax.ShapeDtypeStruct((BLOCKS, 2, ROWS, HEAD_DIM), BF16),
-        in_specs=[pl.BlockSpec(memory_space=pltpu.SMEM), pl.BlockSpec(memory_space=pltpu.VMEM)],
+        in_specs=[pl.BlockSpec(memory_space=pltpu.VMEM)] * 2,
         out_specs=pl.BlockSpec(memory_space=pltpu.VMEM),
         name="spread_cache",
-    )(kv_scales, kv_codes)
+    )(kv_scales.transpose(0, 2, 1), kv_codes)
 
 
 CORE, FLIP, NEAR = 1, 2, 4
@@ -252,14 +257,15 @@
     near, turned, kv, across, across_core = lax.optimization_barrier((near, turned, kv, across, across_core))
     near, turned = move(near, NEAR), move(turned, FLIP)
 
-    *first, sums = attention(blocks, (own, own_core, across, across_core), kv)
-    near, turned, first[0] = lax.optimization_barrier((near, turned, first[0]))
+    d_own, d_own_core, d_across, sums = attention(blocks, (own, own_core, across, across_core), kv)
+    d_across = move(d_across, ACROSS)
     *second, term = attention(blocks, (near, turned), kv, sums)
+    d_across, term = lax.optimization_barrier((d_across, term))
     received = lax.all_to_all(term, "blk", 0, 0, tiled=True)
-    grads = {}
-    for k, grad in zip((0, CORE, ACROSS, ACROSS | CORE, NEAR, NEAR | CORE, FLIP, FLIP | CORE), first + second):
-        grads[k] = move(grad, k) if k else grad
-
+    grads = {0: d_own, CORE: move(d_own_core, CORE), ACROSS: d_across[0], ACROSS | CORE: move(d_across[1], CORE)}
+    for k, grad in zip((NEAR, NEAR | CORE, FLIP, FLIP | CORE), second):
+        grads[k] = move(grad, k)
+    grads = lax.optimization_barrier(grads)
     kv_grad = received.reshape(2, 16, 2, ROWS, HEAD_DIM).astype(F32).sum(1)
     kv_grad = kv_grad.transpose(1, 2, 0, 3).reshape(2, ROWS, 2 * HEAD_DIM)
     query_grad = jnp.zeros((ROWS, 8 * WIDTH), BF16)

time: 151 us -> 142 us (0.940)
  starting transfers between devices: 50.1 us -> 43.7 us
  Pallas kernels: 39.2 us -> 33.9 us
    pallas_call x2, Pallas kernels: 36.7 us -> 31.4 us  [attention(): pl.pallas_call(functools.partial(attention_kernel, first), out_shape=outs...]
    all_to_all x1, starting transfers between devices: 13.5 us -> 8.66 us  [shards(): received = lax.all_to_all(term, 'blk', 0, 0, tiled=True)]
    unnamed x16 -> x11, local copies, waits for them, and re-layouts: 3.58 us -> 2.19 us
  transfers between devices with their start and end apart: 15 -> 15, of which waited for: 6 -> 5; matrix products, arithmetic and copies ran while one was open for 5% -> 7% of each run, Pallas kernels for 12% -> 22%
where the time goes in v6:
time: 142 us; the launch traced here: 141 us
  waiting for transfers between devices  49.1 us (35%)
  starting transfers between devices  43.7 us (31%)
  Pallas kernels  33.9 us (24%)
  local copies, waits for them, and re-layouts  6.73 us (5%)
  other arithmetic  6.24 us (4%)
    ppermute x13, waiting for transfers between devices, move(): return lax.ppermute(x, AXES, partners(k))  49.1 us
    pallas_call x2, Pallas kernels, attention(): pl.pallas_call(functools.partial(attention_kernel, first), out_shape=outs...  31.4 us
    ppermute x13, starting transfers between devices, move(): return lax.ppermute(x, AXES, partners(k))  23.7 us
    all_to_all x1, starting transfers between devices, shards(): lax.all_to_all(spread_cache(kv_codes, kv_scales), 'blk', 0, 0, tiled=True)  11.3 us
    all_to_all x1, starting transfers between devices, shards(): received = lax.all_to_all(term, 'blk', 0, 0, tiled=True)  8.66 us
  transfers between devices with their start and end apart: 15, of which 5 were waited for; matrix products, arithmetic and copies ran while one was open for 7% of the time, Pallas kernels for 22%

profile of v6, /device:TPU:1, one launch (start us, length us, event | category | flops | bytes accessed | tf_op | source)
XLA Modules:
  0.0 140.6 jit_solution(2025209289973980116)
XLA Ops:
  0.6 2.6 %spread_cache.1 = bf16[32,2,128,128]{3,2,1,0:T(8,128)(2,1)} custom-call(f32[2,2,4]{2,1,0:T(2,128)} %bitcast.38, s32[2,128,256]{2,1,0:T(8,128)} %codes_ref.1), custom_call_target="tpu_custom_call" | custom-call | tf_op jit(solution)/shard_map/spread_cache/pallas_call | solution.py:211
  3.2 11.3 %all-to-all-start = ((bf16[32,2,128,128]{3,2,1,0:T(8,128)(2,1)}), bf16[32,2,128,128]{3,2,1,0:T(8,128)(2,1)S(1)}, u32[]{:S(2)}, u32[]{:S(2)}) async-start(bf16[32,2,128,128]{3,2,1,0:T(8,128)(2,1)} %spread_cache.1), calls=%async_computation | async-start | bytes 4194304 | tf_op jit(solution)/shard_map/all_to_all | solution.py:243
  14.6 2.2 %constant_dynamic-slice_fusion = (bf16[1,128,512]{2,1,0:T(8,128)(2,1)S(1)}, bf16[1,128,512]{2,1,0:T(8,128)(2,1)}, bf16[1,128,512]{2,1,0:T(8,128)(2,1)S(1)}, bf16...) fusion(bf16[1,128,4096]{2,1,0:T(8,128)(2,1)S(1)} %copy-done.1, ...), kind=kLoop, calls=%fused_computation.22 | loop fusion | bytes 4194336 | tf_op jit(solution)/shard_map/dynamic_slice | solution.py:248
  16.9 0.8 pad_maximum_fusion
  17.7 1.0 collective-permute-start.1
  18.7 0.7 pad_maximum_fusion.5
  19.4 5.4 %collective-permute-start.2 = (bf16[2,128,512]{2,1,0:T(8,128)(2,1)}, bf16[2,128,512]{2,1,0:T(8,128)(2,1)S(1)}, u32[]{:S(2)}, u32[]{:S(2)}) collective-permute-start(bf16[2,128,512]{2,1,0:T(8,128)(2,1)} %pad_maximum_fusion.5), channel_id=1, source_target_pairs={{0,94},{1,95},{2,92},{3,93},{4,90},{5,91},{6,88},{7,89},{8,86},{9,... | collective-permute-start | bytes 786440 | tf_op jit(solution)/shard_map/ppermute | solution.py:233
  24.8 0.7 pad_maximum_fusion.6
  25.5 0.5 collective-permute-start.3
  26.0 0.7 pad_maximum_fusion.4
  27.0 1.0 maximum_bitcast_fusion.3
  28.1 1.1 fusion
  29.2 0.8 pad_maximum_fusion.2
  30.0 0.8 pad_maximum_fusion.1
  30.9 18.2 %collective-permute-done.2.refs_2_ = bf16[2,128,512]{2,1,0:T(8,128)(2,1)S(1)} collective-permute-done((bf16[2,128,512]{2,1,0:T(8,128)(2,1)}, bf16[2,128,512]{2,1,0:T(8,128)(2,1)S(1)}, u32[]{:S(2)}, u32[]{:S(2)}) %collective-permute-start.2) | collective-permute-done | bytes 262176 | tf_op jit(solution)/shard_map/ppermute | solution.py:233
  49.1 6.1 %collective-permute-done.3.refs_3_ = bf16[2,128,512]{2,1,0:T(8,128)(2,1)S(1)} collective-permute-done((bf16[2,128,512]{2,1,0:T(8,128)(2,1)}, bf16[2,128,512]{2,1,0:T(8,128)(2,1)S(1)}, u32[]{:S(2)}, u32[]{:S(2)}) %collective-permute-start.3) | collective-permute-done | bytes 262176 | tf_op jit(solution)/shard_map/ppermute | solution.py:233
  55.3 0.7 collective-permute-start.5
  56.0 15.7 %attention_first.1 = (bf16[128,512]{1,0:T(8,128)(2,1)S(1)}, bf16[128,512]{1,0:T(8,128)(2,1)S(1)}, bf16[2,128,512]{2,1,0:T(8,128)(2,1)S(1)}, bf16[32,2,128,128]{3,2,1,0:T(8,128)(2,1)S(1)}) custom-call(s32[2]{0:T(128)S(1)} %pad_add_fusion.blocks_ref, bf16[2,128,512]{2,1,0:T(8,128)(2,1)S(1)} %pad_maximum_fusion.3.refs_0_, ...), custom_call_target="tpu_custom_call" | custom-call | flops 12000000000 | bytes 8000000 | tf_op jit(solution)/shard_map/attention_first/pallas_call | solution.py:175
  71.7 5.3 %collective-permute-start.11 = (bf16[2,128,512]{2,1,0:T(8,128)(2,1)S(1)}, bf16[2,128,512]{2,1,0:T(8,128)(2,1)S(1)}, u32[]{:S(2)}, u32[]{:S(2)}) collective-permute-start(bf16[2,128,512]{2,1,0:T(8,128)(2,1)S(1)} %get-tuple-element.38), channel_id=1, source_target_pairs={{0,94},{1,95},{2,92},{3,93},{4,90},{5,91},{6,88},{7,89},{8,86},{9,... | collective-permute-start | bytes 786440 | tf_op jit(solution)/shard_map/ppermute | solution.py:233
  77.0 0.8 collective-permute-start.4
  77.7 15.7 %attention_second.1 = (bf16[128,512]{1,0:T(8,128)(2,1)S(1)}, bf16[128,512]{1,0:T(8,128)(2,1)S(1)}, bf16[128,512]{1,0:T(8,128)(2,1)S(1)}, bf16[128,512]{1,0:T(8,128)(2,1)S(1)}, bf16[32,2,128,128]{3,2,1,0:T(8,128)(2,1)S(1)}) custom-call(s32[2]{0:T(128)S(1)} %pad_add_fusion.blocks_ref, bf16[2,2,128,512]{3,2,1,0:T(8,128)(2,1)S(1)} %collective-permute-done.5.refs_0_, ...), custom_call_target="tpu_custom_call" | custom-call | flops 12000000000 | bytes 8000000 | tf_op jit(solution)/shard_map/attention_second/pallas_call | solution.py:175
  93.5 1.3 copy-done
  94.8 8.7 %all-to-all-start.1 = ((bf16[32,2,128,128]{3,2,1,0:T(8,128)(2,1)}), bf16[32,2,128,128]{3,2,1,0:T(8,128)(2,1)S(1)}, u32[]{:S(2)}, u32[]{:S(2)}) async-start(bf16[32,2,128,128]{3,2,1,0:T(8,128)(2,1)} %copy-done), calls=%async_computation.1 | async-start | bytes 4194304 | tf_op jit(solution)/shard_map/all_to_all | solution.py:264
  103.5 3.1 %collective-permute-start.12 = (bf16[128,512]{1,0:T(8,128)(2,1)S(1)}, bf16[128,512]{1,0:T(8,128)(2,1)S(1)}, u32[]{:S(2)}, u32[]{:S(2)}) collective-permute-start(bf16[128,512]{1,0:T(8,128)(2,1)S(1)} %get-tuple-element.70), channel_id=1, source_target_pairs={{0,32},{1,33},{2,34},{3,35},{4,36},{5,37},{6,38},{7,39},{8,40},{9,... | collective-permute-start | bytes 393224 | tf_op jit(solution)/shard_map/ppermute | solution.py:233
  106.9 4.9 %collective-permute-start.7 = (bf16[128,512]{1,0:T(8,128)(2,1)S(1)}, bf16[128,512]{1,0:T(8,128)(2,1)S(1)}, u32[]{:S(2)}, u32[]{:S(2)}) collective-permute-start(bf16[128,512]{1,0:T(8,128)(2,1)S(1)} %get-tuple-element.34), channel_id=1, source_target_pairs={{0,30},{1,31},{2,28},{3,29},{4,26},{5,27},{6,24},{7,25},{8,22},{9,... | collective-permute-start | bytes 393224 | tf_op jit(solution)/shard_map/ppermute | solution.py:233
  111.8 0.5 collective-permute-start.8
  112.3 1.1 collective-permute-start.9
  113.4 13.0 %collective-permute-done.10 = bf16[128,512]{1,0:T(8,128)(2,1)S(1)} collective-permute-done((bf16[128,512]{1,0:T(8,128)(2,1)S(1)}, bf16[128,512]{1,0:T(8,128)(2,1)S(1)}, u32[]{:S(2)}, u32[]{:S(2)}) %collective-permute-start.10) | collective-permute-done | bytes 131104 | tf_op jit(solution)/shard_map/ppermute | solution.py:233
  126.4 6.5 %collective-permute-done.7 = bf16[128,512]{1,0:T(8,128)(2,1)S(1)} collective-permute-done((bf16[128,512]{1,0:T(8,128)(2,1)S(1)}, bf16[128,512]{1,0:T(8,128)(2,1)S(1)}, u32[]{:S(2)}, u32[]{:S(2)}) %collective-permute-start.7) | collective-permute-done | bytes 131104 | tf_op jit(solution)/shard_map/ppermute | solution.py:233
  133.0 5.1 %collective-permute-done.8 = bf16[128,512]{1,0:T(8,128)(2,1)S(1)} collective-permute-done((bf16[128,512]{1,0:T(8,128)(2,1)S(1)}, bf16[128,512]{1,0:T(8,128)(2,1)S(1)}, u32[]{:S(2)}, u32[]{:S(2)}) %collective-permute-start.8) | collective-permute-done | bytes 131104 | tf_op jit(solution)/shard_map/ppermute | solution.py:233
  138.2 0.9 bitcast_dynamic-update-slice_fusion.6
  139.8 0.8 copy.7
  (38 shorter events, 1.5 us)
Async XLA Ops:
  3.2 11.4 %copy-start.1 = (bf16[1,128,4096]{2,1,0:T(8,128)(2,1)S(1)}, bf16[1,128,4096]{2,1,0:T(8,128)(2,1)}, u32[]{:S(2)}) copy-start(bf16[1,128,4096]{2,1,0:T(8,128)(2,1)} %param.5) | copy-start | bytes 3145732
  3.2 52.1 %all-to-all-start = ((bf16[32,2,128,128]{3,2,1,0:T(8,128)(2,1)}), bf16[32,2,128,128]{3,2,1,0:T(8,128)(2,1)S(1)}, u32[]{:S(2)}, u32[]{:S(2)}) async-start(bf16[32,2,128,128]{3,2,1,0:T(8,128)(2,1)} %spread_cache.1), calls=%async_computation | async-start | bytes 4194304 | tf_op jit(solution)/shard_map/all_to_all | solution.py:243
  16.8 11.2 %copy-start.3 = (bf16[1,128,512]{2,1,0:T(8,128)(2,1)S(1)}, bf16[1,128,512]{2,1,0:T(8,128)(2,1)}, u32[]{:S(2)}) copy-start(bf16[1,128,512]{2,1,0:T(8,128)(2,1)} %get-tuple-element.73) | copy-start | bytes 393220
  17.7 10.4 %collective-permute-start.1 = (bf16[2,2,128,512]{3,2,1,0:T(8,128)(2,1)}, bf16[2,2,128,512]{3,2,1,0:T(8,128)(2,1)}, u32[]{:S(2)}, u32[]{:S(2)}) collective-permute-start(bf16[2,2,128,512]{3,2,1,0:T(8,128)(2,1)} %pad_maximum_fusion), channel_id=1, source_target_pairs={{0,32},{1,33},{2,34},{3,35},{4,36},{5,37},{6,38},{7,39},{8,40},{9,... | collective-permute-start | bytes 1572872 | tf_op jit(solution)/shard_map/ppermute | solution.py:233
  19.4 29.7 %collective-permute-start.2 = (bf16[2,128,512]{2,1,0:T(8,128)(2,1)}, bf16[2,128,512]{2,1,0:T(8,128)(2,1)S(1)}, u32[]{:S(2)}, u32[]{:S(2)}) collective-permute-start(bf16[2,128,512]{2,1,0:T(8,128)(2,1)} %pad_maximum_fusion.5), channel_id=1, source_target_pairs={{0,94},{1,95},{2,92},{3,93},{4,90},{5,91},{6,88},{7,89},{8,86},{9,... | collective-permute-start | bytes 786440 | tf_op jit(solution)/shard_map/ppermute | solution.py:233
  25.5 29.7 %collective-permute-start.3 = (bf16[2,128,512]{2,1,0:T(8,128)(2,1)}, bf16[2,128,512]{2,1,0:T(8,128)(2,1)S(1)}, u32[]{:S(2)}, u32[]{:S(2)}) collective-permute-start(bf16[2,128,512]{2,1,0:T(8,128)(2,1)} %pad_maximum_fusion.6), channel_id=1, source_target_pairs={{0,126},{1,127},{2,124},{3,125},{4,122},{5,123},{6,120},{7,121},{8... | collective-permute-start | bytes 786440 | tf_op jit(solution)/shard_map/ppermute | solution.py:233
  26.7 29.3 %collective-permute-start = (bf16[2,128,512]{2,1,0:T(8,128)(2,1)}, bf16[2,128,512]{2,1,0:T(8,128)(2,1)S(1)}, u32[]{:S(2)}, u32[]{:S(2)}) collective-permute-start(bf16[2,128,512]{2,1,0:T(8,128)(2,1)} %pad_maximum_fusion.4), channel_id=1, source_target_pairs={{0,32},{1,33},{2,34},{3,35},{4,36},{5,37},{6,38},{7,39},{8,40},{9,... | collective-permute-start | bytes 786440 | tf_op jit(solution)/shard_map/ppermute | solution.py:233
  55.3 22.5 %collective-permute-start.5 = (bf16[2,2,128,512]{3,2,1,0:T(8,128)(2,1)}, bf16[2,2,128,512]{3,2,1,0:T(8,128)(2,1)S(1)}, u32[]{:S(2)}, u32[]{:S(2)}) collective-permute-start(bf16[2,2,128,512]{3,2,1,0:T(8,128)(2,1)} %pad_maximum_fusion.1), channel_id=1, source_target_pairs={{0,64},{1,65},{2,66},{3,67},{4,68},{5,69},{6,70},{7,71},{8,72},{9,... | collective-permute-start | bytes 1572872 | tf_op jit(solution)/shard_map/ppermute | solution.py:233
  56.0 21.7 %collective-permute-start.6 = (bf16[2,2,128,512]{3,2,1,0:T(8,128)(2,1)}, bf16[2,2,128,512]{3,2,1,0:T(8,128)(2,1)S(1)}, u32[]{:S(2)}, u32[]{:S(2)}) collective-permute-start(bf16[2,2,128,512]{3,2,1,0:T(8,128)(2,1)} %pad_maximum_fusion.2), channel_id=1, source_target_pairs={{0,30},{1,31},{2,28},{3,29},{4,26},{5,27},{6,24},{7,25},{8,22},{9,... | collective-permute-start | bytes 1572872 | tf_op jit(solution)/shard_map/ppermute | solution.py:233
  71.7 23.1 %collective-permute-start.11 = (bf16[2,128,512]{2,1,0:T(8,128)(2,1)S(1)}, bf16[2,128,512]{2,1,0:T(8,128)(2,1)S(1)}, u32[]{:S(2)}, u32[]{:S(2)}) collective-permute-start(bf16[2,128,512]{2,1,0:T(8,128)(2,1)S(1)} %get-tuple-element.38), channel_id=1, source_target_pairs={{0,94},{1,95},{2,92},{3,93},{4,90},{5,91},{6,88},{7,89},{8,86},{9,... | collective-permute-start | bytes 786440 | tf_op jit(solution)/shard_map/ppermute | solution.py:233
  77.0 35.3 %collective-permute-start.4 = (bf16[128,512]{1,0:T(8,128)(2,1)S(1)}, bf16[128,512]{1,0:T(8,128)(2,1)S(1)}, u32[]{:S(2)}, u32[]{:S(2)}) collective-permute-start(bf16[128,512]{1,0:T(8,128)(2,1)S(1)} %get-tuple-element.30), channel_id=1, source_target_pairs={{0,32},{1,33},{2,34},{3,35},{4,36},{5,37},{6,38},{7,39},{8,40},{9,... | collective-permute-start | bytes 393224 | tf_op jit(solution)/shard_map/ppermute | solution.py:233
  93.4 1.3 copy-start
  94.8 44.5 %all-to-all-start.1 = ((bf16[32,2,128,128]{3,2,1,0:T(8,128)(2,1)}), bf16[32,2,128,128]{3,2,1,0:T(8,128)(2,1)S(1)}, u32[]{:S(2)}, u32[]{:S(2)}) async-start(bf16[32,2,128,128]{3,2,1,0:T(8,128)(2,1)} %copy-done), calls=%async_computation.1 | async-start | bytes 4194304 | tf_op jit(solution)/shard_map/all_to_all | solution.py:264
  103.5 9.9 %collective-permute-start.12 = (bf16[128,512]{1,0:T(8,128)(2,1)S(1)}, bf16[128,512]{1,0:T(8,128)(2,1)S(1)}, u32[]{:S(2)}, u32[]{:S(2)}) collective-permute-start(bf16[128,512]{1,0:T(8,128)(2,1)S(1)} %get-tuple-element.70), channel_id=1, source_target_pairs={{0,32},{1,33},{2,34},{3,35},{4,36},{5,37},{6,38},{7,39},{8,40},{9,... | collective-permute-start | bytes 393224 | tf_op jit(solution)/shard_map/ppermute | solution.py:233
  106.6 19.9 %collective-permute-start.10 = (bf16[128,512]{1,0:T(8,128)(2,1)S(1)}, bf16[128,512]{1,0:T(8,128)(2,1)S(1)}, u32[]{:S(2)}, u32[]{:S(2)}) collective-permute-start(bf16[128,512]{1,0:T(8,128)(2,1)S(1)} %get-tuple-element.37), channel_id=1, source_target_pairs={{0,96},{1,97},{2,98},{3,99},{4,100},{5,101},{6,102},{7,103},{8,104... | collective-permute-start | bytes 393224 | tf_op jit(solution)/shard_map/ppermute | solution.py:233
  106.9 26.1 %collective-permute-start.7 = (bf16[128,512]{1,0:T(8,128)(2,1)S(1)}, bf16[128,512]{1,0:T(8,128)(2,1)S(1)}, u32[]{:S(2)}, u32[]{:S(2)}) collective-permute-start(bf16[128,512]{1,0:T(8,128)(2,1)S(1)} %get-tuple-element.34), channel_id=1, source_target_pairs={{0,30},{1,31},{2,28},{3,29},{4,26},{5,27},{6,24},{7,25},{8,22},{9,... | collective-permute-start | bytes 393224 | tf_op jit(solution)/shard_map/ppermute | solution.py:233
  111.8 26.3 %collective-permute-start.8 = (bf16[128,512]{1,0:T(8,128)(2,1)S(1)}, bf16[128,512]{1,0:T(8,128)(2,1)S(1)}, u32[]{:S(2)}, u32[]{:S(2)}) collective-permute-start(bf16[128,512]{1,0:T(8,128)(2,1)S(1)} %get-tuple-element.35), channel_id=1, source_target_pairs={{0,62},{1,63},{2,60},{3,61},{4,58},{5,59},{6,56},{7,57},{8,54},{9,... | collective-permute-start | bytes 393224 | tf_op jit(solution)/shard_map/ppermute | solution.py:233
  112.3 25.8 %copy-start.4 = (bf16[128,512]{1,0:T(8,128)(2,1)}, bf16[128,512]{1,0:T(8,128)(2,1)S(1)}, u32[]{:S(2)}) copy-start(bf16[128,512]{1,0:T(8,128)(2,1)S(1)} %collective-permute-done.4) | copy-start | bytes 393220
  112.3 25.8 %collective-permute-start.9 = (bf16[128,512]{1,0:T(8,128)(2,1)S(1)}, bf16[128,512]{1,0:T(8,128)(2,1)S(1)}, u32[]{:S(2)}, u32[]{:S(2)}) collective-permute-start(bf16[128,512]{1,0:T(8,128)(2,1)S(1)} %get-tuple-element.36), channel_id=1, source_target_pairs={{0,64},{1,65},{2,66},{3,67},{4,68},{5,69},{6,70},{7,71},{8,72},{9,... | collective-permute-start | bytes 393224 | tf_op jit(solution)/shard_map/ppermute | solution.py:233
  139.3 1.3 copy-start.2

commit v7 on v6

--- a/solution.py
+++ b/solution.py
@@ -24,7 +24,7 @@
 
 LAYERS = 2
 KEYS = 256
-UNROLL = 4
+UNROLL = (6, 3, 1)
 SPAN = KEYS // ROWS
 GROUP_ROWS = LAYERS * WIDTH
 CHUNKS = BLOCKS // SPAN
@@ -89,13 +89,17 @@
             return jnp.max(fold(scores, jnp.max), axis=0, keepdims=True) * EXP2_SCALE
 
         def unrolled(count, step, carry):
-            def several(t, carry):
-                for n in range(UNROLL):
-                    carry = step(t * UNROLL + n, carry)
+            def several(size, start, t, carry):
+                for n in range(size):
+                    carry = step(start + t * size + n, carry)
                 return carry
 
-            carry = lax.fori_loop(0, count // UNROLL, several, carry)
-            return lax.fori_loop(count // UNROLL * UNROLL, count, step, carry)
+            start = 0
+            for size in UNROLL:
+                times = (count - start) // size
+                carry = lax.fori_loop(0, times, functools.partial(several, size, start), carry)
+                start = start + times * size
+            return carry
 
         scores, prob_grad = products(last)
         key_at = lax.broadcasted_iota(jnp.int32, (KEYS, GROUP_ROWS), 0)

time: 142 us -> 143 us (level); the launches traced: 141 us -> 144 us
  waiting for transfers between devices: 49.1 us -> 52.9 us
    ppermute x13, waiting for transfers between devices: 49.1 us -> 52.9 us  [move(): return lax.ppermute(x, AXES, partners(k))]
    all_to_all x1, starting transfers between devices: 8.66 us -> 12.1 us  [shards(): received = lax.all_to_all(term, 'blk', 0, 0, tiled=True)]
    ppermute x13, starting transfers between devices: 23.7 us -> 20.8 us  [move(): return lax.ppermute(x, AXES, partners(k))]
  transfers between devices with their start and end apart: 15 -> 15, of which waited for: 5 -> 5; matrix products, arithmetic and copies ran while one was open for 7% -> 7% of each run, Pallas kernels for 22% -> 21%
where the time goes in v7:
time: 143 us; the launch traced here: 144 us
  waiting for transfers between devices  52.9 us (37%)
  starting transfers between devices  44.2 us (31%)
  Pallas kernels  33.1 us (23%)
  local copies, waits for them, and re-layouts  6.73 us (5%)
  other arithmetic  6.24 us (4%)
    ppermute x13, waiting for transfers between devices, move(): return lax.ppermute(x, AXES, partners(k))  52.9 us
    pallas_call x2, Pallas kernels, attention(): pl.pallas_call(functools.partial(attention_kernel, first), out_shape=outs...  30.5 us
    ppermute x13, starting transfers between devices, move(): return lax.ppermute(x, AXES, partners(k))  20.8 us
    all_to_all x1, starting transfers between devices, shards(): received = lax.all_to_all(term, 'blk', 0, 0, tiled=True)  12.1 us
    all_to_all x1, starting transfers between devices, shards(): lax.all_to_all(spread_cache(kv_codes, kv_scales), 'blk', 0, 0, tiled=True)  11.3 us
  transfers between devices with their start and end apart: 15, of which 5 were waited for; matrix products, arithmetic and copies ran while one was open for 7% of the time, Pallas kernels for 21%

profile of v7, /device:TPU:1, one launch (start us, length us, event | category | flops | bytes accessed | tf_op | source)
XLA Modules:
  0.0 144.1 jit_solution(5705129486423552595)
XLA Ops:
  0.6 2.6 %spread_cache.1 = bf16[32,2,128,128]{3,2,1,0:T(8,128)(2,1)} custom-call(f32[2,2,4]{2,1,0:T(2,128)} %bitcast.38, s32[2,128,256]{2,1,0:T(8,128)} %codes_ref.1), custom_call_target="tpu_custom_call" | custom-call | tf_op jit(solution)/shard_map/spread_cache/pallas_call | solution.py:215
  3.2 11.3 %all-to-all-start = ((bf16[32,2,128,128]{3,2,1,0:T(8,128)(2,1)}), bf16[32,2,128,128]{3,2,1,0:T(8,128)(2,1)S(1)}, u32[]{:S(2)}, u32[]{:S(2)}) async-start(bf16[32,2,128,128]{3,2,1,0:T(8,128)(2,1)} %spread_cache.1), calls=%async_computation | async-start | bytes 4194304 | tf_op jit(solution)/shard_map/all_to_all | solution.py:247
  14.6 2.2 %constant_dynamic-slice_fusion = (bf16[1,128,512]{2,1,0:T(8,128)(2,1)S(1)}, bf16[1,128,512]{2,1,0:T(8,128)(2,1)}, bf16[1,128,512]{2,1,0:T(8,128)(2,1)S(1)}, bf16...) fusion(bf16[1,128,4096]{2,1,0:T(8,128)(2,1)S(1)} %copy-done.1, ...), kind=kLoop, calls=%fused_computation.22 | loop fusion | bytes 4194336 | tf_op jit(solution)/shard_map/dynamic_slice | solution.py:252
  16.9 0.8 pad_maximum_fusion
  17.7 1.0 collective-permute-start.1
  18.7 0.7 pad_maximum_fusion.5
  19.4 5.4 %collective-permute-start.2 = (bf16[2,128,512]{2,1,0:T(8,128)(2,1)}, bf16[2,128,512]{2,1,0:T(8,128)(2,1)S(1)}, u32[]{:S(2)}, u32[]{:S(2)}) collective-permute-start(bf16[2,128,512]{2,1,0:T(8,128)(2,1)} %pad_maximum_fusion.5), channel_id=1, source_target_pairs={{0,94},{1,95},{2,92},{3,93},{4,90},{5,91},{6,88},{7,89},{8,86},{9,... | collective-permute-start | bytes 786440 | tf_op jit(solution)/shard_map/ppermute | solution.py:237
  24.8 0.7 pad_maximum_fusion.6
  25.5 0.5 collective-permute-start.3
  26.0 0.7 pad_maximum_fusion.4
  27.0 1.0 maximum_bitcast_fusion.3
  28.1 1.1 fusion
  29.2 0.8 pad_maximum_fusion.2
  30.0 0.8 pad_maximum_fusion.1
  30.9 18.2 %collective-permute-done.2.refs_2_ = bf16[2,128,512]{2,1,0:T(8,128)(2,1)S(1)} collective-permute-done((bf16[2,128,512]{2,1,0:T(8,128)(2,1)}, bf16[2,128,512]{2,1,0:T(8,128)(2,1)S(1)}, u32[]{:S(2)}, u32[]{:S(2)}) %collective-permute-start.2) | collective-permute-done | bytes 262176 | tf_op jit(solution)/shard_map/ppermute | solution.py:237
  49.1 6.1 %collective-permute-done.3.refs_3_ = bf16[2,128,512]{2,1,0:T(8,128)(2,1)S(1)} collective-permute-done((bf16[2,128,512]{2,1,0:T(8,128)(2,1)}, bf16[2,128,512]{2,1,0:T(8,128)(2,1)S(1)}, u32[]{:S(2)}, u32[]{:S(2)}) %collective-permute-start.3) | collective-permute-done | bytes 262176 | tf_op jit(solution)/shard_map/ppermute | solution.py:237
  55.3 0.7 collective-permute-start.5
  56.0 15.2 %attention_first.1 = (bf16[128,512]{1,0:T(8,128)(2,1)S(1)}, bf16[128,512]{1,0:T(8,128)(2,1)S(1)}, bf16[2,128,512]{2,1,0:T(8,128)(2,1)S(1)}, bf16[32,2,128,128]{3,2,1,0:T(8,128)(2,1)S(1)}) custom-call(s32[2]{0:T(128)S(1)} %pad_add_fusion.blocks_ref, bf16[2,128,512]{2,1,0:T(8,128)(2,1)S(1)} %pad_maximum_fusion.3.refs_0_, ...), custom_call_target="tpu_custom_call" | custom-call | flops 12000000000 | bytes 8000000 | tf_op jit(solution)/shard_map/attention_first/pallas_call | solution.py:179
  71.3 5.3 %collective-permute-start.11 = (bf16[2,128,512]{2,1,0:T(8,128)(2,1)S(1)}, bf16[2,128,512]{2,1,0:T(8,128)(2,1)S(1)}, u32[]{:S(2)}, u32[]{:S(2)}) collective-permute-start(bf16[2,128,512]{2,1,0:T(8,128)(2,1)S(1)} %get-tuple-element.38), channel_id=1, source_target_pairs={{0,94},{1,95},{2,92},{3,93},{4,90},{5,91},{6,88},{7,89},{8,86},{9,... | collective-permute-start | bytes 786440 | tf_op jit(solution)/shard_map/ppermute | solution.py:237
  76.6 0.8 collective-permute-start.4
  77.3 15.3 %attention_second.1 = (bf16[128,512]{1,0:T(8,128)(2,1)S(1)}, bf16[128,512]{1,0:T(8,128)(2,1)S(1)}, bf16[128,512]{1,0:T(8,128)(2,1)S(1)}, bf16[128,512]{1,0:T(8,128)(2,1)S(1)}, bf16[32,2,128,128]{3,2,1,0:T(8,128)(2,1)S(1)}) custom-call(s32[2]{0:T(128)S(1)} %pad_add_fusion.blocks_ref, bf16[2,2,128,512]{3,2,1,0:T(8,128)(2,1)S(1)} %collective-permute-done.5.refs_0_, ...), custom_call_target="tpu_custom_call" | custom-call | flops 12000000000 | bytes 8000000 | tf_op jit(solution)/shard_map/attention_second/pallas_call | solution.py:179
  92.6 1.3 copy-done
  94.0 12.1 %all-to-all-start.1 = ((bf16[32,2,128,128]{3,2,1,0:T(8,128)(2,1)}), bf16[32,2,128,128]{3,2,1,0:T(8,128)(2,1)S(1)}, u32[]{:S(2)}, u32[]{:S(2)}) async-start(bf16[32,2,128,128]{3,2,1,0:T(8,128)(2,1)} %copy-done), calls=%async_computation.1 | async-start | bytes 4194304 | tf_op jit(solution)/shard_map/all_to_all | solution.py:268
  106.3 4.7 %collective-permute-start.7 = (bf16[128,512]{1,0:T(8,128)(2,1)S(1)}, bf16[128,512]{1,0:T(8,128)(2,1)S(1)}, u32[]{:S(2)}, u32[]{:S(2)}) collective-permute-start(bf16[128,512]{1,0:T(8,128)(2,1)S(1)} %get-tuple-element.34), channel_id=1, source_target_pairs={{0,30},{1,31},{2,28},{3,29},{4,26},{5,27},{6,24},{7,25},{8,22},{9,... | collective-permute-start | bytes 393224 | tf_op jit(solution)/shard_map/ppermute | solution.py:237
  111.0 0.6 collective-permute-start.8
  111.7 1.4 %collective-permute-start.9 = (bf16[128,512]{1,0:T(8,128)(2,1)S(1)}, bf16[128,512]{1,0:T(8,128)(2,1)S(1)}, u32[]{:S(2)}, u32[]{:S(2)}) collective-permute-start(bf16[128,512]{1,0:T(8,128)(2,1)S(1)} %get-tuple-element.36), channel_id=1, source_target_pairs={{0,64},{1,65},{2,66},{3,67},{4,68},{5,69},{6,70},{7,71},{8,72},{9,... | collective-permute-start | bytes 393224 | tf_op jit(solution)/shard_map/ppermute | solution.py:237
  113.1 12.2 %collective-permute-done.10 = bf16[128,512]{1,0:T(8,128)(2,1)S(1)} collective-permute-done((bf16[128,512]{1,0:T(8,128)(2,1)S(1)}, bf16[128,512]{1,0:T(8,128)(2,1)S(1)}, u32[]{:S(2)}, u32[]{:S(2)}) %collective-permute-start.10) | collective-permute-done | bytes 131104 | tf_op jit(solution)/shard_map/ppermute | solution.py:237
  125.3 12.8 %collective-permute-done.7 = bf16[128,512]{1,0:T(8,128)(2,1)S(1)} collective-permute-done((bf16[128,512]{1,0:T(8,128)(2,1)S(1)}, bf16[128,512]{1,0:T(8,128)(2,1)S(1)}, u32[]{:S(2)}, u32[]{:S(2)}) %collective-permute-start.7) | collective-permute-done | bytes 131104 | tf_op jit(solution)/shard_map/ppermute | solution.py:237
  138.1 3.5 %collective-permute-done.8 = bf16[128,512]{1,0:T(8,128)(2,1)S(1)} collective-permute-done((bf16[128,512]{1,0:T(8,128)(2,1)S(1)}, bf16[128,512]{1,0:T(8,128)(2,1)S(1)}, u32[]{:S(2)}, u32[]{:S(2)}) %collective-permute-start.8) | collective-permute-done | bytes 131104 | tf_op jit(solution)/shard_map/ppermute | solution.py:237
  141.7 0.9 bitcast_dynamic-update-slice_fusion.6
  142.8 0.3 convert_reduce_fusion
  143.3 0.8 copy.7
  (38 shorter events, 1.0 us)
Async XLA Ops:
  3.2 11.4 %copy-start.1 = (bf16[1,128,4096]{2,1,0:T(8,128)(2,1)S(1)}, bf16[1,128,4096]{2,1,0:T(8,128)(2,1)}, u32[]{:S(2)}) copy-start(bf16[1,128,4096]{2,1,0:T(8,128)(2,1)} %param.5) | copy-start | bytes 3145732
  3.2 52.1 %all-to-all-start = ((bf16[32,2,128,128]{3,2,1,0:T(8,128)(2,1)}), bf16[32,2,128,128]{3,2,1,0:T(8,128)(2,1)S(1)}, u32[]{:S(2)}, u32[]{:S(2)}) async-start(bf16[32,2,128,128]{3,2,1,0:T(8,128)(2,1)} %spread_cache.1), calls=%async_computation | async-start | bytes 4194304 | tf_op jit(solution)/shard_map/all_to_all | solution.py:247
  16.8 11.2 %copy-start.3 = (bf16[1,128,512]{2,1,0:T(8,128)(2,1)S(1)}, bf16[1,128,512]{2,1,0:T(8,128)(2,1)}, u32[]{:S(2)}) copy-start(bf16[1,128,512]{2,1,0:T(8,128)(2,1)} %get-tuple-element.73) | copy-start | bytes 393220
  17.7 10.4 %collective-permute-start.1 = (bf16[2,2,128,512]{3,2,1,0:T(8,128)(2,1)}, bf16[2,2,128,512]{3,2,1,0:T(8,128)(2,1)}, u32[]{:S(2)}, u32[]{:S(2)}) collective-permute-start(bf16[2,2,128,512]{3,2,1,0:T(8,128)(2,1)} %pad_maximum_fusion), channel_id=1, source_target_pairs={{0,32},{1,33},{2,34},{3,35},{4,36},{5,37},{6,38},{7,39},{8,40},{9,... | collective-permute-start | bytes 1572872 | tf_op jit(solution)/shard_map/ppermute | solution.py:237
  19.4 29.7 %collective-permute-start.2 = (bf16[2,128,512]{2,1,0:T(8,128)(2,1)}, bf16[2,128,512]{2,1,0:T(8,128)(2,1)S(1)}, u32[]{:S(2)}, u32[]{:S(2)}) collective-permute-start(bf16[2,128,512]{2,1,0:T(8,128)(2,1)} %pad_maximum_fusion.5), channel_id=1, source_target_pairs={{0,94},{1,95},{2,92},{3,93},{4,90},{5,91},{6,88},{7,89},{8,86},{9,... | collective-permute-start | bytes 786440 | tf_op jit(solution)/shard_map/ppermute | solution.py:237
  25.5 29.7 %collective-permute-start.3 = (bf16[2,128,512]{2,1,0:T(8,128)(2,1)}, bf16[2,128,512]{2,1,0:T(8,128)(2,1)S(1)}, u32[]{:S(2)}, u32[]{:S(2)}) collective-permute-start(bf16[2,128,512]{2,1,0:T(8,128)(2,1)} %pad_maximum_fusion.6), channel_id=1, source_target_pairs={{0,126},{1,127},{2,124},{3,125},{4,122},{5,123},{6,120},{7,121},{8... | collective-permute-start | bytes 786440 | tf_op jit(solution)/shard_map/ppermute | solution.py:237
  26.7 29.3 %collective-permute-start = (bf16[2,128,512]{2,1,0:T(8,128)(2,1)}, bf16[2,128,512]{2,1,0:T(8,128)(2,1)S(1)}, u32[]{:S(2)}, u32[]{:S(2)}) collective-permute-start(bf16[2,128,512]{2,1,0:T(8,128)(2,1)} %pad_maximum_fusion.4), channel_id=1, source_target_pairs={{0,32},{1,33},{2,34},{3,35},{4,36},{5,37},{6,38},{7,39},{8,40},{9,... | collective-permute-start | bytes 786440 | tf_op jit(solution)/shard_map/ppermute | solution.py:237
  55.3 22.1 %collective-permute-start.5 = (bf16[2,2,128,512]{3,2,1,0:T(8,128)(2,1)}, bf16[2,2,128,512]{3,2,1,0:T(8,128)(2,1)S(1)}, u32[]{:S(2)}, u32[]{:S(2)}) collective-permute-start(bf16[2,2,128,512]{3,2,1,0:T(8,128)(2,1)} %pad_maximum_fusion.1), channel_id=1, source_target_pairs={{0,64},{1,65},{2,66},{3,67},{4,68},{5,69},{6,70},{7,71},{8,72},{9,... | collective-permute-start | bytes 1572872 | tf_op jit(solution)/shard_map/ppermute | solution.py:237
  56.0 21.3 %collective-permute-start.6 = (bf16[2,2,128,512]{3,2,1,0:T(8,128)(2,1)}, bf16[2,2,128,512]{3,2,1,0:T(8,128)(2,1)S(1)}, u32[]{:S(2)}, u32[]{:S(2)}) collective-permute-start(bf16[2,2,128,512]{3,2,1,0:T(8,128)(2,1)} %pad_maximum_fusion.2), channel_id=1, source_target_pairs={{0,30},{1,31},{2,28},{3,29},{4,26},{5,27},{6,24},{7,25},{8,22},{9,... | collective-permute-start | bytes 1572872 | tf_op jit(solution)/shard_map/ppermute | solution.py:237
  71.3 22.7 %collective-permute-start.11 = (bf16[2,128,512]{2,1,0:T(8,128)(2,1)S(1)}, bf16[2,128,512]{2,1,0:T(8,128)(2,1)S(1)}, u32[]{:S(2)}, u32[]{:S(2)}) collective-permute-start(bf16[2,128,512]{2,1,0:T(8,128)(2,1)S(1)} %get-tuple-element.38), channel_id=1, source_target_pairs={{0,94},{1,95},{2,92},{3,93},{4,90},{5,91},{6,88},{7,89},{8,86},{9,... | collective-permute-start | bytes 786440 | tf_op jit(solution)/shard_map/ppermute | solution.py:237
  76.6 35.1 %collective-permute-start.4 = (bf16[128,512]{1,0:T(8,128)(2,1)S(1)}, bf16[128,512]{1,0:T(8,128)(2,1)S(1)}, u32[]{:S(2)}, u32[]{:S(2)}) collective-permute-start(bf16[128,512]{1,0:T(8,128)(2,1)S(1)} %get-tuple-element.30), channel_id=1, source_target_pairs={{0,32},{1,33},{2,34},{3,35},{4,36},{5,37},{6,38},{7,39},{8,40},{9,... | collective-permute-start | bytes 393224 | tf_op jit(solution)/shard_map/ppermute | solution.py:237
  92.6 1.3 copy-start
  94.0 48.8 %all-to-all-start.1 = ((bf16[32,2,128,128]{3,2,1,0:T(8,128)(2,1)}), bf16[32,2,128,128]{3,2,1,0:T(8,128)(2,1)S(1)}, u32[]{:S(2)}, u32[]{:S(2)}) async-start(bf16[32,2,128,128]{3,2,1,0:T(8,128)(2,1)} %copy-done), calls=%async_computation.1 | async-start | bytes 4194304 | tf_op jit(solution)/shard_map/all_to_all | solution.py:268
  106.1 7.0 %collective-permute-start.12 = (bf16[128,512]{1,0:T(8,128)(2,1)S(1)}, bf16[128,512]{1,0:T(8,128)(2,1)S(1)}, u32[]{:S(2)}, u32[]{:S(2)}) collective-permute-start(bf16[128,512]{1,0:T(8,128)(2,1)S(1)} %get-tuple-element.70), channel_id=1, source_target_pairs={{0,32},{1,33},{2,34},{3,35},{4,36},{5,37},{6,38},{7,39},{8,40},{9,... | collective-permute-start | bytes 393224 | tf_op jit(solution)/shard_map/ppermute | solution.py:237
  106.2 19.1 %collective-permute-start.10 = (bf16[128,512]{1,0:T(8,128)(2,1)S(1)}, bf16[128,512]{1,0:T(8,128)(2,1)S(1)}, u32[]{:S(2)}, u32[]{:S(2)}) collective-permute-start(bf16[128,512]{1,0:T(8,128)(2,1)S(1)} %get-tuple-element.37), channel_id=1, source_target_pairs={{0,96},{1,97},{2,98},{3,99},{4,100},{5,101},{6,102},{7,103},{8,104... | collective-permute-start | bytes 393224 | tf_op jit(solution)/shard_map/ppermute | solution.py:237
  106.3 31.8 %collective-permute-start.7 = (bf16[128,512]{1,0:T(8,128)(2,1)S(1)}, bf16[128,512]{1,0:T(8,128)(2,1)S(1)}, u32[]{:S(2)}, u32[]{:S(2)}) collective-permute-start(bf16[128,512]{1,0:T(8,128)(2,1)S(1)} %get-tuple-element.34), channel_id=1, source_target_pairs={{0,30},{1,31},{2,28},{3,29},{4,26},{5,27},{6,24},{7,25},{8,22},{9,... | collective-permute-start | bytes 393224 | tf_op jit(solution)/shard_map/ppermute | solution.py:237
  111.0 30.5 %collective-permute-start.8 = (bf16[128,512]{1,0:T(8,128)(2,1)S(1)}, bf16[128,512]{1,0:T(8,128)(2,1)S(1)}, u32[]{:S(2)}, u32[]{:S(2)}) collective-permute-start(bf16[128,512]{1,0:T(8,128)(2,1)S(1)} %get-tuple-element.35), channel_id=1, source_target_pairs={{0,62},{1,63},{2,60},{3,61},{4,58},{5,59},{6,56},{7,57},{8,54},{9,... | collective-permute-start | bytes 393224 | tf_op jit(solution)/shard_map/ppermute | solution.py:237
  111.7 29.9 %copy-start.4 = (bf16[128,512]{1,0:T(8,128)(2,1)}, bf16[128,512]{1,0:T(8,128)(2,1)S(1)}, u32[]{:S(2)}) copy-start(bf16[128,512]{1,0:T(8,128)(2,1)S(1)} %collective-permute-done.4) | copy-start | bytes 393220
  111.7 29.9 %collective-permute-start.9 = (bf16[128,512]{1,0:T(8,128)(2,1)S(1)}, bf16[128,512]{1,0:T(8,128)(2,1)S(1)}, u32[]{:S(2)}, u32[]{:S(2)}) collective-permute-start(bf16[128,512]{1,0:T(8,128)(2,1)S(1)} %get-tuple-element.36), channel_id=1, source_target_pairs={{0,64},{1,65},{2,66},{3,67},{4,68},{5,69},{6,70},{7,71},{8,72},{9,... | collective-permute-start | bytes 393224 | tf_op jit(solution)/shard_map/ppermute | solution.py:237
  142.8 1.3 copy-start.2

commit v8 on v7

--- a/solution.py
+++ b/solution.py
@@ -39,7 +39,7 @@
     if first:
         units, refs = refs[:4], refs[4:]
     else:
-        units, refs = [ref.at[layer] for ref in refs[:2] for layer in range(LAYERS)], refs[2:]
+        units, refs = [*refs[:2], refs[2].at[0], refs[2].at[1]], refs[3:]
     kv_ref, refs = refs[0], refs[1:]
     if not first:
         sums_ref, refs = refs[0], refs[1:]
@@ -157,7 +157,7 @@
     lax.fori_loop(0, 2, one_group, 0)
     for n in range(2):
         for layer in range(LAYERS):
-            grad_ref = grad_refs[2].at[layer] if first and n else grad_refs[n * LAYERS + layer]
+            grad_ref = grad_refs[n].at[layer] if first else grad_refs[n * LAYERS + layer]
             for g in range(GROUPS):
                 lo = layer * WIDTH + g * HEAD_DIM
                 grad_ref[:, g * HEAD_DIM : (g + 1) * HEAD_DIM] = q_s[n, lo : lo + ROWS, :]
@@ -174,7 +174,7 @@
     args = [*units, kv] + ([] if first else [sums])
     grad = jax.ShapeDtypeStruct((ROWS, WIDTH), BF16)
     pair = jax.ShapeDtypeStruct((LAYERS, ROWS, WIDTH), BF16)
-    outs = [grad, grad, pair] if first else [grad] * 4
+    outs = [pair, pair] if first else [grad] * 4
     outs.append(jax.ShapeDtypeStruct((BLOCKS, 2, ROWS, HEAD_DIM), BF16))
     return pl.pallas_call(
         functools.partial(attention_kernel, first),
@@ -253,22 +253,22 @@
         )
 
     blocks = jnp.stack([blk, flip(blk)]).astype(jnp.int32)
-    across = move(pick(ACROSS), ACROSS)
-    across_core = move(pick(ACROSS | CORE), ACROSS | CORE)
+    near, near_core, turned, turned_core = [move(pick(k), k) for k in (NEAR, NEAR | CORE, FLIP, FLIP | CORE)]
     own, own_core = pick(0), move(pick(CORE), CORE)
-    swapped = move(jnp.stack([pick(NEAR | CORE), pick(FLIP | CORE)]), CORE)
-    near, turned = jnp.stack([pick(NEAR), swapped[0]]), jnp.stack([pick(FLIP), swapped[1]])
-    near, turned, kv, across, across_core = lax.optimization_barrier((near, turned, kv, across, across_core))
-    near, turned = move(near, NEAR), move(turned, FLIP)
-
-    d_own, d_own_core, d_across, sums = attention(blocks, (own, own_core, across, across_core), kv)
-    d_across = move(d_across, ACROSS)
-    *second, term = attention(blocks, (near, turned), kv, sums)
-    d_across, term = lax.optimization_barrier((d_across, term))
+    across = jnp.stack([pick(ACROSS), move(pick(ACROSS | CORE), CORE)])
+    across, kv, near, near_core, turned, turned_core = lax.optimization_barrier(
+        (across, kv, near, near_core, turned, turned_core)
+    )
+    across = move(across, ACROSS)
+
+    d_near, d_turned, sums = attention(blocks, (near, near_core, turned, turned_core), kv)
+    d_near, d_turned = move(d_near, NEAR), move(d_turned, FLIP)
+    *second, term = attention(blocks, (own, own_core, across), kv, sums)
+    d_near, d_turned, term = lax.optimization_barrier((d_near, d_turned, term))
     received = lax.all_to_all(term, "blk", 0, 0, tiled=True)
-    grads = {0: d_own, CORE: move(d_own_core, CORE), ACROSS: d_across[0], ACROSS | CORE: move(d_across[1], CORE)}
-    for k, grad in zip((NEAR, NEAR | CORE, FLIP, FLIP | CORE), second):
-        grads[k] = move(grad, k)
+    grads = {NEAR: d_near[0], NEAR | CORE: move(d_near[1], CORE), FLIP: d_turned[0], FLIP | CORE: move(d_turned[1], CORE)}
+    for k, grad in zip((0, CORE, ACROSS, ACROSS | CORE), second):
+        grads[k] = move(grad, k) if k else grad
     grads = lax.optimization_barrier(grads)
     kv_grad = received.reshape(2, 16, 2, ROWS, HEAD_DIM).astype(F32).sum(1)
     kv_grad = kv_grad.transpose(1, 2, 0, 3).reshape(2, ROWS, 2 * HEAD_DIM)

time: 143 us -> 142 us (level)
  waiting for transfers between devices: 52.9 us -> 50.7 us
  other arithmetic: 6.24 us -> 8.29 us
  local copies, waits for them, and re-layouts: 6.73 us -> 4.72 us
    another operation x4 -> x7, other arithmetic: 2.22 us -> 5.3 us  [pick(): jnp.stack([lax.dynamic_slice_in_dim(queries[0], at, WIDTH, 1), lax.dynami...]
    ppermute x13 -> x14, waiting for transfers between devices: 52.9 us -> 50.7 us  [move(): return lax.ppermute(x, AXES, partners(k))]
    another operation x7 -> x2, other arithmetic: 3.6 us -> 2.58 us  [shards(): across = jnp.stack([pick(ACROSS), move(pick(ACROSS | CORE), CORE)])]
    ppermute x13 -> x14, starting transfers between devices: 20.8 us -> 21.5 us  [move(): return lax.ppermute(x, AXES, partners(k))]
  transfers between devices with their start and end apart: 15 -> 16, of which waited for: 5 -> 5; matrix products, arithmetic and copies ran while one was open for 7% -> 7% of each run, Pallas kernels for 21% -> 22%
where the time goes in v8:
time: 142 us; the launch traced here: 143 us
  waiting for transfers between devices  50.7 us (36%)
  starting transfers between devices  44.5 us (31%)
  Pallas kernels  33.5 us (24%)
  other arithmetic  8.29 us (6%)
  local copies, waits for them, and re-layouts  4.72 us (3%)
    ppermute x14, waiting for transfers between devices, move(): return lax.ppermute(x, AXES, partners(k))  50.7 us
    pallas_call x2, Pallas kernels, attention(): pl.pallas_call(functools.partial(attention_kernel, first), out_shape=outs...  30.9 us
    ppermute x14, starting transfers between devices, move(): return lax.ppermute(x, AXES, partners(k))  21.5 us
    all_to_all x1, starting transfers between devices, shards(): received = lax.all_to_all(term, 'blk', 0, 0, tiled=True)  11.7 us
    all_to_all x1, starting transfers between devices, shards(): lax.all_to_all(spread_cache(kv_codes, kv_scales), 'blk', 0, 0, tiled=True)  11.3 us
    another operation x7, other arithmetic, pick(): jnp.stack([lax.dynamic_slice_in_dim(queries[0], at, WIDTH, 1), lax.dynami...  5.3 us
  transfers between devices with their start and end apart: 16, of which 5 were waited for; matrix products, arithmetic and copies ran while one was open for 7% of the time, Pallas kernels for 22%

profile of v8, /device:TPU:1, one launch (start us, length us, event | category | flops | bytes accessed | tf_op | source)
XLA Modules:
  0.0 142.5 jit_solution(12346827584038486665)
XLA Ops:
  0.6 2.6 %spread_cache.1 = bf16[32,2,128,128]{3,2,1,0:T(8,128)(2,1)} custom-call(f32[2,2,4]{2,1,0:T(2,128)} %bitcast.37, s32[2,128,256]{2,1,0:T(8,128)} %codes_ref.1), custom_call_target="tpu_custom_call" | custom-call | tf_op jit(solution)/shard_map/spread_cache/pallas_call | solution.py:215
  3.2 11.3 %all-to-all-start = ((bf16[32,2,128,128]{3,2,1,0:T(8,128)(2,1)}), bf16[32,2,128,128]{3,2,1,0:T(8,128)(2,1)S(1)}, u32[]{:S(2)}, u32[]{:S(2)}) async-start(bf16[32,2,128,128]{3,2,1,0:T(8,128)(2,1)} %spread_cache.1), calls=%async_computation | async-start | bytes 4194304 | tf_op jit(solution)/shard_map/all_to_all | solution.py:247
  14.6 2.2 %constant_dynamic-slice_fusion = (bf16[1,128,512]{2,1,0:T(8,128)(2,1)S(1)}, bf16[1,128,512]{2,1,0:T(8,128)(2,1)S(1)}, bf16[1,128,512]{2,1,0:T(8,128)(2,1)S(1)}, ...) fusion(bf16[1,128,4096]{2,1,0:T(8,128)(2,1)S(1)} %copy-done.1, ...), kind=kLoop, calls=%fused_computation.22 | loop fusion | bytes 4194336 | tf_op jit(solution)/shard_map/dynamic_slice | solution.py:252
  16.8 0.7 pad_maximum_fusion.4
  17.5 0.7 collective-permute-start.2
  18.2 0.7 pad_maximum_fusion.5
  19.0 1.8 %collective-permute-start.3 = (bf16[2,128,512]{2,1,0:T(8,128)(2,1)}, bf16[2,128,512]{2,1,0:T(8,128)(2,1)S(1)}, u32[]{:S(2)}, u32[]{:S(2)}) collective-permute-start(bf16[2,128,512]{2,1,0:T(8,128)(2,1)} %pad_maximum_fusion.5), channel_id=1, source_target_pairs={{0,96},{1,97},{2,98},{3,99},{4,100},{5,101},{6,102},{7,103},{8,104... | collective-permute-start | bytes 786440 | tf_op jit(solution)/shard_map/ppermute | solution.py:237
  20.8 0.7 pad_maximum_fusion.6
  21.5 4.9 %collective-permute-start.4 = (bf16[2,128,512]{2,1,0:T(8,128)(2,1)}, bf16[2,128,512]{2,1,0:T(8,128)(2,1)S(1)}, u32[]{:S(2)}, u32[]{:S(2)}) collective-permute-start(bf16[2,128,512]{2,1,0:T(8,128)(2,1)} %pad_maximum_fusion.6), channel_id=1, source_target_pairs={{0,30},{1,31},{2,28},{3,29},{4,26},{5,27},{6,24},{7,25},{8,22},{9,... | collective-permute-start | bytes 786440 | tf_op jit(solution)/shard_map/ppermute | solution.py:237
  26.5 0.7 pad_maximum_fusion.7
  27.2 0.7 pad_maximum_fusion.3
  27.9 0.4 collective-permute-start.1
  28.3 0.7 maximum_bitcast_fusion
  29.0 0.7 pad_maximum_fusion.2
  29.8 0.9 pad_maximum_fusion.1.refs_0_
  31.0 1.9 %pad_maximum_fusion = bf16[2,2,128,512]{3,2,1,0:T(8,128)(2,1)} fusion(bf16[1,2,128,512]{3,2,1,0:T(8,128)(2,1)} %bitcast.3, bf16[1,2,128,512]{3,2,1,0:T(8,128)(2,1)} %maximum_bitcast_fusion), kind=kLoop, calls=%fused_computation.1 | loop fusion | flops 262144 | bytes 1048576 | tf_op jit(solution)/shard_map/stack | solution.py:258
  32.8 12.2 %collective-permute-done.2.refs_0_ = bf16[2,128,512]{2,1,0:T(8,128)(2,1)S(1)} collective-permute-done((bf16[2,128,512]{2,1,0:T(8,128)(2,1)}, bf16[2,128,512]{2,1,0:T(8,128)(2,1)S(1)}, u32[]{:S(2)}, u32[]{:S(2)}) %collective-permute-start.2) | collective-permute-done | bytes 262176 | tf_op jit(solution)/shard_map/ppermute | solution.py:237
  45.1 6.1 %collective-permute-done.3.refs_1_ = bf16[2,128,512]{2,1,0:T(8,128)(2,1)S(1)} collective-permute-done((bf16[2,128,512]{2,1,0:T(8,128)(2,1)}, bf16[2,128,512]{2,1,0:T(8,128)(2,1)S(1)}, u32[]{:S(2)}, u32[]{:S(2)}) %collective-permute-start.3) | collective-permute-done | bytes 262176 | tf_op jit(solution)/shard_map/ppermute | solution.py:237
  51.2 3.6 %collective-permute-done.5.refs_3_ = bf16[2,128,512]{2,1,0:T(8,128)(2,1)S(1)} collective-permute-done((bf16[2,128,512]{2,1,0:T(8,128)(2,1)}, bf16[2,128,512]{2,1,0:T(8,128)(2,1)S(1)}, u32[]{:S(2)}, u32[]{:S(2)}) %collective-permute-start.5) | collective-permute-done | bytes 262176 | tf_op jit(solution)/shard_map/ppermute | solution.py:237
  54.8 0.6 collective-permute-start.6
  55.4 15.2 %attention_first.1 = (bf16[2,128,512]{2,1,0:T(8,128)(2,1)S(1)}, bf16[2,128,512]{2,1,0:T(8,128)(2,1)S(1)}, bf16[32,2,128,128]{3,2,1,0:T(8,128)(2,1)S(1)}) custom-call(s32[2]{0:T(128)S(1)} %pad_add_fusion.blocks_ref, bf16[2,128,512]{2,1,0:T(8,128)(2,1)S(1)} %collective-permute-done.2.refs_0_, bf16[2,128,512]{2,1,0:T(8,128)(2,1)S(1)} %collective-permute-done.3.refs_1_, ...), custom_call_target="tpu_custom_call" | custom-call | flops 12000000000 | bytes 8000000 | tf_op jit(solution)/shard_map/attention_first/pallas_call | solution.py:179
  70.6 0.8 collective-permute-start.8
  71.4 4.7 %collective-permute-start.9 = (bf16[2,128,512]{2,1,0:T(8,128)(2,1)S(1)}, bf16[2,128,512]{2,1,0:T(8,128)(2,1)S(1)}, u32[]{:S(2)}, u32[]{:S(2)}) collective-permute-start(bf16[2,128,512]{2,1,0:T(8,128)(2,1)S(1)} %get-tuple-element.37), channel_id=1, source_target_pairs={{0,30},{1,31},{2,28},{3,29},{4,26},{5,27},{6,24},{7,25},{8,22},{9,... | collective-permute-start | bytes 786440 | tf_op jit(solution)/shard_map/ppermute | solution.py:237
  76.1 15.7 %attention_second.1 = (bf16[128,512]{1,0:T(8,128)(2,1)S(1)}, bf16[128,512]{1,0:T(8,128)(2,1)S(1)}, bf16[128,512]{1,0:T(8,128)(2,1)S(1)}, bf16[128,512]{1,0:T(8,128)(2,1)S(1)}, bf16[32,2,128,128]{3,2,1,0:T(8,128)(2,1)S(1)}) custom-call(s32[2]{0:T(128)S(1)} %pad_add_fusion.blocks_ref, bf16[2,128,512]{2,1,0:T(8,128)(2,1)S(1)} %pad_maximum_fusion.1.refs_0_, ...), custom_call_target="tpu_custom_call" | custom-call | flops 12000000000 | bytes 8000000 | tf_op jit(solution)/shard_map/attention_second/pallas_call | solution.py:179
  91.8 1.3 copy-done
  93.2 0.8 collective-permute-start.10
  94.0 11.7 %all-to-all-start.1 = ((bf16[32,2,128,128]{3,2,1,0:T(8,128)(2,1)}), bf16[32,2,128,128]{3,2,1,0:T(8,128)(2,1)S(1)}, u32[]{:S(2)}, u32[]{:S(2)}) async-start(bf16[32,2,128,128]{3,2,1,0:T(8,128)(2,1)} %copy-done), calls=%async_computation.1 | async-start | bytes 4194304 | tf_op jit(solution)/shard_map/all_to_all | solution.py:268
  106.1 5.5 %collective-permute-start.12 = (bf16[128,512]{1,0:T(8,128)(2,1)S(1)}, bf16[128,512]{1,0:T(8,128)(2,1)S(1)}, u32[]{:S(2)}, u32[]{:S(2)}) collective-permute-start(bf16[128,512]{1,0:T(8,128)(2,1)S(1)} %get-tuple-element.41), channel_id=1, source_target_pairs={{0,94},{1,95},{2,92},{3,93},{4,90},{5,91},{6,88},{7,89},{8,86},{9,... | collective-permute-start | bytes 393224 | tf_op jit(solution)/shard_map/ppermute | solution.py:237
  111.6 0.6 collective-permute-start.13
  112.2 25.5 %collective-permute-done.12 = bf16[128,512]{1,0:T(8,128)(2,1)S(1)} collective-permute-done((bf16[128,512]{1,0:T(8,128)(2,1)S(1)}, bf16[128,512]{1,0:T(8,128)(2,1)S(1)}, u32[]{:S(2)}, u32[]{:S(2)}) %collective-permute-start.12) | collective-permute-done | bytes 131104 | tf_op jit(solution)/shard_map/ppermute | solution.py:237
  137.8 3.1 %collective-permute-done.13 = bf16[128,512]{1,0:T(8,128)(2,1)S(1)} collective-permute-done((bf16[128,512]{1,0:T(8,128)(2,1)S(1)}, bf16[128,512]{1,0:T(8,128)(2,1)S(1)}, u32[]{:S(2)}, u32[]{:S(2)}) %collective-permute-start.13) | collective-permute-done | bytes 131104 | tf_op jit(solution)/shard_map/ppermute | solution.py:237
  141.7 0.8 copy.7
  (34 shorter events, 1.5 us)
Async XLA Ops:
  3.2 11.4 %copy-start.1 = (bf16[1,128,4096]{2,1,0:T(8,128)(2,1)S(1)}, bf16[1,128,4096]{2,1,0:T(8,128)(2,1)}, u32[]{:S(2)}) copy-start(bf16[1,128,4096]{2,1,0:T(8,128)(2,1)} %param.5) | copy-start | bytes 3145732
  3.2 51.6 %all-to-all-start = ((bf16[32,2,128,128]{3,2,1,0:T(8,128)(2,1)}), bf16[32,2,128,128]{3,2,1,0:T(8,128)(2,1)S(1)}, u32[]{:S(2)}, u32[]{:S(2)}) async-start(bf16[32,2,128,128]{3,2,1,0:T(8,128)(2,1)} %spread_cache.1), calls=%async_computation | async-start | bytes 4194304 | tf_op jit(solution)/shard_map/all_to_all | solution.py:247
  17.5 27.6 %collective-permute-start.2 = (bf16[2,128,512]{2,1,0:T(8,128)(2,1)}, bf16[2,128,512]{2,1,0:T(8,128)(2,1)S(1)}, u32[]{:S(2)}, u32[]{:S(2)}) collective-permute-start(bf16[2,128,512]{2,1,0:T(8,128)(2,1)} %pad_maximum_fusion.4), channel_id=1, source_target_pairs={{0,64},{1,65},{2,66},{3,67},{4,68},{5,69},{6,70},{7,71},{8,72},{9,... | collective-permute-start | bytes 786440 | tf_op jit(solution)/shard_map/ppermute | solution.py:237
  19.0 32.3 %collective-permute-start.3 = (bf16[2,128,512]{2,1,0:T(8,128)(2,1)}, bf16[2,128,512]{2,1,0:T(8,128)(2,1)S(1)}, u32[]{:S(2)}, u32[]{:S(2)}) collective-permute-start(bf16[2,128,512]{2,1,0:T(8,128)(2,1)} %pad_maximum_fusion.5), channel_id=1, source_target_pairs={{0,96},{1,97},{2,98},{3,99},{4,100},{5,101},{6,102},{7,103},{8,104... | collective-permute-start | bytes 786440 | tf_op jit(solution)/shard_map/ppermute | solution.py:237
  21.5 29.7 %collective-permute-start.4 = (bf16[2,128,512]{2,1,0:T(8,128)(2,1)}, bf16[2,128,512]{2,1,0:T(8,128)(2,1)S(1)}, u32[]{:S(2)}, u32[]{:S(2)}) collective-permute-start(bf16[2,128,512]{2,1,0:T(8,128)(2,1)} %pad_maximum_fusion.6), channel_id=1, source_target_pairs={{0,30},{1,31},{2,28},{3,29},{4,26},{5,27},{6,24},{7,25},{8,22},{9,... | collective-permute-start | bytes 786440 | tf_op jit(solution)/shard_map/ppermute | solution.py:237
  27.2 27.6 %collective-permute-start.5 = (bf16[2,128,512]{2,1,0:T(8,128)(2,1)}, bf16[2,128,512]{2,1,0:T(8,128)(2,1)S(1)}, u32[]{:S(2)}, u32[]{:S(2)}) collective-permute-start(bf16[2,128,512]{2,1,0:T(8,128)(2,1)} %pad_maximum_fusion.7), channel_id=1, source_target_pairs={{0,62},{1,63},{2,60},{3,61},{4,58},{5,59},{6,56},{7,57},{8,54},{9,... | collective-permute-start | bytes 786440 | tf_op jit(solution)/shard_map/ppermute | solution.py:237
  27.9 2.8 %collective-permute-start.1 = (bf16[2,128,512]{2,1,0:T(8,128)(2,1)}, bf16[2,128,512]{2,1,0:T(8,128)(2,1)}, u32[]{:S(2)}, u32[]{:S(2)}) collective-permute-start(bf16[2,128,512]{2,1,0:T(8,128)(2,1)} %pad_maximum_fusion.3), channel_id=1, source_target_pairs={{0,32},{1,33},{2,34},{3,35},{4,36},{5,37},{6,38},{7,39},{8,40},{9,... | collective-permute-start | bytes 786440 | tf_op jit(solution)/shard_map/ppermute | solution.py:237
  30.8 45.3 %collective-permute-start = (bf16[2,128,512]{2,1,0:T(8,128)(2,1)}, bf16[2,128,512]{2,1,0:T(8,128)(2,1)}, u32[]{:S(2)}, u32[]{:S(2)}) collective-permute-start(bf16[2,128,512]{2,1,0:T(8,128)(2,1)} %pad_maximum_fusion.2), channel_id=1, source_target_pairs={{0,32},{1,33},{2,34},{3,35},{4,36},{5,37},{6,38},{7,39},{8,40},{9,... | collective-permute-start | bytes 786440 | tf_op jit(solution)/shard_map/ppermute | solution.py:237
  54.8 21.3 %collective-permute-start.6 = (bf16[2,2,128,512]{3,2,1,0:T(8,128)(2,1)}, bf16[2,2,128,512]{3,2,1,0:T(8,128)(2,1)S(1)}, u32[]{:S(2)}, u32[]{:S(2)}) collective-permute-start(bf16[2,2,128,512]{3,2,1,0:T(8,128)(2,1)} %pad_maximum_fusion), channel_id=1, source_target_pairs={{0,94},{1,95},{2,92},{3,93},{4,90},{5,91},{6,88},{7,89},{8,86},{9,... | collective-permute-start | bytes 1572872 | tf_op jit(solution)/shard_map/ppermute | solution.py:237
  70.6 22.5 %collective-permute-start.8 = (bf16[2,128,512]{2,1,0:T(8,128)(2,1)S(1)}, bf16[2,128,512]{2,1,0:T(8,128)(2,1)S(1)}, u32[]{:S(2)}, u32[]{:S(2)}) collective-permute-start(bf16[2,128,512]{2,1,0:T(8,128)(2,1)S(1)} %get-tuple-element.36), channel_id=1, source_target_pairs={{0,64},{1,65},{2,66},{3,67},{4,68},{5,69},{6,70},{7,71},{8,72},{9,... | collective-permute-start | bytes 786440 | tf_op jit(solution)/shard_map/ppermute | solution.py:237
  71.4 21.7 %collective-permute-start.9 = (bf16[2,128,512]{2,1,0:T(8,128)(2,1)S(1)}, bf16[2,128,512]{2,1,0:T(8,128)(2,1)S(1)}, u32[]{:S(2)}, u32[]{:S(2)}) collective-permute-start(bf16[2,128,512]{2,1,0:T(8,128)(2,1)S(1)} %get-tuple-element.37), channel_id=1, source_target_pairs={{0,30},{1,31},{2,28},{3,29},{4,26},{5,27},{6,24},{7,25},{8,22},{9,... | collective-permute-start | bytes 786440 | tf_op jit(solution)/shard_map/ppermute | solution.py:237
  91.8 1.3 copy-start
  93.2 19.1 %collective-permute-start.10 = (bf16[128,512]{1,0:T(8,128)(2,1)S(1)}, bf16[128,512]{1,0:T(8,128)(2,1)S(1)}, u32[]{:S(2)}, u32[]{:S(2)}) collective-permute-start(bf16[128,512]{1,0:T(8,128)(2,1)S(1)} %get-tuple-element.72), channel_id=1, source_target_pairs={{0,32},{1,33},{2,34},{3,35},{4,36},{5,37},{6,38},{7,39},{8,40},{9,... | collective-permute-start | bytes 393224 | tf_op jit(solution)/shard_map/ppermute | solution.py:237
  94.0 47.2 %all-to-all-start.1 = ((bf16[32,2,128,128]{3,2,1,0:T(8,128)(2,1)}), bf16[32,2,128,128]{3,2,1,0:T(8,128)(2,1)S(1)}, u32[]{:S(2)}, u32[]{:S(2)}) async-start(bf16[32,2,128,128]{3,2,1,0:T(8,128)(2,1)} %copy-done), calls=%async_computation.1 | async-start | bytes 4194304 | tf_op jit(solution)/shard_map/all_to_all | solution.py:268
  105.8 6.5 %collective-permute-start.11 = (bf16[128,512]{1,0:T(8,128)(2,1)S(1)}, bf16[128,512]{1,0:T(8,128)(2,1)S(1)}, u32[]{:S(2)}, u32[]{:S(2)}) collective-permute-start(bf16[128,512]{1,0:T(8,128)(2,1)S(1)} %get-tuple-element.70), channel_id=1, source_target_pairs={{0,32},{1,33},{2,34},{3,35},{4,36},{5,37},{6,38},{7,39},{8,40},{9,... | collective-permute-start | bytes 393224 | tf_op jit(solution)/shard_map/ppermute | solution.py:237
  106.1 31.6 %collective-permute-start.12 = (bf16[128,512]{1,0:T(8,128)(2,1)S(1)}, bf16[128,512]{1,0:T(8,128)(2,1)S(1)}, u32[]{:S(2)}, u32[]{:S(2)}) collective-permute-start(bf16[128,512]{1,0:T(8,128)(2,1)S(1)} %get-tuple-element.41), channel_id=1, source_target_pairs={{0,94},{1,95},{2,92},{3,93},{4,90},{5,91},{6,88},{7,89},{8,86},{9,... | collective-permute-start | bytes 393224 | tf_op jit(solution)/shard_map/ppermute | solution.py:237
  111.6 29.3 %collective-permute-start.13 = (bf16[128,512]{1,0:T(8,128)(2,1)S(1)}, bf16[128,512]{1,0:T(8,128)(2,1)S(1)}, u32[]{:S(2)}, u32[]{:S(2)}) collective-permute-start(bf16[128,512]{1,0:T(8,128)(2,1)S(1)} %get-tuple-element.42), channel_id=1, source_target_pairs={{0,126},{1,127},{2,124},{3,125},{4,122},{5,123},{6,120},{7,121},{8... | collective-permute-start | bytes 393224 | tf_op jit(solution)/shard_map/ppermute | solution.py:237
  112.2 28.7 %collective-permute-start.7 = (bf16[128,512]{1,0:T(8,128)(2,1)S(1)}, bf16[128,512]{1,0:T(8,128)(2,1)S(1)}, u32[]{:S(2)}, u32[]{:S(2)}) collective-permute-start(bf16[128,512]{1,0:T(8,128)(2,1)S(1)} %get-tuple-element.35), channel_id=1, source_target_pairs={{0,32},{1,33},{2,34},{3,35},{4,36},{5,37},{6,38},{7,39},{8,40},{9,... | collective-permute-start | bytes 393224 | tf_op jit(solution)/shard_map/ppermute | solution.py:237
  141.2 1.3 copy-start.2

commit v9 on v8

--- a/solution.py
+++ b/solution.py
@@ -24,7 +24,7 @@
 
 LAYERS = 2
 KEYS = 256
-UNROLL = (6, 3, 1)
+UNROLL = (6, 3, 2, 1)
 SPAN = KEYS // ROWS
 GROUP_ROWS = LAYERS * WIDTH
 CHUNKS = BLOCKS // SPAN
@@ -193,7 +193,7 @@
             pltpu.VMEM((HEAD_DIM, GROUP_ROWS), F32),
             pltpu.VMEM((24, GROUP_ROWS), F32),
         ],
-        compiler_params=pltpu.CompilerParams(vmem_limit_bytes=42 * 1024 * 1024),
+        compiler_params=pltpu.CompilerParams(vmem_limit_bytes=46 * 1024 * 1024),
         cost_estimate=pl.CostEstimate(flops=12_000_000_000, bytes_accessed=8_000_000, transcendentals=4_500_000),
         name="attention_first" if first else "attention_second",
     )(blocks, *args)

time: 142 us -> 142 us (level); the launches traced: 143 us -> 141 us
  no operation moved by 1% of the time
where the time goes in v9:
time: 142 us; the launch traced here: 141 us
  waiting for transfers between devices  49.5 us (35%)
  starting transfers between devices  44 us (31%)
  Pallas kernels  33.6 us (24%)
  other arithmetic  8.29 us (6%)
  local copies, waits for them, and re-layouts  4.72 us (3%)
    ppermute x14, waiting for transfers between devices, move(): return lax.ppermute(x, AXES, partners(k))  49.5 us
    pallas_call x2, Pallas kernels, attention(): pl.pallas_call(functools.partial(attention_kernel, first), out_shape=outs...  31 us
    ppermute x14, starting transfers between devices, move(): return lax.ppermute(x, AXES, partners(k))  21.5 us
    all_to_all x1, starting transfers between devices, shards(): lax.all_to_all(spread_cache(kv_codes, kv_scales), 'blk', 0, 0, tiled=True)  11.3 us
    all_to_all x1, starting transfers between devices, shards(): received = lax.all_to_all(term, 'blk', 0, 0, tiled=True)  11.3 us
    another operation x7, other arithmetic, pick(): jnp.stack([lax.dynamic_slice_in_dim(queries[0], at, WIDTH, 1), lax.dynami...  5.3 us
  transfers between devices with their start and end apart: 16, of which 5 were waited for; matrix products, arithmetic and copies ran while one was open for 7% of the time, Pallas kernels for 22%

profile of v9, /device:TPU:1, one launch (start us, length us, event | category | flops | bytes accessed | tf_op | source)
XLA Modules:
  0.0 141.1 jit_solution(17825345127594122615)
XLA Ops:
  0.6 2.6 %spread_cache.1 = bf16[32,2,128,128]{3,2,1,0:T(8,128)(2,1)} custom-call(f32[2,2,4]{2,1,0:T(2,128)} %bitcast.37, s32[2,128,256]{2,1,0:T(8,128)} %codes_ref.1), custom_call_target="tpu_custom_call" | custom-call | tf_op jit(solution)/shard_map/spread_cache/pallas_call | solution.py:215
  3.2 11.3 %all-to-all-start = ((bf16[32,2,128,128]{3,2,1,0:T(8,128)(2,1)}), bf16[32,2,128,128]{3,2,1,0:T(8,128)(2,1)S(1)}, u32[]{:S(2)}, u32[]{:S(2)}) async-start(bf16[32,2,128,128]{3,2,1,0:T(8,128)(2,1)} %spread_cache.1), calls=%async_computation | async-start | bytes 4194304 | tf_op jit(solution)/shard_map/all_to_all | solution.py:247
  14.6 2.2 %constant_dynamic-slice_fusion = (bf16[1,128,512]{2,1,0:T(8,128)(2,1)S(1)}, bf16[1,128,512]{2,1,0:T(8,128)(2,1)S(1)}, bf16[1,128,512]{2,1,0:T(8,128)(2,1)S(1)}, ...) fusion(bf16[1,128,4096]{2,1,0:T(8,128)(2,1)S(1)} %copy-done.1, ...), kind=kLoop, calls=%fused_computation.22 | loop fusion | bytes 4194336 | tf_op jit(solution)/shard_map/dynamic_slice | solution.py:252
  16.8 0.7 pad_maximum_fusion.4
  17.5 0.7 collective-permute-start.2
  18.2 0.7 pad_maximum_fusion.5
  19.0 1.8 %collective-permute-start.3 = (bf16[2,128,512]{2,1,0:T(8,128)(2,1)}, bf16[2,128,512]{2,1,0:T(8,128)(2,1)S(1)}, u32[]{:S(2)}, u32[]{:S(2)}) collective-permute-start(bf16[2,128,512]{2,1,0:T(8,128)(2,1)} %pad_maximum_fusion.5), channel_id=1, source_target_pairs={{0,96},{1,97},{2,98},{3,99},{4,100},{5,101},{6,102},{7,103},{8,104... | collective-permute-start | bytes 786440 | tf_op jit(solution)/shard_map/ppermute | solution.py:237
  20.8 0.7 pad_maximum_fusion.6
  21.5 4.9 %collective-permute-start.4 = (bf16[2,128,512]{2,1,0:T(8,128)(2,1)}, bf16[2,128,512]{2,1,0:T(8,128)(2,1)S(1)}, u32[]{:S(2)}, u32[]{:S(2)}) collective-permute-start(bf16[2,128,512]{2,1,0:T(8,128)(2,1)} %pad_maximum_fusion.6), channel_id=1, source_target_pairs={{0,30},{1,31},{2,28},{3,29},{4,26},{5,27},{6,24},{7,25},{8,22},{9,... | collective-permute-start | bytes 786440 | tf_op jit(solution)/shard_map/ppermute | solution.py:237
  26.5 0.7 pad_maximum_fusion.7
  27.2 0.7 pad_maximum_fusion.3
  27.9 0.4 collective-permute-start.1
  28.3 0.7 maximum_bitcast_fusion
  29.0 0.7 pad_maximum_fusion.2
  29.8 0.9 pad_maximum_fusion.1.refs_0_
  31.0 1.9 %pad_maximum_fusion = bf16[2,2,128,512]{3,2,1,0:T(8,128)(2,1)} fusion(bf16[1,2,128,512]{3,2,1,0:T(8,128)(2,1)} %bitcast.3, bf16[1,2,128,512]{3,2,1,0:T(8,128)(2,1)} %maximum_bitcast_fusion), kind=kLoop, calls=%fused_computation.1 | loop fusion | flops 262144 | bytes 1048576 | tf_op jit(solution)/shard_map/stack | solution.py:258
  32.8 12.2 %collective-permute-done.2.refs_0_ = bf16[2,128,512]{2,1,0:T(8,128)(2,1)S(1)} collective-permute-done((bf16[2,128,512]{2,1,0:T(8,128)(2,1)}, bf16[2,128,512]{2,1,0:T(8,128)(2,1)S(1)}, u32[]{:S(2)}, u32[]{:S(2)}) %collective-permute-start.2) | collective-permute-done | bytes 262176 | tf_op jit(solution)/shard_map/ppermute | solution.py:237
  45.1 6.1 %collective-permute-done.3.refs_1_ = bf16[2,128,512]{2,1,0:T(8,128)(2,1)S(1)} collective-permute-done((bf16[2,128,512]{2,1,0:T(8,128)(2,1)}, bf16[2,128,512]{2,1,0:T(8,128)(2,1)S(1)}, u32[]{:S(2)}, u32[]{:S(2)}) %collective-permute-start.3) | collective-permute-done | bytes 262176 | tf_op jit(solution)/shard_map/ppermute | solution.py:237
  51.2 3.6 %collective-permute-done.5.refs_3_ = bf16[2,128,512]{2,1,0:T(8,128)(2,1)S(1)} collective-permute-done((bf16[2,128,512]{2,1,0:T(8,128)(2,1)}, bf16[2,128,512]{2,1,0:T(8,128)(2,1)S(1)}, u32[]{:S(2)}, u32[]{:S(2)}) %collective-permute-start.5) | collective-permute-done | bytes 262176 | tf_op jit(solution)/shard_map/ppermute | solution.py:237
  54.8 0.6 collective-permute-start.6
  55.4 15.3 %attention_first.1 = (bf16[2,128,512]{2,1,0:T(8,128)(2,1)S(1)}, bf16[2,128,512]{2,1,0:T(8,128)(2,1)S(1)}, bf16[32,2,128,128]{3,2,1,0:T(8,128)(2,1)S(1)}) custom-call(s32[2]{0:T(128)S(1)} %pad_add_fusion.blocks_ref, bf16[2,128,512]{2,1,0:T(8,128)(2,1)S(1)} %collective-permute-done.2.refs_0_, bf16[2,128,512]{2,1,0:T(8,128)(2,1)S(1)} %collective-permute-done.3.refs_1_, ...), custom_call_target="tpu_custom_call" | custom-call | flops 12000000000 | bytes 8000000 | tf_op jit(solution)/shard_map/attention_first/pallas_call | solution.py:179
  70.6 0.8 collective-permute-start.8
  71.5 4.7 %collective-permute-start.9 = (bf16[2,128,512]{2,1,0:T(8,128)(2,1)S(1)}, bf16[2,128,512]{2,1,0:T(8,128)(2,1)S(1)}, u32[]{:S(2)}, u32[]{:S(2)}) collective-permute-start(bf16[2,128,512]{2,1,0:T(8,128)(2,1)S(1)} %get-tuple-element.37), channel_id=1, source_target_pairs={{0,30},{1,31},{2,28},{3,29},{4,26},{5,27},{6,24},{7,25},{8,22},{9,... | collective-permute-start | bytes 786440 | tf_op jit(solution)/shard_map/ppermute | solution.py:237
  76.1 15.7 %attention_second.1 = (bf16[128,512]{1,0:T(8,128)(2,1)S(1)}, bf16[128,512]{1,0:T(8,128)(2,1)S(1)}, bf16[128,512]{1,0:T(8,128)(2,1)S(1)}, bf16[128,512]{1,0:T(8,128)(2,1)S(1)}, bf16[32,2,128,128]{3,2,1,0:T(8,128)(2,1)S(1)}) custom-call(s32[2]{0:T(128)S(1)} %pad_add_fusion.blocks_ref, bf16[2,128,512]{2,1,0:T(8,128)(2,1)S(1)} %pad_maximum_fusion.1.refs_0_, ...), custom_call_target="tpu_custom_call" | custom-call | flops 12000000000 | bytes 8000000 | tf_op jit(solution)/shard_map/attention_second/pallas_call | solution.py:179
  91.9 1.3 copy-done
  93.3 0.8 collective-permute-start.10
  94.1 11.3 %all-to-all-start.1 = ((bf16[32,2,128,128]{3,2,1,0:T(8,128)(2,1)}), bf16[32,2,128,128]{3,2,1,0:T(8,128)(2,1)S(1)}, u32[]{:S(2)}, u32[]{:S(2)}) async-start(bf16[32,2,128,128]{3,2,1,0:T(8,128)(2,1)} %copy-done), calls=%async_computation.1 | async-start | bytes 4194304 | tf_op jit(solution)/shard_map/all_to_all | solution.py:268
  105.8 4.8 %collective-permute-start.12 = (bf16[128,512]{1,0:T(8,128)(2,1)S(1)}, bf16[128,512]{1,0:T(8,128)(2,1)S(1)}, u32[]{:S(2)}, u32[]{:S(2)}) collective-permute-start(bf16[128,512]{1,0:T(8,128)(2,1)S(1)} %get-tuple-element.41), channel_id=1, source_target_pairs={{0,94},{1,95},{2,92},{3,93},{4,90},{5,91},{6,88},{7,89},{8,86},{9,... | collective-permute-start | bytes 393224 | tf_op jit(solution)/shard_map/ppermute | solution.py:237
  110.6 1.3 collective-permute-start.13
  111.9 24.2 %collective-permute-done.12 = bf16[128,512]{1,0:T(8,128)(2,1)S(1)} collective-permute-done((bf16[128,512]{1,0:T(8,128)(2,1)S(1)}, bf16[128,512]{1,0:T(8,128)(2,1)S(1)}, u32[]{:S(2)}, u32[]{:S(2)}) %collective-permute-start.12) | collective-permute-done | bytes 131104 | tf_op jit(solution)/shard_map/ppermute | solution.py:237
  136.1 3.4 %collective-permute-done.13 = bf16[128,512]{1,0:T(8,128)(2,1)S(1)} collective-permute-done((bf16[128,512]{1,0:T(8,128)(2,1)S(1)}, bf16[128,512]{1,0:T(8,128)(2,1)S(1)}, u32[]{:S(2)}, u32[]{:S(2)}) %collective-permute-start.13) | collective-permute-done | bytes 131104 | tf_op jit(solution)/shard_map/ppermute | solution.py:237
  140.2 0.8 copy.7
  (34 shorter events, 1.5 us)
Async XLA Ops:
  3.2 11.4 %copy-start.1 = (bf16[1,128,4096]{2,1,0:T(8,128)(2,1)S(1)}, bf16[1,128,4096]{2,1,0:T(8,128)(2,1)}, u32[]{:S(2)}) copy-start(bf16[1,128,4096]{2,1,0:T(8,128)(2,1)} %param.5) | copy-start | bytes 3145732
  3.2 51.6 %all-to-all-start = ((bf16[32,2,128,128]{3,2,1,0:T(8,128)(2,1)}), bf16[32,2,128,128]{3,2,1,0:T(8,128)(2,1)S(1)}, u32[]{:S(2)}, u32[]{:S(2)}) async-start(bf16[32,2,128,128]{3,2,1,0:T(8,128)(2,1)} %spread_cache.1), calls=%async_computation | async-start | bytes 4194304 | tf_op jit(solution)/shard_map/all_to_all | solution.py:247
  17.5 27.6 %collective-permute-start.2 = (bf16[2,128,512]{2,1,0:T(8,128)(2,1)}, bf16[2,128,512]{2,1,0:T(8,128)(2,1)S(1)}, u32[]{:S(2)}, u32[]{:S(2)}) collective-permute-start(bf16[2,128,512]{2,1,0:T(8,128)(2,1)} %pad_maximum_fusion.4), channel_id=1, source_target_pairs={{0,64},{1,65},{2,66},{3,67},{4,68},{5,69},{6,70},{7,71},{8,72},{9,... | collective-permute-start | bytes 786440 | tf_op jit(solution)/shard_map/ppermute | solution.py:237
  19.0 32.3 %collective-permute-start.3 = (bf16[2,128,512]{2,1,0:T(8,128)(2,1)}, bf16[2,128,512]{2,1,0:T(8,128)(2,1)S(1)}, u32[]{:S(2)}, u32[]{:S(2)}) collective-permute-start(bf16[2,128,512]{2,1,0:T(8,128)(2,1)} %pad_maximum_fusion.5), channel_id=1, source_target_pairs={{0,96},{1,97},{2,98},{3,99},{4,100},{5,101},{6,102},{7,103},{8,104... | collective-permute-start | bytes 786440 | tf_op jit(solution)/shard_map/ppermute | solution.py:237
  21.5 29.7 %collective-permute-start.4 = (bf16[2,128,512]{2,1,0:T(8,128)(2,1)}, bf16[2,128,512]{2,1,0:T(8,128)(2,1)S(1)}, u32[]{:S(2)}, u32[]{:S(2)}) collective-permute-start(bf16[2,128,512]{2,1,0:T(8,128)(2,1)} %pad_maximum_fusion.6), channel_id=1, source_target_pairs={{0,30},{1,31},{2,28},{3,29},{4,26},{5,27},{6,24},{7,25},{8,22},{9,... | collective-permute-start | bytes 786440 | tf_op jit(solution)/shard_map/ppermute | solution.py:237
  27.2 27.6 %collective-permute-start.5 = (bf16[2,128,512]{2,1,0:T(8,128)(2,1)}, bf16[2,128,512]{2,1,0:T(8,128)(2,1)S(1)}, u32[]{:S(2)}, u32[]{:S(2)}) collective-permute-start(bf16[2,128,512]{2,1,0:T(8,128)(2,1)} %pad_maximum_fusion.7), channel_id=1, source_target_pairs={{0,62},{1,63},{2,60},{3,61},{4,58},{5,59},{6,56},{7,57},{8,54},{9,... | collective-permute-start | bytes 786440 | tf_op jit(solution)/shard_map/ppermute | solution.py:237
  27.9 2.8 %collective-permute-start.1 = (bf16[2,128,512]{2,1,0:T(8,128)(2,1)}, bf16[2,128,512]{2,1,0:T(8,128)(2,1)}, u32[]{:S(2)}, u32[]{:S(2)}) collective-permute-start(bf16[2,128,512]{2,1,0:T(8,128)(2,1)} %pad_maximum_fusion.3), channel_id=1, source_target_pairs={{0,32},{1,33},{2,34},{3,35},{4,36},{5,37},{6,38},{7,39},{8,40},{9,... | collective-permute-start | bytes 786440 | tf_op jit(solution)/shard_map/ppermute | solution.py:237
  30.8 45.4 %collective-permute-start = (bf16[2,128,512]{2,1,0:T(8,128)(2,1)}, bf16[2,128,512]{2,1,0:T(8,128)(2,1)}, u32[]{:S(2)}, u32[]{:S(2)}) collective-permute-start(bf16[2,128,512]{2,1,0:T(8,128)(2,1)} %pad_maximum_fusion.2), channel_id=1, source_target_pairs={{0,32},{1,33},{2,34},{3,35},{4,36},{5,37},{6,38},{7,39},{8,40},{9,... | collective-permute-start | bytes 786440 | tf_op jit(solution)/shard_map/ppermute | solution.py:237
  54.8 21.3 %collective-permute-start.6 = (bf16[2,2,128,512]{3,2,1,0:T(8,128)(2,1)}, bf16[2,2,128,512]{3,2,1,0:T(8,128)(2,1)S(1)}, u32[]{:S(2)}, u32[]{:S(2)}) collective-permute-start(bf16[2,2,128,512]{3,2,1,0:T(8,128)(2,1)} %pad_maximum_fusion), channel_id=1, source_target_pairs={{0,94},{1,95},{2,92},{3,93},{4,90},{5,91},{6,88},{7,89},{8,86},{9,... | collective-permute-start | bytes 1572872 | tf_op jit(solution)/shard_map/ppermute | solution.py:237
  70.6 22.6 %collective-permute-start.8 = (bf16[2,128,512]{2,1,0:T(8,128)(2,1)S(1)}, bf16[2,128,512]{2,1,0:T(8,128)(2,1)S(1)}, u32[]{:S(2)}, u32[]{:S(2)}) collective-permute-start(bf16[2,128,512]{2,1,0:T(8,128)(2,1)S(1)} %get-tuple-element.36), channel_id=1, source_target_pairs={{0,64},{1,65},{2,66},{3,67},{4,68},{5,69},{6,70},{7,71},{8,72},{9,... | collective-permute-start | bytes 786440 | tf_op jit(solution)/shard_map/ppermute | solution.py:237
  71.5 21.8 %collective-permute-start.9 = (bf16[2,128,512]{2,1,0:T(8,128)(2,1)S(1)}, bf16[2,128,512]{2,1,0:T(8,128)(2,1)S(1)}, u32[]{:S(2)}, u32[]{:S(2)}) collective-permute-start(bf16[2,128,512]{2,1,0:T(8,128)(2,1)S(1)} %get-tuple-element.37), channel_id=1, source_target_pairs={{0,30},{1,31},{2,28},{3,29},{4,26},{5,27},{6,24},{7,25},{8,22},{9,... | collective-permute-start | bytes 786440 | tf_op jit(solution)/shard_map/ppermute | solution.py:237
  91.9 1.3 copy-start
  93.3 18.6 %collective-permute-start.10 = (bf16[128,512]{1,0:T(8,128)(2,1)S(1)}, bf16[128,512]{1,0:T(8,128)(2,1)S(1)}, u32[]{:S(2)}, u32[]{:S(2)}) collective-permute-start(bf16[128,512]{1,0:T(8,128)(2,1)S(1)} %get-tuple-element.72), channel_id=1, source_target_pairs={{0,32},{1,33},{2,34},{3,35},{4,36},{5,37},{6,38},{7,39},{8,40},{9,... | collective-permute-start | bytes 393224 | tf_op jit(solution)/shard_map/ppermute | solution.py:237
  94.1 45.6 %all-to-all-start.1 = ((bf16[32,2,128,128]{3,2,1,0:T(8,128)(2,1)}), bf16[32,2,128,128]{3,2,1,0:T(8,128)(2,1)S(1)}, u32[]{:S(2)}, u32[]{:S(2)}) async-start(bf16[32,2,128,128]{3,2,1,0:T(8,128)(2,1)} %copy-done), calls=%async_computation.1 | async-start | bytes 4194304 | tf_op jit(solution)/shard_map/all_to_all | solution.py:268
  105.4 6.5 %collective-permute-start.11 = (bf16[128,512]{1,0:T(8,128)(2,1)S(1)}, bf16[128,512]{1,0:T(8,128)(2,1)S(1)}, u32[]{:S(2)}, u32[]{:S(2)}) collective-permute-start(bf16[128,512]{1,0:T(8,128)(2,1)S(1)} %get-tuple-element.70), channel_id=1, source_target_pairs={{0,32},{1,33},{2,34},{3,35},{4,36},{5,37},{6,38},{7,39},{8,40},{9,... | collective-permute-start | bytes 393224 | tf_op jit(solution)/shard_map/ppermute | solution.py:237
  105.8 30.3 %collective-permute-start.12 = (bf16[128,512]{1,0:T(8,128)(2,1)S(1)}, bf16[128,512]{1,0:T(8,128)(2,1)S(1)}, u32[]{:S(2)}, u32[]{:S(2)}) collective-permute-start(bf16[128,512]{1,0:T(8,128)(2,1)S(1)} %get-tuple-element.41), channel_id=1, source_target_pairs={{0,94},{1,95},{2,92},{3,93},{4,90},{5,91},{6,88},{7,89},{8,86},{9,... | collective-permute-start | bytes 393224 | tf_op jit(solution)/shard_map/ppermute | solution.py:237
  110.6 28.8 %collective-permute-start.13 = (bf16[128,512]{1,0:T(8,128)(2,1)S(1)}, bf16[128,512]{1,0:T(8,128)(2,1)S(1)}, u32[]{:S(2)}, u32[]{:S(2)}) collective-permute-start(bf16[128,512]{1,0:T(8,128)(2,1)S(1)} %get-tuple-element.42), channel_id=1, source_target_pairs={{0,126},{1,127},{2,124},{3,125},{4,122},{5,123},{6,120},{7,121},{8... | collective-permute-start | bytes 393224 | tf_op jit(solution)/shard_map/ppermute | solution.py:237
  111.8 27.6 %collective-permute-start.7 = (bf16[128,512]{1,0:T(8,128)(2,1)S(1)}, bf16[128,512]{1,0:T(8,128)(2,1)S(1)}, u32[]{:S(2)}, u32[]{:S(2)}) collective-permute-start(bf16[128,512]{1,0:T(8,128)(2,1)S(1)} %get-tuple-element.35), channel_id=1, source_target_pairs={{0,32},{1,33},{2,34},{3,35},{4,36},{5,37},{6,38},{7,39},{8,40},{9,... | collective-permute-start | bytes 393224 | tf_op jit(solution)/shard_map/ppermute | solution.py:237
  139.7 1.3 copy-start.2
